TPU v7x, 32 devices: a whole 2x2x4 slice. The times are simulated.
32 devices in a mesh: chan: 4 (over z), bl: 4 (over y, x), pol: 2 (over core).
Axes of the slice: x: 2, y: 2, z: 4, core: 2. Of those that a mesh axis runs over, the one named last changes fastest.
Arguments:
- visibilities: bfloat16 [2, 20480, 2, 256], P('pol', ('chan', 'bl')), may hold values from -1.5 to 1.5
- uv_coords: bfloat16 [20480, 2, 256], P(('chan', 'bl')), may hold values from -12 to 12
- block_slot: int32 [20480], P('chan'), may hold values from 0 to 63, as said below
- slot_table: int32 [3, 256], P(None, ('chan', 'bl')), may hold values from 0 to 2016, as said below
Outputs:
- stokes_grid: float32 [2, 2, 2048, 2048], P('pol', None, 'bl', 'chan')
Inputs may be any that keep to these rules, and one draw needn't show every extreme that they name: `block_slot`: entry j names a subgrid of block j's channel group; that subgrid's owner is entry // 16. Within the 1280 blocks of one baseline shard in one channel group (aligned runs of 1280 entries) no owner is named more than 640 times, and in every channel group one owner is named exactly 640 times by every shard. `slot_table`: column g belongs to subgrid g mod (64) of channel group g // 64, owned by shard b = (g // 16) mod 4. Row 0 is its corner's grid row, from b * 512 to (b + 1) * 512 - 32; row 1 its corner's grid column, up to 2016; row 2 its w-plane, below 32.
All inputs are finite; a program needn't handle non-finite values.
Results may differ from a plain program's by a relative error of at most 0.0035.
Values may be sent and summed in bfloat16 or wider, within the bound.
No kernel may reach another device: no remote copies, remote signals or barrier semaphores. Data moves between devices by JAX's collectives and lax.ppermute only.
A program may use at most 64 MiB of HBM per device.

v0:
```python
import math

import jax
import jax.numpy as jnp
from jax import lax
from jax.sharding import PartitionSpec as P

G = 2048
SUB = 32
VB = 256


two_pi = 2.0 * math.pi
w_step = 0.25
highest = lax.Precision.HIGHEST


def partner_2(block, axis, distance):
    count = lax.axis_size(axis)
    route = []
    for low in range(count):
        high = low | 1 << distance
        if high != low and high < count:
            route += [(low, high), (high, low)]
    return lax.ppermute(block, axis, route)


def pixel_offsets():
    return (jnp.arange(SUB, dtype=jnp.float32) - SUB // 2) / SUB


def kernel_images(packed):
    offsets = pixel_offsets()
    norm_scale = 1.0 / math.sqrt(VB)
    u_pos = packed[:, 2, :].astype(jnp.float32)
    v_pos = packed[:, 3, :].astype(jnp.float32)
    vis_real = packed[:, 0, :].astype(jnp.float32)[:, None, :]
    vis_imag = packed[:, 1, :].astype(jnp.float32)[:, None, :]
    angle_u = two_pi * u_pos[:, None, :] * offsets[None, :, None]
    left_phasor = jnp.concatenate([jnp.cos(angle_u), jnp.sin(angle_u)], axis=1).astype(jnp.bfloat16)
    angle_v = two_pi * v_pos[:, None, :] * offsets[None, :, None]
    phase_real = jnp.cos(angle_v) * norm_scale
    phase_imag = jnp.sin(angle_v) * norm_scale
    weighted_real = vis_real * phase_real - vis_imag * phase_imag
    weighted_imag = vis_real * phase_imag + vis_imag * phase_real
    right_phasor = jnp.concatenate([weighted_real, weighted_imag], axis=1).astype(jnp.bfloat16)
    product = jnp.einsum(
        "kav,kbv->kab", left_phasor, right_phasor, preferred_element_type=jnp.float32
    )
    real_part = product[:, :SUB, :SUB] - product[:, SUB:, SUB:]
    imag_part = product[:, :SUB, SUB:] + product[:, SUB:, :SUB]
    return jnp.stack([real_part, imag_part], axis=1).reshape(packed.shape[0], 2 * SUB * SUB)


def slot_sums(packed, slot_ids, slot_count):
    block_count = packed.shape[0]
    group_size = 128
    group_count = block_count // group_size
    packed_groups = packed.reshape(group_count, group_size, packed.shape[1], packed.shape[2])
    id_groups = slot_ids.reshape(group_count, group_size)
    slot_range = jnp.arange(slot_count, dtype=jnp.int32)

    def add_group(totals, inputs):
        blocks_group, group_ids = inputs
        images = kernel_images(blocks_group)
        onehot = (group_ids[None, :] == slot_range[:, None]).astype(jnp.float32)
        return (
            totals + jnp.dot(onehot, images, precision=highest, preferred_element_type=jnp.float32),
            None,
        )

    totals, _ = lax.scan(
        add_group, jnp.zeros((slot_count, 2 * SUB * SUB), jnp.float32), (packed_groups, id_groups)
    )
    return totals


def subgrid_transform(images, planes):
    slot_count = images.shape[0]
    cells = images.reshape(slot_count, 2, SUB, SUB)
    real_part = cells[:, 0]
    imag_part = cells[:, 1]
    offsets = pixel_offsets()
    tapers = jnp.sin(math.pi * (jnp.arange(SUB, dtype=jnp.float32) + 0.5) / SUB)
    taper_grid = tapers[:, None] * tapers[None, :]
    n_term = jnp.sqrt(1.0 - offsets[:, None] ** 2 - offsets[None, :] ** 2) - 1.0
    w_phase = (
        (0.0 - two_pi * w_step) * planes.astype(jnp.float32)[:, None, None] * n_term[None, :, :]
    )
    screen_cos = jnp.cos(w_phase)
    screen_sin = jnp.sin(w_phase)
    tapered_real = taper_grid * (real_part * screen_cos - imag_part * screen_sin)
    tapered_imag = taper_grid * (real_part * screen_sin + imag_part * screen_cos)
    centred = jnp.arange(SUB, dtype=jnp.int32) - SUB // 2
    product_mod = centred[:, None] * centred[None, :] % SUB
    angles = (0.0 - two_pi) * product_mod.astype(jnp.float32) / SUB
    dft_real = jnp.cos(angles) / math.sqrt(SUB)
    dft_imag = jnp.sin(angles) / math.sqrt(SUB)

    def along_rows(matrix, values):
        return jnp.einsum("kl,slm->skm", matrix, values, precision=highest)

    def along_cols(values, matrix):
        return jnp.einsum("skm,jm->skj", values, matrix, precision=highest)

    rows_real = along_rows(dft_real, tapered_real) - along_rows(dft_imag, tapered_imag)
    rows_imag = along_rows(dft_real, tapered_imag) + along_rows(dft_imag, tapered_real)
    cols_real = along_cols(rows_real, dft_real) - along_cols(rows_imag, dft_imag)
    cols_imag = along_cols(rows_real, dft_imag) + along_cols(rows_imag, dft_real)
    return jnp.stack([cols_real, cols_imag], axis=1)


def place_dense(subgrids, row_corner, col_corner, strip_rows, grid_cols):
    empty_strip = jnp.zeros((2, strip_rows, grid_cols), jnp.float32)
    zero_index = jnp.zeros((), jnp.int32)

    def add_one(which, current):
        row_at = row_corner[which]
        col_at = col_corner[which]
        window = lax.dynamic_slice(current, (zero_index, row_at, col_at), (2, SUB, SUB))
        return lax.dynamic_update_slice(
            current, window + subgrids[which], (zero_index, row_at, col_at)
        )

    return lax.fori_loop(0, subgrids.shape[0], add_one, empty_strip)


def on_device(visibilities, uv_coords, block_slot, slot_table):
    shard_count = lax.axis_size("bl")
    my_shard = lax.axis_index("bl")
    blocks = uv_coords.shape[0]
    slots = slot_table.shape[1]
    samples = uv_coords.shape[2]
    strip_rows = G // shard_count
    packed = jnp.concatenate([visibilities[0], uv_coords], axis=1)
    capacity = blocks // 2
    shard_lists = block_slot.reshape(shard_count, blocks)
    owners = shard_lists // slots
    owner_hits = (
        owners[:, :, None] == jnp.arange(shard_count, dtype=jnp.int32)[None, None, :]
    ).astype(jnp.int32)
    rank_in_owner = jnp.sum((jnp.cumsum(owner_hits, axis=1) - owner_hits) * owner_hits, axis=2)
    my_owners = lax.dynamic_index_in_dim(owners, my_shard, 0, keepdims=False)
    my_ranks = lax.dynamic_index_in_dim(rank_in_owner, my_shard, 0, keepdims=False)
    outgoing = jnp.zeros((shard_count * capacity, 4, samples), jnp.bfloat16)
    outgoing = outgoing.at[my_owners * capacity + my_ranks].set(packed)
    incoming = lax.all_to_all(
        outgoing.reshape(shard_count, capacity, 4, samples),
        "bl",
        split_axis=0,
        concat_axis=0,
        tiled=True,
    )
    arrival_rows = jnp.where(owners == my_shard, rank_in_owner, capacity)
    source_rows = jnp.broadcast_to(jnp.arange(shard_count, dtype=jnp.int32)[:, None], owners.shape)
    slot_ids = jnp.full((shard_count, capacity), -1, jnp.int32)
    slot_ids = slot_ids.at[source_rows, arrival_rows].set(
        shard_lists - my_shard * slots, mode="drop"
    )
    images = slot_sums(
        incoming.reshape(shard_count * capacity, 4, samples),
        slot_ids.reshape(shard_count * capacity),
        slots,
    )
    subgrids = subgrid_transform(images, slot_table[2])
    row_corner = slot_table[0] - my_shard * strip_rows
    col_corner = slot_table[1]
    strip = place_dense(subgrids, row_corner, col_corner, strip_rows, G)
    own_part = lax.psum_scatter(strip, "chan", scatter_dimension=2, tiled=True)
    partner = partner_2(own_part, "pol", 0)
    stokes_sign = 1.0 - 2.0 * lax.axis_index("pol").astype(jnp.float32)
    return (0.5 * (partner + stokes_sign * own_part))[None]


def solution(mesh):
    return jax.shard_map(
        on_device,
        mesh=mesh,
        in_specs=(
            P("pol", ("chan", "bl"), None, None),
            P(("chan", "bl"), None, None),
            P("chan"),
            P(None, ("chan", "bl")),
        ),
        out_specs=P("pol", None, "bl", "chan"),
        check_vma=False,
    )
```

profile of v0, /device:TPU:0, one launch (start us, length us, event | category | flops | bytes accessed | tf_op | source)
XLA Modules:
  0.0 1366.8 jit_solution(12747484511065041569)
XLA Ops:
  8.1 4.6 reduce-window.6
  14.1 4.1 pad_maximum_fusion.1
  18.2 3.8 broadcast_in_dim.21
  22.0 132.2 %scatter_fusion = bf16[2560,4,256]{2,1,0:T(4,128)(2,1)} fusion(bf16[2560,4,256]{2,1,0:T(4,128)(2,1)} %broadcast_in_dim.21, s32[1280]{0:T(1024)S(1)} %fusion.78, bf16[1280,4,256]{2,1,0:T(4,128)(2,1)S(1)} %pad_maximum_fusion.1), kind=kCustom, calls=%fused_computation | custom fusion | bytes 7869440 | tf_op jit(solution)/shard_map/scatter | solution.py:146
  154.2 5.7 copy.24
  159.9 5.2 all-to-all-start
  165.5 19.4 %scatter_custom_fusion.1 = s32[2560]{0:T(1024)S(1)} fusion(s32[5120]{0:T(1024)S(1)} %reshape.317, s32[5120]{0:T(1024)S(1)} %reshape.319, s32[]{:T(128)} %constant.162.clone.1), kind=kCustom, calls=%fused_computation.132 | custom fusion | bytes 10244
  185.3 39.9 %all-to-all-done = bf16[4,640,4,256]{3,1,2,0:T(8,128)(2,1)} async-done(((bf16[4,640,4,256]{3,1,2,0:T(8,128)(2,1)}), bf16[4,640,4,256]{3,1,2,0:T(8,128)(2,1)}, u32[]{:S(2)}, u32[]{:S(2)}) %all-to-all-start) | async-done | bytes 5242912 | tf_op jit(solution)/shard_map/all_to_all | solution.py:147
  225.2 5.3 copy.25
  230.5 817.6 %while.27 = (s32[]{:T(128)}, f32[16,2048]{1,0:T(8,128)S(1)}, s32[20,128]{1,0:T(8,128)S(1)}, bf16[20,128,4,256]{3,1,0,2:T(8,128)(2,1)}, s32[]{:T(128)}, /*index=5*/s32[]{:T(128)}) while((s32[]{:T(128)}, f32[16,2048]{1,0:T(8,128)S(1)}, s32[20,128]{1,0:T(8,128)S(1)}, bf16[20,128,4,256]{3,1,0,2:T(8,128)(2,1)}, s32[]{:T(128)}, ...), condition=%wide.region_6.7_spmd.clone, body=%wide.region_5.6_spmd.clone.sunk | while | flops 348981312 | bytes 29362004 | solution.py:72
  231.5 31.0 %fusion.138 = (bf16[128,32,256]{2,1,0:T(8,128)(2,1)S(1)}, bf16[128,32,256]{2,1,0:T(8,128)(2,1)S(1)}, bf16[128,32,256]{2,1,0:T(8,128)(2,1)S(1)}, bf16[128,32,256]{2,1,0:T(8,128)(2,1)S(1)}) fusion(f32[128,256]{1,0:T(8,128)S(1)} %get-tuple-element.310, f32[128,256]{1,0:T(8,128)S(1)} %get-tuple-element.311, f32[128,256]{1,0:T(8,128)S(1)} %get-tuple-element.312, ...), kind=kLoop, calls=%fused_computation.13.clone.1 | loop fusion | flops 12582912 | bytes 8913024 | tf_op jit(solution)/shard_map/convert
  272.4 31.0 %fusion.138 = (bf16[128,32,256]{2,1,0:T(8,128)(2,1)S(1)}, bf16[128,32,256]{2,1,0:T(8,128)(2,1)S(1)}, bf16[128,32,256]{2,1,0:T(8,128)(2,1)S(1)}, bf16[128,32,256]{2,1,0:T(8,128)(2,1)S(1)}) fusion(f32[128,256]{1,0:T(8,128)S(1)} %get-tuple-element.310, f32[128,256]{1,0:T(8,128)S(1)} %get-tuple-element.311, f32[128,256]{1,0:T(8,128)S(1)} %get-tuple-element.312, ...), kind=kLoop, calls=%fused_computation.13.clone.1 | loop fusion | flops 12582912 | bytes 8913024 | tf_op jit(solution)/shard_map/convert
  313.2 31.0 %fusion.138 = (bf16[128,32,256]{2,1,0:T(8,128)(2,1)S(1)}, bf16[128,32,256]{2,1,0:T(8,128)(2,1)S(1)}, bf16[128,32,256]{2,1,0:T(8,128)(2,1)S(1)}, bf16[128,32,256]{2,1,0:T(8,128)(2,1)S(1)}) fusion(f32[128,256]{1,0:T(8,128)S(1)} %get-tuple-element.310, f32[128,256]{1,0:T(8,128)S(1)} %get-tuple-element.311, f32[128,256]{1,0:T(8,128)S(1)} %get-tuple-element.312, ...), kind=kLoop, calls=%fused_computation.13.clone.1 | loop fusion | flops 12582912 | bytes 8913024 | tf_op jit(solution)/shard_map/convert
  354.1 31.0 %fusion.138 = (bf16[128,32,256]{2,1,0:T(8,128)(2,1)S(1)}, bf16[128,32,256]{2,1,0:T(8,128)(2,1)S(1)}, bf16[128,32,256]{2,1,0:T(8,128)(2,1)S(1)}, bf16[128,32,256]{2,1,0:T(8,128)(2,1)S(1)}) fusion(f32[128,256]{1,0:T(8,128)S(1)} %get-tuple-element.310, f32[128,256]{1,0:T(8,128)S(1)} %get-tuple-element.311, f32[128,256]{1,0:T(8,128)S(1)} %get-tuple-element.312, ...), kind=kLoop, calls=%fused_computation.13.clone.1 | loop fusion | flops 12582912 | bytes 8913024 | tf_op jit(solution)/shard_map/convert
  395.0 31.0 %fusion.138 = (bf16[128,32,256]{2,1,0:T(8,128)(2,1)S(1)}, bf16[128,32,256]{2,1,0:T(8,128)(2,1)S(1)}, bf16[128,32,256]{2,1,0:T(8,128)(2,1)S(1)}, bf16[128,32,256]{2,1,0:T(8,128)(2,1)S(1)}) fusion(f32[128,256]{1,0:T(8,128)S(1)} %get-tuple-element.310, f32[128,256]{1,0:T(8,128)S(1)} %get-tuple-element.311, f32[128,256]{1,0:T(8,128)S(1)} %get-tuple-element.312, ...), kind=kLoop, calls=%fused_computation.13.clone.1 | loop fusion | flops 12582912 | bytes 8913024 | tf_op jit(solution)/shard_map/convert
  435.8 31.0 %fusion.138 = (bf16[128,32,256]{2,1,0:T(8,128)(2,1)S(1)}, bf16[128,32,256]{2,1,0:T(8,128)(2,1)S(1)}, bf16[128,32,256]{2,1,0:T(8,128)(2,1)S(1)}, bf16[128,32,256]{2,1,0:T(8,128)(2,1)S(1)}) fusion(f32[128,256]{1,0:T(8,128)S(1)} %get-tuple-element.310, f32[128,256]{1,0:T(8,128)S(1)} %get-tuple-element.311, f32[128,256]{1,0:T(8,128)S(1)} %get-tuple-element.312, ...), kind=kLoop, calls=%fused_computation.13.clone.1 | loop fusion | flops 12582912 | bytes 8913024 | tf_op jit(solution)/shard_map/convert
  476.7 31.0 %fusion.138 = (bf16[128,32,256]{2,1,0:T(8,128)(2,1)S(1)}, bf16[128,32,256]{2,1,0:T(8,128)(2,1)S(1)}, bf16[128,32,256]{2,1,0:T(8,128)(2,1)S(1)}, bf16[128,32,256]{2,1,0:T(8,128)(2,1)S(1)}) fusion(f32[128,256]{1,0:T(8,128)S(1)} %get-tuple-element.310, f32[128,256]{1,0:T(8,128)S(1)} %get-tuple-element.311, f32[128,256]{1,0:T(8,128)S(1)} %get-tuple-element.312, ...), kind=kLoop, calls=%fused_computation.13.clone.1 | loop fusion | flops 12582912 | bytes 8913024 | tf_op jit(solution)/shard_map/convert
  517.6 31.0 %fusion.138 = (bf16[128,32,256]{2,1,0:T(8,128)(2,1)S(1)}, bf16[128,32,256]{2,1,0:T(8,128)(2,1)S(1)}, bf16[128,32,256]{2,1,0:T(8,128)(2,1)S(1)}, bf16[128,32,256]{2,1,0:T(8,128)(2,1)S(1)}) fusion(f32[128,256]{1,0:T(8,128)S(1)} %get-tuple-element.310, f32[128,256]{1,0:T(8,128)S(1)} %get-tuple-element.311, f32[128,256]{1,0:T(8,128)S(1)} %get-tuple-element.312, ...), kind=kLoop, calls=%fused_computation.13.clone.1 | loop fusion | flops 12582912 | bytes 8913024 | tf_op jit(solution)/shard_map/convert
  558.5 31.0 %fusion.138 = (bf16[128,32,256]{2,1,0:T(8,128)(2,1)S(1)}, bf16[128,32,256]{2,1,0:T(8,128)(2,1)S(1)}, bf16[128,32,256]{2,1,0:T(8,128)(2,1)S(1)}, bf16[128,32,256]{2,1,0:T(8,128)(2,1)S(1)}) fusion(f32[128,256]{1,0:T(8,128)S(1)} %get-tuple-element.310, f32[128,256]{1,0:T(8,128)S(1)} %get-tuple-element.311, f32[128,256]{1,0:T(8,128)S(1)} %get-tuple-element.312, ...), kind=kLoop, calls=%fused_computation.13.clone.1 | loop fusion | flops 12582912 | bytes 8913024 | tf_op jit(solution)/shard_map/convert
  599.3 31.0 %fusion.138 = (bf16[128,32,256]{2,1,0:T(8,128)(2,1)S(1)}, bf16[128,32,256]{2,1,0:T(8,128)(2,1)S(1)}, bf16[128,32,256]{2,1,0:T(8,128)(2,1)S(1)}, bf16[128,32,256]{2,1,0:T(8,128)(2,1)S(1)}) fusion(f32[128,256]{1,0:T(8,128)S(1)} %get-tuple-element.310, f32[128,256]{1,0:T(8,128)S(1)} %get-tuple-element.311, f32[128,256]{1,0:T(8,128)S(1)} %get-tuple-element.312, ...), kind=kLoop, calls=%fused_computation.13.clone.1 | loop fusion | flops 12582912 | bytes 8913024 | tf_op jit(solution)/shard_map/convert
  640.2 31.0 %fusion.138 = (bf16[128,32,256]{2,1,0:T(8,128)(2,1)S(1)}, bf16[128,32,256]{2,1,0:T(8,128)(2,1)S(1)}, bf16[128,32,256]{2,1,0:T(8,128)(2,1)S(1)}, bf16[128,32,256]{2,1,0:T(8,128)(2,1)S(1)}) fusion(f32[128,256]{1,0:T(8,128)S(1)} %get-tuple-element.310, f32[128,256]{1,0:T(8,128)S(1)} %get-tuple-element.311, f32[128,256]{1,0:T(8,128)S(1)} %get-tuple-element.312, ...), kind=kLoop, calls=%fused_computation.13.clone.1 | loop fusion | flops 12582912 | bytes 8913024 | tf_op jit(solution)/shard_map/convert
  681.1 31.0 %fusion.138 = (bf16[128,32,256]{2,1,0:T(8,128)(2,1)S(1)}, bf16[128,32,256]{2,1,0:T(8,128)(2,1)S(1)}, bf16[128,32,256]{2,1,0:T(8,128)(2,1)S(1)}, bf16[128,32,256]{2,1,0:T(8,128)(2,1)S(1)}) fusion(f32[128,256]{1,0:T(8,128)S(1)} %get-tuple-element.310, f32[128,256]{1,0:T(8,128)S(1)} %get-tuple-element.311, f32[128,256]{1,0:T(8,128)S(1)} %get-tuple-element.312, ...), kind=kLoop, calls=%fused_computation.13.clone.1 | loop fusion | flops 12582912 | bytes 8913024 | tf_op jit(solution)/shard_map/convert
  722.0 31.0 %fusion.138 = (bf16[128,32,256]{2,1,0:T(8,128)(2,1)S(1)}, bf16[128,32,256]{2,1,0:T(8,128)(2,1)S(1)}, bf16[128,32,256]{2,1,0:T(8,128)(2,1)S(1)}, bf16[128,32,256]{2,1,0:T(8,128)(2,1)S(1)}) fusion(f32[128,256]{1,0:T(8,128)S(1)} %get-tuple-element.310, f32[128,256]{1,0:T(8,128)S(1)} %get-tuple-element.311, f32[128,256]{1,0:T(8,128)S(1)} %get-tuple-element.312, ...), kind=kLoop, calls=%fused_computation.13.clone.1 | loop fusion | flops 12582912 | bytes 8913024 | tf_op jit(solution)/shard_map/convert
  762.8 31.0 %fusion.138 = (bf16[128,32,256]{2,1,0:T(8,128)(2,1)S(1)}, bf16[128,32,256]{2,1,0:T(8,128)(2,1)S(1)}, bf16[128,32,256]{2,1,0:T(8,128)(2,1)S(1)}, bf16[128,32,256]{2,1,0:T(8,128)(2,1)S(1)}) fusion(f32[128,256]{1,0:T(8,128)S(1)} %get-tuple-element.310, f32[128,256]{1,0:T(8,128)S(1)} %get-tuple-element.311, f32[128,256]{1,0:T(8,128)S(1)} %get-tuple-element.312, ...), kind=kLoop, calls=%fused_computation.13.clone.1 | loop fusion | flops 12582912 | bytes 8913024 | tf_op jit(solution)/shard_map/convert
  803.7 31.0 %fusion.138 = (bf16[128,32,256]{2,1,0:T(8,128)(2,1)S(1)}, bf16[128,32,256]{2,1,0:T(8,128)(2,1)S(1)}, bf16[128,32,256]{2,1,0:T(8,128)(2,1)S(1)}, bf16[128,32,256]{2,1,0:T(8,128)(2,1)S(1)}) fusion(f32[128,256]{1,0:T(8,128)S(1)} %get-tuple-element.310, f32[128,256]{1,0:T(8,128)S(1)} %get-tuple-element.311, f32[128,256]{1,0:T(8,128)S(1)} %get-tuple-element.312, ...), kind=kLoop, calls=%fused_computation.13.clone.1 | loop fusion | flops 12582912 | bytes 8913024 | tf_op jit(solution)/shard_map/convert
  844.6 31.0 %fusion.138 = (bf16[128,32,256]{2,1,0:T(8,128)(2,1)S(1)}, bf16[128,32,256]{2,1,0:T(8,128)(2,1)S(1)}, bf16[128,32,256]{2,1,0:T(8,128)(2,1)S(1)}, bf16[128,32,256]{2,1,0:T(8,128)(2,1)S(1)}) fusion(f32[128,256]{1,0:T(8,128)S(1)} %get-tuple-element.310, f32[128,256]{1,0:T(8,128)S(1)} %get-tuple-element.311, f32[128,256]{1,0:T(8,128)S(1)} %get-tuple-element.312, ...), kind=kLoop, calls=%fused_computation.13.clone.1 | loop fusion | flops 12582912 | bytes 8913024 | tf_op jit(solution)/shard_map/convert
  885.4 31.0 %fusion.138 = (bf16[128,32,256]{2,1,0:T(8,128)(2,1)S(1)}, bf16[128,32,256]{2,1,0:T(8,128)(2,1)S(1)}, bf16[128,32,256]{2,1,0:T(8,128)(2,1)S(1)}, bf16[128,32,256]{2,1,0:T(8,128)(2,1)S(1)}) fusion(f32[128,256]{1,0:T(8,128)S(1)} %get-tuple-element.310, f32[128,256]{1,0:T(8,128)S(1)} %get-tuple-element.311, f32[128,256]{1,0:T(8,128)S(1)} %get-tuple-element.312, ...), kind=kLoop, calls=%fused_computation.13.clone.1 | loop fusion | flops 12582912 | bytes 8913024 | tf_op jit(solution)/shard_map/convert
  926.3 31.0 %fusion.138 = (bf16[128,32,256]{2,1,0:T(8,128)(2,1)S(1)}, bf16[128,32,256]{2,1,0:T(8,128)(2,1)S(1)}, bf16[128,32,256]{2,1,0:T(8,128)(2,1)S(1)}, bf16[128,32,256]{2,1,0:T(8,128)(2,1)S(1)}) fusion(f32[128,256]{1,0:T(8,128)S(1)} %get-tuple-element.310, f32[128,256]{1,0:T(8,128)S(1)} %get-tuple-element.311, f32[128,256]{1,0:T(8,128)S(1)} %get-tuple-element.312, ...), kind=kLoop, calls=%fused_computation.13.clone.1 | loop fusion | flops 12582912 | bytes 8913024 | tf_op jit(solution)/shard_map/convert
  967.2 31.0 %fusion.138 = (bf16[128,32,256]{2,1,0:T(8,128)(2,1)S(1)}, bf16[128,32,256]{2,1,0:T(8,128)(2,1)S(1)}, bf16[128,32,256]{2,1,0:T(8,128)(2,1)S(1)}, bf16[128,32,256]{2,1,0:T(8,128)(2,1)S(1)}) fusion(f32[128,256]{1,0:T(8,128)S(1)} %get-tuple-element.310, f32[128,256]{1,0:T(8,128)S(1)} %get-tuple-element.311, f32[128,256]{1,0:T(8,128)S(1)} %get-tuple-element.312, ...), kind=kLoop, calls=%fused_computation.13.clone.1 | loop fusion | flops 12582912 | bytes 8913024 | tf_op jit(solution)/shard_map/convert
  1008.0 31.0 %fusion.138 = (bf16[128,32,256]{2,1,0:T(8,128)(2,1)S(1)}, bf16[128,32,256]{2,1,0:T(8,128)(2,1)S(1)}, bf16[128,32,256]{2,1,0:T(8,128)(2,1)S(1)}, bf16[128,32,256]{2,1,0:T(8,128)(2,1)S(1)}) fusion(f32[128,256]{1,0:T(8,128)S(1)} %get-tuple-element.310, f32[128,256]{1,0:T(8,128)S(1)} %get-tuple-element.311, f32[128,256]{1,0:T(8,128)S(1)} %get-tuple-element.312, ...), kind=kLoop, calls=%fused_computation.13.clone.1 | loop fusion | flops 12582912 | bytes 8913024 | tf_op jit(solution)/shard_map/convert
  1056.8 4.3 broadcast_in_dim.16
  1061.1 143.9 %while.26 = (s32[]{:T(128)}, f32[2,512,2048]{2,1,0:T(8,128)}, s32[16]{0:T(128)S(1)}, s32[16]{0:T(128)S(1)}, f32[16,2,32,32]{3,2,0,1:T(8,128)S(1)}, /*index=5*/s32[]{:T(128)}, s32[]{:T(128)}, s32[]{:T(128)}, s32[]{:T(128)}) while((s32[]{:T(128)}, f32[2,512,2048]{2,1,0:T(8,128)}, s32[16]{0:T(128)S(1)}, s32[16]{0:T(128)S(1)}, ...), condition=%wide.region_8.9_spmd, body=%wide.region_7.8_spmd.sunk | while | flops 2056 | bytes 41161 | solution.py:125
  1067.1 3.1 dynamic_update_slice.8
  1076.3 3.1 dynamic_update_slice.8
  1085.4 3.1 dynamic_update_slice.8
  1094.6 3.1 dynamic_update_slice.8
  1103.7 3.1 dynamic_update_slice.8
  1112.8 3.1 dynamic_update_slice.8
  1121.9 3.1 dynamic_update_slice.8
  1131.0 3.1 dynamic_update_slice.8
  1140.2 3.1 dynamic_update_slice.8
  1149.3 3.1 dynamic_update_slice.8
  1175.3 3.1 dynamic_update_slice.8
  1184.4 3.1 dynamic_update_slice.8
  1193.5 3.1 dynamic_update_slice.8
  1205.1 147.1 %reduce-scatter.2.cloned.1.call-done = f32[2,512,512]{2,1,0:T(8,128)} async-done(((f32[2,512,2048]{2,1,0:T(8,128)}), f32[2,512,512]{2,1,0:T(8,128)}) %reduce-scatter.2.cloned.1.call-update) | async-done | bytes 2097168 | tf_op jit(solution)/shard_map/reduce_scatter | solution.py:169
  1352.1 4.4 collective-permute-done
  1356.5 3.4 multiply_bitcast_fusion.4
  (302 shorter events, 249.9 us)
Async XLA Ops:
  159.9 5.3 copy-start
  159.9 5.4 copy-start.2
  159.9 5.5 copy-start.1
  159.9 25.2 %copy-start.3 = (s32[3,16]{1,0:T(4,128)S(1)}, s32[3,16]{1,0:T(4,128)}, u32[]{:S(2)}) copy-start(s32[3,16]{1,0:T(4,128)} %param.11) | copy-start | bytes 580
  159.9 65.3 %all-to-all-start = ((bf16[4,640,4,256]{3,1,2,0:T(8,128)(2,1)}), bf16[4,640,4,256]{3,1,2,0:T(8,128)(2,1)}, u32[]{:S(2)}, u32[]{:S(2)}) async-start(bf16[4,640,4,256]{3,1,2,0:T(8,128)(2,1)} %copy.24), calls=%async_computation | async-start | bytes 10485760 | tf_op jit(solution)/shard_map/all_to_all | solution.py:147
  165.1 1187.0 %reduce-scatter.2.cloned.1.call-start = ((), (), s32[]{:S(2)}) async-start(), calls=%async_computation.2 | async-start | bytes 10485760 | tf_op jit(solution)/shard_map/reduce_scatter | solution.py:169
  1352.1 4.4 collective-permute-start
Sparse Core Ops, SparseCore 0:
  1205.2 146.8 reduce-scatter.1
where the time goes:
time: 1380 us; the launch traced here: 1370 us
  other arithmetic  700 us (51%)
  local copies, waits for them, and re-layouts  338 us (24%)
  waiting for transfers between devices  191 us (14%)
  loops' own time  63.9 us (5%)
  matrix products  54.4 us (4%)
    another operation x23, other arithmetic  625 us
    reduce_scatter x1, waiting for transfers between devices, on_device(): own_part = lax.psum_scatter(strip, 'chan', scatter_dimension=2, tiled=True)  147 us
    scatter x1, local copies, waits for them, and re-layouts, on_device(): outgoing = outgoing.at[my_owners * capacity + my_ranks].set(packed)  132 us
    another operation x40, local copies, waits for them, and re-layouts, kernel_images(): jnp.stack([real_part, imag_part], axis=1)  78.5 us
    another operation x1, loops' own time, place_dense(): return lax.fori_loop(0, subgrids.shape[0], add_one, empty_strip)  62.2 us
    another operation x40, other arithmetic, kernel_images(): jnp.stack([real_part, imag_part], axis=1)  50.4 us
    dynamic_update_slice x16, local copies, waits for them, and re-layouts, add_one(): lax.dynamic_update_slice(current, window + subgrids[which], (zero_index,...  47.5 us
    all_to_all x1, waiting for transfers between devices, on_device(): lax.all_to_all(outgoing.reshape(shard_count, capacity, 4, samples), 'bl',...  39.9 us
  transfers between devices with their start and end apart: 3, of which 3 were waited for; matrix products, arithmetic and copies ran while one was open for 1% of the time, Pallas kernels for 0%

commit v1 on v0

v1 whole, which is shorter than its diff:
```python
import functools
import math

import jax
import jax.numpy as jnp
import numpy as np
from jax import lax
from jax.experimental import pallas as pl
from jax.experimental.pallas import tpu as pltpu
from jax.sharding import PartitionSpec as P

G = 2048
SUB = 32
VB = 256
HALF = SUB // 2
LANES = 128
ROWS = 40
W_STEP = 0.25
highest = lax.Precision.HIGHEST
f32 = jnp.float32
bf16 = jnp.bfloat16


def cos_sin(angle, terms):
    square = angle * angle
    cos_sum = f32((-1.0) ** (terms - 1) / math.factorial(2 * terms - 2))
    sin_sum = f32((-1.0) ** (terms - 1) / math.factorial(2 * terms - 1))
    for n in range(terms - 2, -1, -1):
        cos_sum = cos_sum * square + f32((-1.0) ** n / math.factorial(2 * n))
        sin_sum = sin_sum * square + f32((-1.0) ** n / math.factorial(2 * n + 1))
    return cos_sum, sin_sum * angle


def multiples(coords):
    c_half, s_half = cos_sin(coords * (math.pi / SUB), 6)
    cosines = {1: 1.0 - 2.0 * s_half * s_half}
    sines = {1: 2.0 * s_half * c_half}
    for k in range(2, HALF + 1):
        base = 1 << ((k - 1).bit_length() - 1)
        twice = 2.0 * cosines[base]
        if k == 2 * base:
            cosines[k] = twice * cosines[base] - 1.0
            sines[k] = twice * sines[base]
        else:
            cosines[k] = twice * cosines[k - base] - cosines[2 * base - k]
            sines[k] = twice * sines[k - base] + sines[2 * base - k]
    return cosines, sines


GROUP = 8
BATCH = 2


def phases(start, scale, inputs, angles, values, coords):
    first, uv_ref, mine_ref, theirs_ref = inputs
    for group in range(BATCH):
        block = start + group * GROUP
        there = pl.ds(pl.multiple_of(block * 4, 4 * GROUP), 4 * GROUP)
        here = pl.ds(pl.multiple_of(first + block * 4, 4 * GROUP), 4 * GROUP)
        coords[...] = uv_ref[here, :].astype(f32)
        for part in range(2):
            for side in range(2):
                at = (group * 2 + part) * 8 * SUB
                cosines, sines = multiples(coords[pl.ds(part * 16 + side, 8, 2), :])
                for k in range(1, HALF + 1):
                    angles[side, at + (k - 1) * 8 : at + k * 8, :] = cosines[k]
                    angles[side, at + (HALF + k - 1) * 8 : at + (HALF + k) * 8, :] = sines[k]
        rows = slice(group * 4 * GROUP, (group + 1) * 4 * GROUP)
        values[0, rows, :] = mine_ref[here, :].astype(f32) * scale
        values[1, rows, :] = theirs_ref[there, :].astype(f32) * scale


def operands(angles, values, left, right):
    last = lax.broadcasted_iota(jnp.int32, (HALF, LANES), 0) == HALF - 1
    for block in range(BATCH * GROUP):
        for half in range(2):
            chunk = 2 * block + half
            lanes = slice(half * LANES, (half + 1) * LANES)
            at = pl.ds(chunk // 8 * 8 * SUB + chunk % 8, SUB, 8)
            left[block, :SUB, lanes] = angles[0, at, :].astype(bf16)
            phase = angles[1, at, :]
            cosine, sine = phase[:HALF], phase[HALF:]
            row = 0
            for product in range(2):
                real = values[product, 2 * chunk : 2 * chunk + 1, :]
                imag = values[product, 2 * chunk + 1 : 2 * chunk + 2, :]
                rc, is_, rs, ic = real * cosine, imag * sine, real * sine, imag * cosine
                for up, down, centre in ((rc - is_, rc + is_, real), (ic + rs, ic - rs, imag)):
                    right[block, row : row + HALF, lanes] = jnp.where(last, centre, up).astype(bf16)
                    right[block, row + HALF : row + SUB, lanes] = down.astype(bf16)
                    row += SUB


def products(id_at, ids_ref, left, right, sums):
    for block in range(BATCH * GROUP):
        image = lax.dot_general(
            left[block], right[block], (((1,), (1,)), ((), ())), preferred_element_type=f32
        )
        at = pl.ds(pl.multiple_of(ids_ref[id_at + block] * ROWS, 8), ROWS)
        sums[at, :] += image[:ROWS]


def slot_sums_kernel(place_ref, sign_ref, ids_ref, uv_ref, mine_ref, theirs_ref, keep_ref, send_ref, sums, *scratch):
    blocks = theirs_ref.shape[0] // 4
    step = BATCH * GROUP
    first = place_ref[0]
    id_at = place_ref[1]
    scale = 0.5 / math.sqrt(VB)
    inputs = (first * 4, uv_ref, mine_ref, theirs_ref)
    even, odd = scratch[:5], scratch[5:]
    sums[...] = jnp.zeros_like(sums)
    for left in (even[2], odd[2]):
        left[...] = jnp.ones_like(left)

    def fill(start, buffers):
        angles, values, left, right, coords = buffers
        phases(start, scale, inputs, angles, values, coords)
        operands(angles, values, left, right)

    fill(0, even)

    def two_batches(trip, carry):
        start = trip * 2 * step
        products(id_at + start, ids_ref, even[2], even[3], sums)
        fill(start + step, odd)
        products(id_at + start + step, ids_ref, odd[2], odd[3], sums)
        fill(jnp.minimum(start + 2 * step, blocks - step), even)
        return carry

    lax.fori_loop(0, blocks // (2 * step), two_batches, 0)

    owners = keep_ref.shape[0]
    pairs = sums.shape[0] // ROWS // owners // 2
    sign = sign_ref[0]
    low = lax.broadcasted_iota(jnp.int32, (1, LANES), 1) < LANES // 2

    def store(owner, rows, one, two):
        one_back, two_back = pltpu.roll(one, LANES // 2, 1), pltpu.roll(two, LANES // 2, 1)
        own = jnp.where(low, one_back + sign * one, two + sign * two_back)
        other = jnp.where(low, one - sign * one_back, two_back - sign * two)
        keep_ref[owner, rows, :] = own.astype(keep_ref.dtype)
        send_ref[owner, rows, :] = other.astype(send_ref.dtype)

    def store_owner(owner, carry):
        base = owner * (2 * pairs * ROWS)

        def rows_of(slot, row, count):
            return sums[pl.ds(pl.multiple_of(base + slot * ROWS + row, 8), count), :]

        for pair in range(pairs):
            store(
                owner, slice(pair * SUB, (pair + 1) * SUB), rows_of(pair, 0, SUB), rows_of(pairs + pair, 0, SUB)
            )
        blank = [jnp.zeros((16 - pairs, LANES), f32)]
        one = jnp.concatenate([rows_of(pair, SUB, 8)[:1] for pair in range(pairs)] + blank, axis=0)
        two = jnp.concatenate([rows_of(pairs + pair, SUB, 8)[:1] for pair in range(pairs)] + blank, axis=0)
        store(owner, slice(pairs * SUB, pairs * SUB + 16), one, two)
        return carry

    lax.fori_loop(0, owners, store_owner, 0)


def slot_sums(place, sign, block_slot, uv, mine, theirs, shard_count, slots):
    pairs = slots // 2
    rows = pairs * SUB + 16
    vmem = pl.BlockSpec(memory_space=pltpu.VMEM)
    smem = pl.BlockSpec(memory_space=pltpu.SMEM)
    buffers = [
        pltpu.VMEM((2, BATCH * 2 * GROUP * SUB, LANES), f32),
        pltpu.VMEM((2, BATCH * 4 * GROUP, LANES), f32),
        pltpu.VMEM((BATCH * GROUP, SUB + HALF, VB), bf16),
        pltpu.VMEM((BATCH * GROUP, 4 * SUB, VB), bf16),
        pltpu.VMEM((4 * GROUP, LANES), f32),
    ]
    return pl.pallas_call(
        slot_sums_kernel,
        out_shape=[
            jax.ShapeDtypeStruct((shard_count, rows, LANES), f32),
            jax.ShapeDtypeStruct((shard_count, rows, LANES), bf16),
        ],
        in_specs=[smem, smem, smem, vmem, vmem, vmem],
        out_specs=[vmem, vmem],
        scratch_shapes=[pltpu.VMEM((shard_count * slots * ROWS, LANES), f32)] + buffers + buffers,
        compiler_params=pltpu.CompilerParams(vmem_limit_bytes=32 * 1024 * 1024),
        cost_estimate=pl.CostEstimate(flops=60_000_000_000, bytes_accessed=4_000_000, transcendentals=0),
        name="slot_sums",
    )(place, sign, block_slot, uv, mine, theirs)


def row_order():
    return np.array(list(range(HALF + 1, SUB)) + [HALF] + list(range(HALF - 1, -1, -1)))


def dft_matrix():
    centred = np.arange(SUB) - HALF
    product_mod = centred[:, None] * centred[None, :] % SUB
    return np.exp(-2j * np.pi * product_mod / SUB) / math.sqrt(SUB)


def spread(matrix):
    parts = []
    for factor in (1, 1j):
        scaled = matrix * factor
        one = np.concatenate([scaled.real, scaled.imag], axis=1)
        parts.append(np.kron(np.eye(2), one))
    return np.concatenate(parts, axis=1).astype(np.float32)


def constants():
    order = row_order()
    dft = dft_matrix()
    cols = dft.T[order]
    columns = spread(np.concatenate([cols, 1j * cols], axis=0))
    rows = dft[:, order]
    rows = np.concatenate([rows.real, rows.imag], axis=1).astype(np.float32)
    offsets = (order - HALF) / SUB
    taper = np.sin(np.pi * (order + 0.5) / SUB)
    n_term = np.sqrt(1.0 - offsets[:, None] ** 2 - offsets[None, :] ** 2) - 1.0
    turns = np.tile(-W_STEP * n_term, (1, 4)).astype(np.float32)
    tapers = np.tile(taper[:, None] * taper[None, :], (1, 4)).astype(np.float32)
    return turns, tapers, columns, rows


def transform_kernel(planes_ref, sums_ref, turns_ref, tapers_ref, columns_ref, rows_ref, out_ref):
    pairs = out_ref.shape[0]
    plain = sums_ref[0].astype(f32)
    for source in range(1, sums_ref.shape[0]):
        plain = plain + sums_ref[source].astype(f32)
    lane = lax.broadcasted_iota(jnp.int32, (1, LANES), 1)
    turned = jnp.where(
        (lane // SUB) % 2 == 0, -pltpu.roll(plain, LANES - SUB, 1), pltpu.roll(plain, SUB, 1)
    )
    last = lax.broadcasted_iota(jnp.int32, (HALF, LANES), 0) == HALF - 1
    pieces = []
    for pair in range(pairs):
        at = pair * SUB
        cos_p, sin_p = plain[at : at + HALF], plain[at + HALF : at + SUB]
        cos_t, sin_t = turned[at : at + HALF], turned[at + HALF : at + SUB]
        zero = pairs * SUB + pair
        up = jnp.where(last, plain[zero : zero + 1], cos_p + sin_t)
        up_i = jnp.where(last, turned[zero : zero + 1], cos_t - sin_p)
        image = jnp.concatenate([up, cos_p - sin_t], axis=0)
        image_i = jnp.concatenate([up_i, cos_t + sin_p], axis=0)
        plane = jnp.where(lane < LANES // 2, planes_ref[pair], planes_ref[pairs + pair]).astype(f32)
        turns = plane * turns_ref[...]
        c_half, s_half = cos_sin((turns - jnp.floor(turns + 0.5)) * math.pi, 7)
        screen_cos = (1.0 - 2.0 * s_half * s_half) * tapers_ref[...]
        screen_sin = (2.0 * s_half * c_half) * tapers_ref[...]
        pieces.append(image * screen_cos + image_i * screen_sin)
    both = jnp.dot(jnp.concatenate(pieces, axis=0), columns_ref[...], precision=highest, preferred_element_type=f32)
    for pair in range(pairs):
        at = slice(pair * SUB, (pair + 1) * SUB)
        stacked = jnp.concatenate([both[at, :LANES], both[at, LANES:]], axis=0)
        out_ref[pair] = jnp.dot(rows_ref[...], stacked, precision=highest, preferred_element_type=f32).astype(
            out_ref.dtype
        )


def subgrid_transform(sums, planes, slots):
    vmem = pl.BlockSpec(memory_space=pltpu.VMEM)
    smem = pl.BlockSpec(memory_space=pltpu.SMEM)
    return pl.pallas_call(
        transform_kernel,
        out_shape=jax.ShapeDtypeStruct((slots // 2, SUB, LANES), bf16),
        in_specs=[smem] + [vmem] * 5,
        out_specs=vmem,
        compiler_params=pltpu.CompilerParams(vmem_limit_bytes=32 * 1024 * 1024),
        name="subgrid_transform",
    )(planes, sums, *constants())


def place_kernel(origin_ref, *refs):
    count = (len(refs) - 3) // 2
    corner_refs, sub_refs = refs[:count], refs[count : 2 * count]
    out_ref, strip, sem = refs[2 * count :]
    pairs = sub_refs[0].shape[0]
    cols = out_ref.shape[2]
    strip[...] = jnp.zeros_like(strip)
    lane = lax.broadcasted_iota(jnp.int32, (SUB, LANES), 1)

    for corner_ref, sub_ref in zip(corner_refs, sub_refs):

        def add_pair(pair, carry):
            for half in range(2):
                row = corner_ref[0, half * pairs + pair] - origin_ref[0]
                col = corner_ref[1, half * pairs + pair] - origin_ref[1]

                @pl.when((col > -SUB) & (col < cols))
                def _():
                    padded = col + LANES
                    tile = padded // LANES
                    at = padded % LANES
                    piece = sub_ref[pair].astype(f32)
                    left = (lane >= at) & (lane < at + SUB)
                    right = lane < at + SUB - LANES
                    for part in range(2):
                        start = half * 2 * SUB + part * SUB
                        turned = pltpu.roll(piece, (at + (LANES - start)) % LANES, 1)
                        rows = pl.ds(row, SUB)
                        strip[part, tile, rows, :] += jnp.where(left, turned, 0.0)
                        strip[part, tile + 1, rows, :] += jnp.where(right, turned, 0.0)

            return carry

        lax.fori_loop(0, pairs, add_pair, 0)
    copies = [
        pltpu.make_async_copy(
            strip.at[part, tile + 1], out_ref.at[part, :, pl.ds(tile * LANES, LANES)], sem.at[part, tile]
        )
        for part in range(2)
        for tile in range(cols // LANES)
    ]
    for copy in copies:
        copy.start()
    for copy in copies:
        copy.wait()


def place(origin, corners, subs, strip_rows, cols):
    smem = pl.BlockSpec(memory_space=pltpu.SMEM)
    vmem = pl.BlockSpec(memory_space=pltpu.VMEM)
    return pl.pallas_call(
        place_kernel,
        out_shape=jax.ShapeDtypeStruct((2, strip_rows, cols), f32),
        in_specs=[smem] * (1 + len(corners)) + [vmem] * len(subs),
        out_specs=pl.BlockSpec(memory_space=pl.ANY),
        scratch_shapes=[
            pltpu.VMEM((2, cols // LANES + 2, strip_rows, LANES), f32),
            pltpu.SemaphoreType.DMA((2, cols // LANES)),
        ],
        compiler_params=pltpu.CompilerParams(vmem_limit_bytes=32 * 1024 * 1024),
        name="place",
    )(origin, *corners, *subs)


def around(block, axis):
    count = lax.axis_size(axis)
    return [block] + [
        lax.ppermute(block, axis, [(i, (i + step) % count) for i in range(count)]) for step in range(1, count)
    ]


def on_device(visibilities, uv_coords, block_slot, slot_table):
    shard_count = lax.axis_size("bl")
    chan_count = lax.axis_size("chan")
    my_shard = lax.axis_index("bl")
    my_chan = lax.axis_index("chan")
    my_pol = lax.axis_index("pol")
    blocks = uv_coords.shape[0]
    slots = slot_table.shape[1]
    half = blocks // 2
    strip_rows = G // shard_count
    cols = G // chan_count

    def rows_of(values):
        count = values.shape[0]
        return values.reshape(count, 2, VB // LANES, LANES).transpose(0, 2, 1, 3).reshape(count * 4, LANES)

    vis = rows_of(visibilities[0])
    theirs = lax.ppermute(
        lax.dynamic_slice_in_dim(vis, (1 - my_pol) * (half * 4), half * 4, 0), "pol", [(0, 1), (1, 0)]
    )
    corners = around(slot_table[:2], "chan")
    sign = (1.0 - 2.0 * my_pol.astype(f32))[None]
    at = jnp.stack([my_pol * half, my_shard * blocks + my_pol * half])
    keep, send = slot_sums(at, sign, block_slot, rows_of(uv_coords), vis, theirs, shard_count, slots)
    got = lax.ppermute(send, "pol", [(0, 1), (1, 0)])
    partial = (keep + got.astype(f32)).astype(bf16)
    partial = lax.all_to_all(partial, "bl", split_axis=0, concat_axis=0, tiled=True)
    subs = around(subgrid_transform(partial, slot_table[2], slots), "chan")
    origin = jnp.stack([my_shard * strip_rows, my_chan * cols])
    return place(origin, corners, subs, strip_rows, cols)[None]


def solution(mesh):
    return jax.shard_map(
        on_device,
        mesh=mesh,
        in_specs=(
            P("pol", ("chan", "bl"), None, None),
            P(("chan", "bl"), None, None),
            P("chan"),
            P(None, ("chan", "bl")),
        ),
        out_specs=P("pol", None, "bl", "chan"),
        check_vma=False,
    )
```

time: 1380 us -> 65.7 us (0.05)
  other arithmetic: 700 us -> 0.91 us
  local copies, waits for them, and re-layouts: 338 us -> 2.59 us
  waiting for transfers between devices: 191 us -> 12.9 us
  loops' own time: 63.9 us -> 0 us
  matrix products: 54.4 us -> 0 us
  Pallas kernels: 0 us -> 34.4 us
    another operation x64 -> x2, other arithmetic: 676 us -> 0.15 us  [the longest x1 0.07 us: on_device(): at = jnp.stack([my_pol * half, my_shard * blocks + my_pol * half])]
    reduce_scatter x1 -> x0, waiting for transfers between devices: 147 us -> none  [on_device(): own_part = lax.psum_scatter(strip, 'chan', scatter_dimension=2, tiled=True)]
    scatter x1 -> x0, local copies, waits for them, and re-layouts: 132 us -> none  [on_device(): outgoing = outgoing.at[my_owners * capacity + my_ranks].set(packed)]
    another operation x41 -> x0, local copies, waits for them, and re-layouts: 78.6 us -> none  [the longest x40 78.5 us: kernel_images(): jnp.stack([real_part, imag_part], axis=1)]
    another operation x2 -> x0, loops' own time: 63.9 us -> none  [the longest x1 62.2 us: place_dense(): return lax.fori_loop(0, subgrids.shape[0], add_one, empty_strip)]
    dot_general x48 -> x0, matrix products: 54.4 us -> none  [the longest x20 34.2 us: kernel_images(): jnp.einsum('kav,kbv->kab', left_phasor, right_phasor, preferred_element_t...]
    dynamic_update_slice x16 -> x0, local copies, waits for them, and re-layouts: 47.5 us -> none  [add_one(): lax.dynamic_update_slice(current, window + subgrids[which], (zero_index,...]
    all_to_all x1, waiting for transfers between devices: 39.9 us -> 5.41 us  [on_device(): lax.all_to_all(partial, 'bl', split_axis=0, concat_axis=0, tiled=True)]
  transfers between devices with their start and end apart: 3 -> 9, of which waited for: 3 -> 5; matrix products, arithmetic and copies ran while one was open for 1% -> 1% of each run, Pallas kernels for 0% -> 3%
where the time goes in v1:
time: 65.7 us; the launch traced here: 65.4 us
  Pallas kernels  34.4 us (52%)
  starting transfers between devices  14.5 us (22%)
  waiting for transfers between devices  12.9 us (20%)
  local copies, waits for them, and re-layouts  2.59 us (4%)
  other arithmetic  0.91 us (1%)
    pallas_call x1, Pallas kernels, slot_sums(): pl.pallas_call(slot_sums_kernel, out_shape=[jax.ShapeDtypeStruct((shard_c...  29.1 us
    ppermute x6, starting transfers between devices, around(): lax.ppermute(block, axis, [(i, (i + step) % count) for i in range(count)])  9.75 us
    ppermute x6, waiting for transfers between devices, around(): lax.ppermute(block, axis, [(i, (i + step) % count) for i in range(count)])  5.87 us
    all_to_all x1, waiting for transfers between devices, on_device(): lax.all_to_all(partial, 'bl', split_axis=0, concat_axis=0, tiled=True)  5.41 us
    all_to_all x1, starting transfers between devices, on_device(): lax.all_to_all(partial, 'bl', split_axis=0, concat_axis=0, tiled=True)  3.74 us
    pallas_call x1, Pallas kernels, place(): pl.pallas_call(place_kernel, out_shape=jax.ShapeDtypeStruct((2, strip_row...  3.58 us
    pallas_call x1, Pallas kernels, subgrid_transform(): pl.pallas_call(transform_kernel, out_shape=jax.ShapeDtypeStruct((slots //...  1.73 us
    ppermute x1, waiting for transfers between devices, on_device(): lax.ppermute(lax.dynamic_slice_in_dim(vis, (1 - my_pol) * (half * 4), hal...  1.65 us
  transfers between devices with their start and end apart: 9, of which 5 were waited for; matrix products, arithmetic and copies ran while one was open for 1% of the time, Pallas kernels for 3%

profile of v1, /device:TPU:0, one launch (start us, length us, event | category | flops | bytes accessed | tf_op | source)
XLA Modules:
  0.0 65.4 jit_solution(17191350851910135335)
XLA Ops:
  0.0 0.0 copy-start
  0.0 0.0 copy-start.6
  0.0 1.2 %constant_dynamic-slice_fusion = bf16[2560,128]{1,0:T(8,128)(2,1)S(1)} fusion(bf16[5120,128]{1,0:T(8,128)(2,1)} %bitcast.18, s32[]{:T(128)S(6)} %select_n.3), kind=kLoop, calls=%fused_computation.4 | loop fusion | bytes 1310724 | tf_op jit(solution)/shard_map/dynamic_slice | solution.py:361
  1.2 0.5 collective-permute-start.3
  1.8 0.1 pad_add_fusion.1.place_ref
  1.8 1.6 %collective-permute-done.3.theirs_ref = bf16[2560,128]{1,0:T(8,128)(2,1)S(1)} collective-permute-done((bf16[2560,128]{1,0:T(8,128)(2,1)S(1)}, bf16[2560,128]{1,0:T(8,128)(2,1)S(1)}, u32[]{:S(2)}, u32[]{:S(2)}) %collective-permute-start.3) | collective-permute-done | bytes 655392 | tf_op jit(solution)/shard_map/ppermute | solution.py:360
  3.5 0.0 copy-done
  3.5 0.0 copy-done.6
  3.5 0.0 copy-start.5
  3.5 1.3 %copy-done.5 = bf16[1280,2,256]{2,1,0:T(2,128)(2,1)S(1)} copy-done((bf16[1280,2,256]{2,1,0:T(2,128)(2,1)S(1)}, bf16[1280,2,256]{2,1,0:T(2,128)(2,1)}, u32[]{:S(2)}) %copy-start.5) | copy-done | bytes 1310744
  4.8 0.0 copy-start.7
  4.8 29.1 %slot_sums.1 = (f32[4,272,128]{2,1,0:T(8,128)S(1)}, bf16[4,272,128]{2,1,0:T(8,128)(2,1)S(1)}) custom-call(s32[2]{0:T(128)S(1)} %pad_add_fusion.1.place_ref, f32[1]{0:T(128)} %bitcast.5.sign_ref, s32[5120]{0:T(1024)S(1)} %copy-done.6, bf16[5120,128]{1,0:T(8,128)(2,1)S(1)} %bitcast.20, bf16[5120,128]{1,0:T(8,128)(2,1)S(1)} %bitcast.19, ...), custom_call_target="tpu_custom_call" | custom-call | flops 60000002048 | bytes 4000000 | tf_op jit(solution)/shard_map/slot_sums/pallas_call | solution.py:175
  34.0 0.0 copy-start.1
  34.0 0.0 copy-start.2
  34.0 0.0 copy-start.3
  34.0 0.0 copy-start.4
  34.0 0.4 collective-permute-start.4
  34.5 0.0 copy-done.7
  34.5 4.7 %collective-permute-start.2 = (s32[2,16]{1,0:T(2,128)S(1)}, s32[2,16]{1,0:T(2,128)S(1)}, u32[]{:S(2)}, u32[]{:S(2)}) collective-permute-start(s32[2,16]{1,0:T(2,128)S(1)} %slice.6.refs_0_), channel_id=1, source_target_pairs={{0,24},{8,0},{16,8},{24,16},{1,25},{9,1},{17,9},{25,17},{2,26},{10... | collective-permute-start | bytes 392 | tf_op jit(solution)/shard_map/ppermute | solution.py:339
  39.2 0.0 collective-permute-start.1
  39.2 1.0 %collective-permute-start = (s32[2,16]{1,0:T(2,128)S(1)}, s32[2,16]{1,0:T(2,128)S(1)}, u32[]{:S(2)}, u32[]{:S(2)}) collective-permute-start(s32[2,16]{1,0:T(2,128)S(1)} %slice.6.refs_0_), channel_id=1, source_target_pairs={{0,8},{8,16},{16,24},{24,0},{1,9},{9,17},{17,25},{25,1},{2,10},{10... | collective-permute-start | bytes 392 | tf_op jit(solution)/shard_map/ppermute | solution.py:339
  40.2 0.0 collective-permute-done.4
  40.2 0.8 %add_convert_fusion = bf16[4,272,128]{2,1,0:T(8,128)(2,1)} fusion(f32[4,272,128]{2,1,0:T(8,128)S(1)} %get-tuple-element.7, bf16[4,272,128]{2,1,0:T(8,128)(2,1)S(1)} %collective-permute-done.4), kind=kLoop, calls=%fused_computation | loop fusion | flops 417792 | bytes 1114112 | tf_op jit(solution)/shard_map/convert_element_type | solution.py:368
  41.0 3.7 %all-to-all-start = ((bf16[4,272,128]{2,1,0:T(8,128)(2,1)}), bf16[4,272,128]{2,1,0:T(8,128)(2,1)S(1)}, u32[]{:S(2)}, u32[]{:S(2)}) async-start(bf16[4,272,128]{2,1,0:T(8,128)(2,1)} %add_convert_fusion), calls=%async_computation | async-start | bytes 557056 | tf_op jit(solution)/shard_map/all_to_all | solution.py:369
  44.7 5.4 %all-to-all-done.sums_ref = bf16[4,272,128]{2,1,0:T(8,128)(2,1)S(1)} async-done(((bf16[4,272,128]{2,1,0:T(8,128)(2,1)}), bf16[4,272,128]{2,1,0:T(8,128)(2,1)S(1)}, u32[]{:S(2)}, u32[]{:S(2)}) %all-to-all-start) | async-done | bytes 278560 | tf_op jit(solution)/shard_map/all_to_all | solution.py:369
  50.1 0.0 copy-done.1
  50.1 0.0 copy-done.2
  50.1 0.0 copy-done.3
  50.1 0.0 copy-done.4
  50.1 1.7 %subgrid_transform.1.refs_4_ = bf16[8,32,128]{2,1,0:T(8,128)(2,1)S(1)} custom-call(s32[16]{0:T(128)S(1)} %slice_bitcast_fusion.planes_ref, bf16[4,272,128]{2,1,0:T(8,128)(2,1)S(1)} %all-to-all-done.sums_ref, f32[32,128]{1,0:T(8,128)S(1)} %copy-done.4, f32[32,128]{1,0:T(8,128)S(1)} %copy-done.3, f32[128,256]{1,0:T(8,128)S(1)} %copy-done.1, f32[32,64]{1,0:T(8,128)S(1)} %copy-done.2), custom_call_target="tpu_custom_call" | custom-call | tf_op jit(solution)/shard_map/subgrid_transform/pallas_call | solution.py:262
  51.9 2.9 %collective-permute-start.7 = (bf16[8,32,128]{2,1,0:T(8,128)(2,1)S(1)}, bf16[8,32,128]{2,1,0:T(8,128)(2,1)S(1)}, u32[]{:S(2)}, u32[]{:S(2)}) collective-permute-start(bf16[8,32,128]{2,1,0:T(8,128)(2,1)S(1)} %subgrid_transform.1.refs_4_), channel_id=1, source_target_pairs={{0,24},{8,0},{16,8},{24,16},{1,25},{9,1},{17,9},{25,17},{2,26},{10... | collective-permute-start | bytes 196616 | tf_op jit(solution)/shard_map/ppermute | solution.py:339
  54.8 1.0 %collective-permute-start.6 = (bf16[8,32,128]{2,1,0:T(8,128)(2,1)S(1)}, bf16[8,32,128]{2,1,0:T(8,128)(2,1)S(1)}, u32[]{:S(2)}, u32[]{:S(2)}) collective-permute-start(bf16[8,32,128]{2,1,0:T(8,128)(2,1)S(1)} %subgrid_transform.1.refs_4_), channel_id=1, source_target_pairs={{0,16},{8,24},{16,0},{24,8},{1,17},{9,25},{17,1},{25,9},{2,18},{10... | collective-permute-start | bytes 196616 | tf_op jit(solution)/shard_map/ppermute | solution.py:339
  55.8 0.0 collective-permute-done.2.refs_3_
  55.8 0.1 collective-permute-start.5
  55.9 0.1 pad_add_fusion.origin_ref
  56.0 0.0 collective-permute-done.1.refs_2_
  56.0 0.0 collective-permute-done.refs_1_
  56.0 0.7 %collective-permute-done.7.refs_7_ = bf16[8,32,128]{2,1,0:T(8,128)(2,1)S(1)} collective-permute-done((bf16[8,32,128]{2,1,0:T(8,128)(2,1)S(1)}, bf16[8,32,128]{2,1,0:T(8,128)(2,1)S(1)}, u32[]{:S(2)}, u32[]{:S(2)}) %collective-permute-start.7) | collective-permute-done | bytes 65568 | tf_op jit(solution)/shard_map/ppermute | solution.py:339
  56.7 3.5 %collective-permute-done.6.refs_6_ = bf16[8,32,128]{2,1,0:T(8,128)(2,1)S(1)} collective-permute-done((bf16[8,32,128]{2,1,0:T(8,128)(2,1)S(1)}, bf16[8,32,128]{2,1,0:T(8,128)(2,1)S(1)}, u32[]{:S(2)}, u32[]{:S(2)}) %collective-permute-start.6) | collective-permute-done | bytes 65568 | tf_op jit(solution)/shard_map/ppermute | solution.py:339
  60.1 1.7 %collective-permute-done.5.refs_5_ = bf16[8,32,128]{2,1,0:T(8,128)(2,1)S(1)} collective-permute-done((bf16[8,32,128]{2,1,0:T(8,128)(2,1)S(1)}, bf16[8,32,128]{2,1,0:T(8,128)(2,1)S(1)}, u32[]{:S(2)}, u32[]{:S(2)}) %collective-permute-start.5) | collective-permute-done | bytes 65568 | tf_op jit(solution)/shard_map/ppermute | solution.py:339
  61.8 3.6 %place.1 = f32[2,512,512]{2,1,0:T(8,128)} custom-call(s32[2]{0:T(128)S(1)} %pad_add_fusion.origin_ref, s32[2,16]{1,0:T(2,128)S(1)} %slice.6.refs_0_, s32[2,16]{1,0:T(2,128)S(1)} %collective-permute-done.refs_1_, s32[2,16]{1,0:T(2,128)S(1)} %collective-permute-done.1.refs_2_, s32[2,16]{1,0:T(2,128)S(1)} %collective-permute-done.2.refs_3_, ...), custom_call_target="tpu_custom_call" | custom-call | tf_op jit(solution)/shard_map/place/pallas_call | solution.py:322
  (2 shorter events, 0.0 us)
Async XLA Ops:
  0.0 3.5 %copy-start = (bf16[1,1280,2,256]{3,2,1,0:T(2,128)(2,1)S(1)}, bf16[1,1280,2,256]{3,2,1,0:T(2,128)(2,1)}, u32[]{:S(2)}) copy-start(bf16[1,1280,2,256]{3,2,1,0:T(2,128)(2,1)} %param.8) | copy-start | bytes 3932164
  0.0 3.5 %copy-start.6 = (s32[5120]{0:T(1024)S(1)}, s32[5120]{0:T(1024)}, u32[]{:S(2)}) copy-start(s32[5120]{0:T(1024)} %ids_ref.1) | copy-start | bytes 61444
  1.2 2.2 %collective-permute-start.3 = (bf16[2560,128]{1,0:T(8,128)(2,1)S(1)}, bf16[2560,128]{1,0:T(8,128)(2,1)S(1)}, u32[]{:S(2)}, u32[]{:S(2)}) collective-permute-start(bf16[2560,128]{1,0:T(8,128)(2,1)S(1)} %constant_dynamic-slice_fusion), channel_id=1, source_target_pairs={{0,1},{1,0},{2,3},{3,2},{4,5},{5,4},{6,7},{7,6},{8,9},{9,8},{10,11... | collective-permute-start | bytes 1966088 | tf_op jit(solution)/shard_map/ppermute | solution.py:360
  3.5 1.3 %copy-start.5 = (bf16[1280,2,256]{2,1,0:T(2,128)(2,1)S(1)}, bf16[1280,2,256]{2,1,0:T(2,128)(2,1)}, u32[]{:S(2)}) copy-start(bf16[1280,2,256]{2,1,0:T(2,128)(2,1)} %param.9) | copy-start | bytes 3932164
  4.8 29.7 %copy-start.7 = (s32[3,16]{1,0:T(4,128)S(1)}, s32[3,16]{1,0:T(4,128)}, u32[]{:S(2)}) copy-start(s32[3,16]{1,0:T(4,128)} %param.11) | copy-start | bytes 580
  34.0 16.2 %copy-start.1 = (f32[128,256]{1,0:T(8,128)S(1)}, f32[128,256]{1,0:T(8,128)}, u32[]{:S(2)}) copy-start(f32[128,256]{1,0:T(8,128)} %constant.39.clone.columns_ref) | copy-start | bytes 393220
  34.0 16.2 %copy-start.2 = (f32[32,64]{1,0:T(8,128)S(1)}, f32[32,64]{1,0:T(8,128)}, u32[]{:S(2)}) copy-start(f32[32,64]{1,0:T(8,128)} %constant.40.clone.rows_ref) | copy-start | bytes 24580
  34.0 16.1 %copy-start.3 = (f32[32,128]{1,0:T(8,128)S(1)}, f32[32,128]{1,0:T(8,128)}, u32[]{:S(2)}) copy-start(f32[32,128]{1,0:T(8,128)} %constant.38.clone.tapers_ref) | copy-start | bytes 49156
  34.0 16.1 %copy-start.4 = (f32[32,128]{1,0:T(8,128)S(1)}, f32[32,128]{1,0:T(8,128)}, u32[]{:S(2)}) copy-start(f32[32,128]{1,0:T(8,128)} %constant.37.clone.turns_ref) | copy-start | bytes 49156
  34.0 6.2 %collective-permute-start.4 = (bf16[4,272,128]{2,1,0:T(8,128)(2,1)S(1)}, bf16[4,272,128]{2,1,0:T(8,128)(2,1)S(1)}, u32[]{:S(2)}, u32[]{:S(2)}) collective-permute-start(bf16[4,272,128]{2,1,0:T(8,128)(2,1)S(1)} %get-tuple-element.8), channel_id=1, source_target_pairs={{0,1},{1,0},{2,3},{3,2},{4,5},{5,4},{6,7},{7,6},{8,9},{9,8},{10,11... | collective-permute-start | bytes 835592 | tf_op jit(solution)/shard_map/ppermute | solution.py:367
  34.5 21.3 %collective-permute-start.2 = (s32[2,16]{1,0:T(2,128)S(1)}, s32[2,16]{1,0:T(2,128)S(1)}, u32[]{:S(2)}, u32[]{:S(2)}) collective-permute-start(s32[2,16]{1,0:T(2,128)S(1)} %slice.6.refs_0_), channel_id=1, source_target_pairs={{0,24},{8,0},{16,8},{24,16},{1,25},{9,1},{17,9},{25,17},{2,26},{10... | collective-permute-start | bytes 392 | tf_op jit(solution)/shard_map/ppermute | solution.py:339
  39.2 16.8 %collective-permute-start.1 = (s32[2,16]{1,0:T(2,128)S(1)}, s32[2,16]{1,0:T(2,128)S(1)}, u32[]{:S(2)}, u32[]{:S(2)}) collective-permute-start(s32[2,16]{1,0:T(2,128)S(1)} %slice.6.refs_0_), channel_id=1, source_target_pairs={{0,16},{8,24},{16,0},{24,8},{1,17},{9,25},{17,1},{25,9},{2,18},{10... | collective-permute-start | bytes 392 | tf_op jit(solution)/shard_map/ppermute | solution.py:339
  39.2 16.8 %collective-permute-start = (s32[2,16]{1,0:T(2,128)S(1)}, s32[2,16]{1,0:T(2,128)S(1)}, u32[]{:S(2)}, u32[]{:S(2)}) collective-permute-start(s32[2,16]{1,0:T(2,128)S(1)} %slice.6.refs_0_), channel_id=1, source_target_pairs={{0,8},{8,16},{16,24},{24,0},{1,9},{9,17},{17,25},{25,1},{2,10},{10... | collective-permute-start | bytes 392 | tf_op jit(solution)/shard_map/ppermute | solution.py:339
  41.0 9.2 %all-to-all-start = ((bf16[4,272,128]{2,1,0:T(8,128)(2,1)}), bf16[4,272,128]{2,1,0:T(8,128)(2,1)S(1)}, u32[]{:S(2)}, u32[]{:S(2)}) async-start(bf16[4,272,128]{2,1,0:T(8,128)(2,1)} %add_convert_fusion), calls=%async_computation | async-start | bytes 557056 | tf_op jit(solution)/shard_map/all_to_all | solution.py:369
  51.9 4.8 %collective-permute-start.7 = (bf16[8,32,128]{2,1,0:T(8,128)(2,1)S(1)}, bf16[8,32,128]{2,1,0:T(8,128)(2,1)S(1)}, u32[]{:S(2)}, u32[]{:S(2)}) collective-permute-start(bf16[8,32,128]{2,1,0:T(8,128)(2,1)S(1)} %subgrid_transform.1.refs_4_), channel_id=1, source_target_pairs={{0,24},{8,0},{16,8},{24,16},{1,25},{9,1},{17,9},{25,17},{2,26},{10... | collective-permute-start | bytes 196616 | tf_op jit(solution)/shard_map/ppermute | solution.py:339
  54.8 5.4 %collective-permute-start.6 = (bf16[8,32,128]{2,1,0:T(8,128)(2,1)S(1)}, bf16[8,32,128]{2,1,0:T(8,128)(2,1)S(1)}, u32[]{:S(2)}, u32[]{:S(2)}) collective-permute-start(bf16[8,32,128]{2,1,0:T(8,128)(2,1)S(1)} %subgrid_transform.1.refs_4_), channel_id=1, source_target_pairs={{0,16},{8,24},{16,0},{24,8},{1,17},{9,25},{17,1},{25,9},{2,18},{10... | collective-permute-start | bytes 196616 | tf_op jit(solution)/shard_map/ppermute | solution.py:339
  55.8 6.1 %collective-permute-start.5 = (bf16[8,32,128]{2,1,0:T(8,128)(2,1)S(1)}, bf16[8,32,128]{2,1,0:T(8,128)(2,1)S(1)}, u32[]{:S(2)}, u32[]{:S(2)}) collective-permute-start(bf16[8,32,128]{2,1,0:T(8,128)(2,1)S(1)} %subgrid_transform.1.refs_4_), channel_id=1, source_target_pairs={{0,8},{8,16},{16,24},{24,0},{1,9},{9,17},{17,25},{25,1},{2,10},{10... | collective-permute-start | bytes 196616 | tf_op jit(solution)/shard_map/ppermute | solution.py:339

commit v2 on v1

--- a/solution.py
+++ b/solution.py
@@ -48,86 +48,96 @@
 
 
 GROUP = 8
-BATCH = 2
+BATCH = 4
+PITCH = 9
 
 
 def phases(start, scale, inputs, angles, values, coords):
-    first, uv_ref, mine_ref, theirs_ref = inputs
+    uv_ref, mine_ref, theirs_ref = inputs
     for group in range(BATCH):
         block = start + group * GROUP
-        there = pl.ds(pl.multiple_of(block * 4, 4 * GROUP), 4 * GROUP)
-        here = pl.ds(pl.multiple_of(first + block * 4, 4 * GROUP), 4 * GROUP)
+        here = pl.ds(pl.multiple_of(block * 4, 4 * GROUP), 4 * GROUP)
         coords[...] = uv_ref[here, :].astype(f32)
         for part in range(2):
             for side in range(2):
-                at = (group * 2 + part) * 8 * SUB
+                at = (group * 2 + part) * PITCH * SUB
                 cosines, sines = multiples(coords[pl.ds(part * 16 + side, 8, 2), :])
                 for k in range(1, HALF + 1):
-                    angles[side, at + (k - 1) * 8 : at + k * 8, :] = cosines[k]
-                    angles[side, at + (HALF + k - 1) * 8 : at + (HALF + k) * 8, :] = sines[k]
+                    row = at + (k - 1) * PITCH
+                    angles[side, row : row + 8, :] = cosines[k]
+                    row += HALF * PITCH
+                    angles[side, row : row + 8, :] = sines[k]
         rows = slice(group * 4 * GROUP, (group + 1) * 4 * GROUP)
         values[0, rows, :] = mine_ref[here, :].astype(f32) * scale
-        values[1, rows, :] = theirs_ref[there, :].astype(f32) * scale
-
-
-def operands(angles, values, left, right):
+        values[1, rows, :] = theirs_ref[here, :].astype(f32) * scale
+
+
+def add_products(id_at, ids_ref, angles, values, sums):
     last = lax.broadcasted_iota(jnp.int32, (HALF, LANES), 0) == HALF - 1
+    ones = jnp.ones((HALF, VB), bf16)
     for block in range(BATCH * GROUP):
-        for half in range(2):
-            chunk = 2 * block + half
-            lanes = slice(half * LANES, (half + 1) * LANES)
-            at = pl.ds(chunk // 8 * 8 * SUB + chunk % 8, SUB, 8)
-            left[block, :SUB, lanes] = angles[0, at, :].astype(bf16)
+        lefts, rights = [], []
+        for chunk in (2 * block, 2 * block + 1):
+            at = pl.ds(chunk // 8 * PITCH * SUB + chunk % 8, SUB, PITCH)
+            lefts.append(angles[0, at, :].astype(bf16))
             phase = angles[1, at, :]
             cosine, sine = phase[:HALF], phase[HALF:]
-            row = 0
+            pieces = []
             for product in range(2):
                 real = values[product, 2 * chunk : 2 * chunk + 1, :]
                 imag = values[product, 2 * chunk + 1 : 2 * chunk + 2, :]
                 rc, is_, rs, ic = real * cosine, imag * sine, real * sine, imag * cosine
                 for up, down, centre in ((rc - is_, rc + is_, real), (ic + rs, ic - rs, imag)):
-                    right[block, row : row + HALF, lanes] = jnp.where(last, centre, up).astype(bf16)
-                    right[block, row + HALF : row + SUB, lanes] = down.astype(bf16)
-                    row += SUB
-
-
-def products(id_at, ids_ref, left, right, sums):
-    for block in range(BATCH * GROUP):
+                    pieces.append(jnp.where(last, centre, up).astype(bf16))
+                    pieces.append(down.astype(bf16))
+            rights.append(jnp.concatenate(pieces, axis=0))
         image = lax.dot_general(
-            left[block], right[block], (((1,), (1,)), ((), ())), preferred_element_type=f32
+            jnp.concatenate([jnp.concatenate(lefts, axis=1), ones], axis=0),
+            jnp.concatenate(rights, axis=1),
+            (((1,), (1,)), ((), ())),
+            preferred_element_type=f32,
         )
         at = pl.ds(pl.multiple_of(ids_ref[id_at + block] * ROWS, 8), ROWS)
         sums[at, :] += image[:ROWS]
 
 
 def slot_sums_kernel(place_ref, sign_ref, ids_ref, uv_ref, mine_ref, theirs_ref, keep_ref, send_ref, sums, *scratch):
-    blocks = theirs_ref.shape[0] // 4
+    local, sem, scratch = scratch[:3], scratch[3], scratch[4:]
+    blocks = local[0].shape[0] // 4
     step = BATCH * GROUP
-    first = place_ref[0]
     id_at = place_ref[1]
     scale = 0.5 / math.sqrt(VB)
-    inputs = (first * 4, uv_ref, mine_ref, theirs_ref)
-    even, odd = scratch[:5], scratch[5:]
+    own_half = pl.ds(pl.multiple_of(place_ref[0] * 4, 16), blocks * 4)
+    sources = (uv_ref.at[own_half, :], mine_ref.at[own_half, :], theirs_ref)
+    copies = [pltpu.make_async_copy(source, local[n], sem.at[n]) for n, source in enumerate(sources)]
+    for copy in copies:
+        copy.start()
+    even, odd = scratch[:3], scratch[3:]
     sums[...] = jnp.zeros_like(sums)
-    for left in (even[2], odd[2]):
-        left[...] = jnp.ones_like(left)
+    for copy in copies:
+        copy.wait()
 
     def fill(start, buffers):
-        angles, values, left, right, coords = buffers
-        phases(start, scale, inputs, angles, values, coords)
-        operands(angles, values, left, right)
+        phases(start, scale, local, *buffers)
+
+    def add(start, buffers):
+        add_products(id_at + start, ids_ref, buffers[0], buffers[1], sums)
 
     fill(0, even)
 
     def two_batches(trip, carry):
         start = trip * 2 * step
-        products(id_at + start, ids_ref, even[2], even[3], sums)
+        add(start, even)
         fill(start + step, odd)
-        products(id_at + start + step, ids_ref, odd[2], odd[3], sums)
-        fill(jnp.minimum(start + 2 * step, blocks - step), even)
+        add(start + step, odd)
+        fill(start + 2 * step, even)
         return carry
 
-    lax.fori_loop(0, blocks // (2 * step), two_batches, 0)
+    trips = blocks // (2 * step) - 1
+    lax.fori_loop(0, trips, two_batches, 0)
+    add(trips * 2 * step, even)
+    fill((trips * 2 + 1) * step, odd)
+    add((trips * 2 + 1) * step, odd)
 
     owners = keep_ref.shape[0]
     pairs = sums.shape[0] // ROWS // owners // 2
@@ -165,11 +175,10 @@
     rows = pairs * SUB + 16
     vmem = pl.BlockSpec(memory_space=pltpu.VMEM)
     smem = pl.BlockSpec(memory_space=pltpu.SMEM)
+    hbm = pl.BlockSpec(memory_space=pltpu.HBM)
     buffers = [
-        pltpu.VMEM((2, BATCH * 2 * GROUP * SUB, LANES), f32),
+        pltpu.VMEM((2, BATCH * 2 * PITCH * SUB, LANES), f32),
         pltpu.VMEM((2, BATCH * 4 * GROUP, LANES), f32),
-        pltpu.VMEM((BATCH * GROUP, SUB + HALF, VB), bf16),
-        pltpu.VMEM((BATCH * GROUP, 4 * SUB, VB), bf16),
         pltpu.VMEM((4 * GROUP, LANES), f32),
     ]
     return pl.pallas_call(
@@ -178,9 +187,13 @@
             jax.ShapeDtypeStruct((shard_count, rows, LANES), f32),
             jax.ShapeDtypeStruct((shard_count, rows, LANES), bf16),
         ],
-        in_specs=[smem, smem, smem, vmem, vmem, vmem],
+        in_specs=[smem, smem, smem, hbm, hbm, pl.BlockSpec(memory_space=pl.ANY)],
         out_specs=[vmem, vmem],
-        scratch_shapes=[pltpu.VMEM((shard_count * slots * ROWS, LANES), f32)] + buffers + buffers,
+        scratch_shapes=[pltpu.VMEM((shard_count * slots * ROWS, LANES), f32)]
+        + [pltpu.VMEM(theirs.shape, bf16)] * 3
+        + [pltpu.SemaphoreType.DMA((3,))]
+        + buffers
+        + buffers,
         compiler_params=pltpu.CompilerParams(vmem_limit_bytes=32 * 1024 * 1024),
         cost_estimate=pl.CostEstimate(flops=60_000_000_000, bytes_accessed=4_000_000, transcendentals=0),
         name="slot_sums",
@@ -221,8 +234,8 @@
     return turns, tapers, columns, rows
 
 
-def transform_kernel(planes_ref, sums_ref, turns_ref, tapers_ref, columns_ref, rows_ref, out_ref):
-    pairs = out_ref.shape[0]
+def transform_kernel(planes_ref, corners_ref, sums_ref, turns_ref, tapers_ref, columns_ref, rows_ref, out_ref):
+    pairs = out_ref.shape[0] // SUB
     plain = sums_ref[0].astype(f32)
     for source in range(1, sums_ref.shape[0]):
         plain = plain + sums_ref[source].astype(f32)
@@ -251,46 +264,59 @@
     for pair in range(pairs):
         at = slice(pair * SUB, (pair + 1) * SUB)
         stacked = jnp.concatenate([both[at, :LANES], both[at, LANES:]], axis=0)
-        out_ref[pair] = jnp.dot(rows_ref[...], stacked, precision=highest, preferred_element_type=f32).astype(
+        out_ref[at, :] = jnp.dot(rows_ref[...], stacked, precision=highest, preferred_element_type=f32).astype(
             out_ref.dtype
         )
-
-
-def subgrid_transform(sums, planes, slots):
+    out_ref[pairs * SUB :, :] = corners_ref[...].astype(out_ref.dtype)
+
+
+def corner_rows(corners):
+    digits = jnp.stack([corners // 16, corners % 16], axis=1).reshape(1, -1).astype(f32)
+    return jnp.pad(digits, ((0, 15), (0, LANES - digits.shape[1])))
+
+
+def subgrid_transform(sums, planes, corners, slots):
     vmem = pl.BlockSpec(memory_space=pltpu.VMEM)
     smem = pl.BlockSpec(memory_space=pltpu.SMEM)
     return pl.pallas_call(
         transform_kernel,
-        out_shape=jax.ShapeDtypeStruct((slots // 2, SUB, LANES), bf16),
-        in_specs=[smem] + [vmem] * 5,
+        out_shape=jax.ShapeDtypeStruct((slots // 2 * SUB + 16, LANES), bf16),
+        in_specs=[smem] + [vmem] * 6,
         out_specs=vmem,
         compiler_params=pltpu.CompilerParams(vmem_limit_bytes=32 * 1024 * 1024),
         name="subgrid_transform",
-    )(planes, sums, *constants())
+    )(planes, corner_rows(corners), sums, *constants())
 
 
 def place_kernel(origin_ref, *refs):
-    count = (len(refs) - 3) // 2
-    corner_refs, sub_refs = refs[:count], refs[count : 2 * count]
-    out_ref, strip, sem = refs[2 * count :]
-    pairs = sub_refs[0].shape[0]
+    sub_refs = refs[:-5]
+    out_ref, strip, decoded, corners, sem = refs[-5:]
+    pairs = sub_refs[0].shape[0] // SUB
+    slots = 2 * pairs
     cols = out_ref.shape[2]
+    for source, sub_ref in enumerate(sub_refs):
+        digits = sub_ref[pairs * SUB :, :].astype(f32)
+        joined = 16.0 * digits + pltpu.roll(digits, LANES - slots, 1)
+        decoded[source * 8 : source * 8 + 8, :] = joined[:8].astype(jnp.int32)
+    fetch = pltpu.make_async_copy(decoded, corners, sem.at[0, 0])
+    fetch.start()
     strip[...] = jnp.zeros_like(strip)
     lane = lax.broadcasted_iota(jnp.int32, (SUB, LANES), 1)
-
-    for corner_ref, sub_ref in zip(corner_refs, sub_refs):
-
-        def add_pair(pair, carry):
+    fetch.wait()
+
+    for source, sub_ref in enumerate(sub_refs):
+
+        def add_pair(pair, carry, source=source, sub_ref=sub_ref):
             for half in range(2):
-                row = corner_ref[0, half * pairs + pair] - origin_ref[0]
-                col = corner_ref[1, half * pairs + pair] - origin_ref[1]
+                row = corners[source * 8, half * pairs + pair] - origin_ref[0]
+                col = corners[source * 8, 2 * slots + half * pairs + pair] - origin_ref[1]
 
                 @pl.when((col > -SUB) & (col < cols))
                 def _():
                     padded = col + LANES
                     tile = padded // LANES
                     at = padded % LANES
-                    piece = sub_ref[pair].astype(f32)
+                    piece = sub_ref[pl.ds(pl.multiple_of(pair * SUB, SUB), SUB), :].astype(f32)
                     left = (lane >= at) & (lane < at + SUB)
                     right = lane < at + SUB - LANES
                     for part in range(2):
@@ -316,21 +342,23 @@
         copy.wait()
 
 
-def place(origin, corners, subs, strip_rows, cols):
+def place(origin, subs, strip_rows, cols):
     smem = pl.BlockSpec(memory_space=pltpu.SMEM)
     vmem = pl.BlockSpec(memory_space=pltpu.VMEM)
     return pl.pallas_call(
         place_kernel,
         out_shape=jax.ShapeDtypeStruct((2, strip_rows, cols), f32),
-        in_specs=[smem] * (1 + len(corners)) + [vmem] * len(subs),
+        in_specs=[smem] + [vmem] * len(subs),
         out_specs=pl.BlockSpec(memory_space=pl.ANY),
         scratch_shapes=[
             pltpu.VMEM((2, cols // LANES + 2, strip_rows, LANES), f32),
+            pltpu.VMEM((8 * len(subs), LANES), jnp.int32),
+            pltpu.SMEM((8 * len(subs), LANES), jnp.int32),
             pltpu.SemaphoreType.DMA((2, cols // LANES)),
         ],
         compiler_params=pltpu.CompilerParams(vmem_limit_bytes=32 * 1024 * 1024),
         name="place",
-    )(origin, *corners, *subs)
+    )(origin, *subs)
 
 
 def around(block, axis):
@@ -360,16 +388,15 @@
     theirs = lax.ppermute(
         lax.dynamic_slice_in_dim(vis, (1 - my_pol) * (half * 4), half * 4, 0), "pol", [(0, 1), (1, 0)]
     )
-    corners = around(slot_table[:2], "chan")
     sign = (1.0 - 2.0 * my_pol.astype(f32))[None]
     at = jnp.stack([my_pol * half, my_shard * blocks + my_pol * half])
     keep, send = slot_sums(at, sign, block_slot, rows_of(uv_coords), vis, theirs, shard_count, slots)
     got = lax.ppermute(send, "pol", [(0, 1), (1, 0)])
     partial = (keep + got.astype(f32)).astype(bf16)
     partial = lax.all_to_all(partial, "bl", split_axis=0, concat_axis=0, tiled=True)
-    subs = around(subgrid_transform(partial, slot_table[2], slots), "chan")
+    subs = around(subgrid_transform(partial, slot_table[2], slot_table[:2], slots), "chan")
     origin = jnp.stack([my_shard * strip_rows, my_chan * cols])
-    return place(origin, corners, subs, strip_rows, cols)[None]
+    return place(origin, subs, strip_rows, cols)[None]
 
 
 def solution(mesh):

time: 65.7 us -> 55.6 us (0.85)
  Pallas kernels: 34.4 us -> 27.5 us
  starting transfers between devices: 14.5 us -> 10.7 us
    pallas_call x1, Pallas kernels: 29.1 us -> 21.3 us  [slot_sums(): pl.pallas_call(slot_sums_kernel, out_shape=[jax.ShapeDtypeStruct((shard_c...]
    ppermute x6 -> x3, starting transfers between devices: 9.75 us -> 4.63 us  [around(): lax.ppermute(block, axis, [(i, (i + step) % count) for i in range(count)])]
    all_to_all x1, starting transfers between devices: 3.74 us -> 5.08 us  [on_device(): lax.all_to_all(partial, 'bl', split_axis=0, concat_axis=0, tiled=True)]
    ppermute x1, waiting for transfers between devices: 0.01 us -> 1.06 us  [on_device(): got = lax.ppermute(send, 'pol', [(0, 1), (1, 0)])]
    pallas_call x1, Pallas kernels: 3.58 us -> 4.51 us  [place(): pl.pallas_call(place_kernel, out_shape=jax.ShapeDtypeStruct((2, strip_row...]
    ppermute x6 -> x3, waiting for transfers between devices: 5.87 us -> 5.03 us  [around(): lax.ppermute(block, axis, [(i, (i + step) % count) for i in range(count)])]
  transfers between devices with their start and end apart: 9 -> 6, of which waited for: 5 -> 6; matrix products, arithmetic and copies ran while one was open for 1% -> 0% of each run, Pallas kernels for 3% -> 0%
where the time goes in v2:
time: 55.6 us; the launch traced here: 55.4 us
  Pallas kernels  27.5 us (49%)
  waiting for transfers between devices  13.5 us (24%)
  starting transfers between devices  10.7 us (19%)
  local copies, waits for them, and re-layouts  2.69 us (5%)
  other arithmetic  0.93 us (2%)
    pallas_call x1, Pallas kernels, slot_sums(): pl.pallas_call(slot_sums_kernel, out_shape=[jax.ShapeDtypeStruct((shard_c...  21.3 us
    all_to_all x1, waiting for transfers between devices, on_device(): lax.all_to_all(partial, 'bl', split_axis=0, concat_axis=0, tiled=True)  5.79 us
    all_to_all x1, starting transfers between devices, on_device(): lax.all_to_all(partial, 'bl', split_axis=0, concat_axis=0, tiled=True)  5.08 us
    ppermute x3, waiting for transfers between devices, around(): lax.ppermute(block, axis, [(i, (i + step) % count) for i in range(count)])  5.03 us
    ppermute x3, starting transfers between devices, around(): lax.ppermute(block, axis, [(i, (i + step) % count) for i in range(count)])  4.63 us
    pallas_call x1, Pallas kernels, place(): pl.pallas_call(place_kernel, out_shape=jax.ShapeDtypeStruct((2, strip_row...  4.51 us
    pallas_call x1, Pallas kernels, subgrid_transform(): pl.pallas_call(transform_kernel, out_shape=jax.ShapeDtypeStruct((slots //...  1.73 us
    ppermute x1, waiting for transfers between devices, on_device(): lax.ppermute(lax.dynamic_slice_in_dim(vis, (1 - my_pol) * (half * 4), hal...  1.65 us
  transfers between devices with their start and end apart: 6, of which 6 were waited for; matrix products, arithmetic and copies ran while one was open for 0% of the time, Pallas kernels for 0%

profile of v2, /device:TPU:0, one launch (start us, length us, event | category | flops | bytes accessed | tf_op | source)
XLA Modules:
  0.0 55.4 jit_solution(3309435018690546527)
XLA Ops:
  0.0 0.0 copy-start
  0.0 0.0 copy-start.6
  0.0 1.2 %constant_dynamic-slice_fusion = bf16[2560,128]{1,0:T(8,128)(2,1)S(1)} fusion(bf16[5120,128]{1,0:T(8,128)(2,1)} %bitcast.22, s32[]{:T(128)S(6)} %select_n.17), kind=kLoop, calls=%fused_computation.14 | loop fusion | bytes 1310724 | tf_op jit(solution)/shard_map/dynamic_slice | solution.py:389
  1.2 0.5 collective-permute-start
  1.8 0.1 pad_add_fusion.1.place_ref
  1.8 1.6 %collective-permute-done.theirs_ref = bf16[2560,128]{1,0:T(8,128)(2,1)S(1)} collective-permute-done((bf16[2560,128]{1,0:T(8,128)(2,1)S(1)}, bf16[2560,128]{1,0:T(8,128)(2,1)S(1)}, u32[]{:S(2)}, u32[]{:S(2)}) %collective-permute-start) | collective-permute-done | bytes 655392 | tf_op jit(solution)/shard_map/ppermute | solution.py:388
  3.5 0.0 copy-done
  3.5 0.0 copy-done.6
  3.5 0.0 copy-start.5
  3.5 1.3 %copy-done.5 = bf16[1280,2,256]{2,1,0:T(2,128)(2,1)S(1)} copy-done((bf16[1280,2,256]{2,1,0:T(2,128)(2,1)S(1)}, bf16[1280,2,256]{2,1,0:T(2,128)(2,1)}, u32[]{:S(2)}) %copy-start.5) | copy-done | bytes 1310744
  4.8 0.0 copy-start.7
  4.8 21.3 %slot_sums.1 = (f32[4,272,128]{2,1,0:T(8,128)S(1)}, bf16[4,272,128]{2,1,0:T(8,128)(2,1)S(1)}) custom-call(s32[2]{0:T(128)S(1)} %pad_add_fusion.1.place_ref, f32[1]{0:T(128)} %bitcast.7.sign_ref, s32[5120]{0:T(1024)S(1)} %copy-done.6, bf16[5120,128]{1,0:T(8,128)(2,1)S(1)} %bitcast.24, bf16[5120,128]{1,0:T(8,128)(2,1)S(1)} %bitcast.23, ...), custom_call_target="tpu_custom_call" | custom-call | flops 60000002048 | bytes 4000000 | tf_op jit(solution)/shard_map/slot_sums/pallas_call | solution.py:184
  26.1 0.0 copy-start.1
  26.1 0.0 copy-start.2
  26.1 0.0 copy-start.3
  26.2 0.0 copy-start.4
  26.2 0.4 collective-permute-start.1
  26.6 0.0 copy-done.7
  26.7 0.1 convert_element_type.26
  26.8 1.1 %collective-permute-done.1 = bf16[4,272,128]{2,1,0:T(8,128)(2,1)S(1)} collective-permute-done((bf16[4,272,128]{2,1,0:T(8,128)(2,1)S(1)}, bf16[4,272,128]{2,1,0:T(8,128)(2,1)S(1)}, u32[]{:S(2)}, u32[]{:S(2)}) %collective-permute-start.1) | collective-permute-done | bytes 278560 | tf_op jit(solution)/shard_map/ppermute | solution.py:394
  27.8 0.8 %add_convert_fusion = bf16[4,272,128]{2,1,0:T(8,128)(2,1)} fusion(f32[4,272,128]{2,1,0:T(8,128)S(1)} %get-tuple-element.7, bf16[4,272,128]{2,1,0:T(8,128)(2,1)S(1)} %collective-permute-done.1), kind=kLoop, calls=%fused_computation | loop fusion | flops 417792 | bytes 1114112 | tf_op jit(solution)/shard_map/convert_element_type | solution.py:395
  28.6 5.1 %all-to-all-start = ((bf16[4,272,128]{2,1,0:T(8,128)(2,1)}), bf16[4,272,128]{2,1,0:T(8,128)(2,1)S(1)}, u32[]{:S(2)}, u32[]{:S(2)}) async-start(bf16[4,272,128]{2,1,0:T(8,128)(2,1)} %add_convert_fusion), calls=%async_computation | async-start | bytes 557056 | tf_op jit(solution)/shard_map/all_to_all | solution.py:396
  33.7 5.8 %all-to-all-done.sums_ref = bf16[4,272,128]{2,1,0:T(8,128)(2,1)S(1)} async-done(((bf16[4,272,128]{2,1,0:T(8,128)(2,1)}), bf16[4,272,128]{2,1,0:T(8,128)(2,1)S(1)}, u32[]{:S(2)}, u32[]{:S(2)}) %all-to-all-start) | async-done | bytes 278560 | tf_op jit(solution)/shard_map/all_to_all | solution.py:396
  39.5 0.0 copy-done.1
  39.5 0.0 copy-done.2
  39.5 0.0 copy-done.3
  39.5 0.0 copy-done.4
  39.5 1.7 %subgrid_transform.1.refs_0_ = bf16[272,128]{1,0:T(8,128)(2,1)S(1)} custom-call(s32[16]{0:T(128)S(1)} %slice_bitcast_fusion.planes_ref, f32[16,128]{1,0:T(8,128)S(1)} %pad.4.corners_ref, bf16[4,272,128]{2,1,0:T(8,128)(2,1)S(1)} %all-to-all-done.sums_ref, f32[32,128]{1,0:T(8,128)S(1)} %copy-done.4, f32[32,128]{1,0:T(8,128)S(1)} %copy-done.3, ...), custom_call_target="tpu_custom_call" | custom-call | tf_op jit(solution)/shard_map/subgrid_transform/pallas_call | solution.py:281
  41.2 3.6 %collective-permute-start.4 = (bf16[272,128]{1,0:T(8,128)(2,1)S(1)}, bf16[272,128]{1,0:T(8,128)(2,1)S(1)}, u32[]{:S(2)}, u32[]{:S(2)}) collective-permute-start(bf16[272,128]{1,0:T(8,128)(2,1)S(1)} %subgrid_transform.1.refs_0_), channel_id=1, source_target_pairs={{0,24},{8,0},{16,8},{24,16},{1,25},{9,1},{17,9},{25,17},{2,26},{10... | collective-permute-start | bytes 208904 | tf_op jit(solution)/shard_map/ppermute | solution.py:367
  44.8 0.0 collective-permute-start.3
  44.8 1.0 %collective-permute-start.2 = (bf16[272,128]{1,0:T(8,128)(2,1)S(1)}, bf16[272,128]{1,0:T(8,128)(2,1)S(1)}, u32[]{:S(2)}, u32[]{:S(2)}) collective-permute-start(bf16[272,128]{1,0:T(8,128)(2,1)S(1)} %subgrid_transform.1.refs_0_), channel_id=1, source_target_pairs={{0,8},{8,16},{16,24},{24,0},{1,9},{9,17},{17,25},{25,1},{2,10},{10... | collective-permute-start | bytes 208904 | tf_op jit(solution)/shard_map/ppermute | solution.py:367
  45.8 0.1 pad_add_fusion.origin_ref
  45.9 0.9 %collective-permute-done.4.refs_3_ = bf16[272,128]{1,0:T(8,128)(2,1)S(1)} collective-permute-done((bf16[272,128]{1,0:T(8,128)(2,1)S(1)}, bf16[272,128]{1,0:T(8,128)(2,1)S(1)}, u32[]{:S(2)}, u32[]{:S(2)}) %collective-permute-start.4) | collective-permute-done | bytes 69664 | tf_op jit(solution)/shard_map/ppermute | solution.py:367
  46.8 3.3 %collective-permute-done.3.refs_2_ = bf16[272,128]{1,0:T(8,128)(2,1)S(1)} collective-permute-done((bf16[272,128]{1,0:T(8,128)(2,1)S(1)}, bf16[272,128]{1,0:T(8,128)(2,1)S(1)}, u32[]{:S(2)}, u32[]{:S(2)}) %collective-permute-start.3) | collective-permute-done | bytes 69664 | tf_op jit(solution)/shard_map/ppermute | solution.py:367
  50.0 0.9 %collective-permute-done.2.refs_1_ = bf16[272,128]{1,0:T(8,128)(2,1)S(1)} collective-permute-done((bf16[272,128]{1,0:T(8,128)(2,1)S(1)}, bf16[272,128]{1,0:T(8,128)(2,1)S(1)}, u32[]{:S(2)}, u32[]{:S(2)}) %collective-permute-start.2) | collective-permute-done | bytes 69664 | tf_op jit(solution)/shard_map/ppermute | solution.py:367
  50.9 4.5 %place.1 = f32[2,512,512]{2,1,0:T(8,128)} custom-call(s32[2]{0:T(128)S(1)} %pad_add_fusion.origin_ref, bf16[272,128]{1,0:T(8,128)(2,1)S(1)} %subgrid_transform.1.refs_0_, bf16[272,128]{1,0:T(8,128)(2,1)S(1)} %collective-permute-done.2.refs_1_, bf16[272,128]{1,0:T(8,128)(2,1)S(1)} %collective-permute-done.3.refs_2_, ...), custom_call_target="tpu_custom_call" | custom-call | tf_op jit(solution)/shard_map/place/pallas_call | solution.py:348
  (5 shorter events, 0.0 us)
Async XLA Ops:
  0.0 3.5 %copy-start = (bf16[1,1280,2,256]{3,2,1,0:T(2,128)(2,1)S(1)}, bf16[1,1280,2,256]{3,2,1,0:T(2,128)(2,1)}, u32[]{:S(2)}) copy-start(bf16[1,1280,2,256]{3,2,1,0:T(2,128)(2,1)} %param.8) | copy-start | bytes 3932164
  0.0 3.5 %copy-start.6 = (s32[5120]{0:T(1024)S(1)}, s32[5120]{0:T(1024)}, u32[]{:S(2)}) copy-start(s32[5120]{0:T(1024)} %ids_ref.1) | copy-start | bytes 61444
  1.2 2.2 %collective-permute-start = (bf16[2560,128]{1,0:T(8,128)(2,1)S(1)}, bf16[2560,128]{1,0:T(8,128)(2,1)S(1)}, u32[]{:S(2)}, u32[]{:S(2)}) collective-permute-start(bf16[2560,128]{1,0:T(8,128)(2,1)S(1)} %constant_dynamic-slice_fusion), channel_id=1, source_target_pairs={{0,1},{1,0},{2,3},{3,2},{4,5},{5,4},{6,7},{7,6},{8,9},{9,8},{10,11... | collective-permute-start | bytes 1966088 | tf_op jit(solution)/shard_map/ppermute | solution.py:388
  3.5 1.3 %copy-start.5 = (bf16[1280,2,256]{2,1,0:T(2,128)(2,1)S(1)}, bf16[1280,2,256]{2,1,0:T(2,128)(2,1)}, u32[]{:S(2)}) copy-start(bf16[1280,2,256]{2,1,0:T(2,128)(2,1)} %param.9) | copy-start | bytes 3932164
  4.8 21.8 %copy-start.7 = (s32[3,16]{1,0:T(4,128)S(1)}, s32[3,16]{1,0:T(4,128)}, u32[]{:S(2)}) copy-start(s32[3,16]{1,0:T(4,128)} %param.11) | copy-start | bytes 580
  26.1 13.3 %copy-start.1 = (f32[128,256]{1,0:T(8,128)S(1)}, f32[128,256]{1,0:T(8,128)}, u32[]{:S(2)}) copy-start(f32[128,256]{1,0:T(8,128)} %constant.67.clone.columns_ref) | copy-start | bytes 393220
  26.1 13.3 %copy-start.2 = (f32[32,64]{1,0:T(8,128)S(1)}, f32[32,64]{1,0:T(8,128)}, u32[]{:S(2)}) copy-start(f32[32,64]{1,0:T(8,128)} %constant.68.clone.rows_ref) | copy-start | bytes 24580
  26.1 13.3 %copy-start.3 = (f32[32,128]{1,0:T(8,128)S(1)}, f32[32,128]{1,0:T(8,128)}, u32[]{:S(2)}) copy-start(f32[32,128]{1,0:T(8,128)} %constant.66.clone.tapers_ref) | copy-start | bytes 49156
  26.2 13.3 %copy-start.4 = (f32[32,128]{1,0:T(8,128)S(1)}, f32[32,128]{1,0:T(8,128)}, u32[]{:S(2)}) copy-start(f32[32,128]{1,0:T(8,128)} %constant.65.clone.turns_ref) | copy-start | bytes 49156
  26.2 1.6 %collective-permute-start.1 = (bf16[4,272,128]{2,1,0:T(8,128)(2,1)S(1)}, bf16[4,272,128]{2,1,0:T(8,128)(2,1)S(1)}, u32[]{:S(2)}, u32[]{:S(2)}) collective-permute-start(bf16[4,272,128]{2,1,0:T(8,128)(2,1)S(1)} %get-tuple-element.8), channel_id=1, source_target_pairs={{0,1},{1,0},{2,3},{3,2},{4,5},{5,4},{6,7},{7,6},{8,9},{9,8},{10,11... | collective-permute-start | bytes 835592 | tf_op jit(solution)/shard_map/ppermute | solution.py:394
  28.6 10.9 %all-to-all-start = ((bf16[4,272,128]{2,1,0:T(8,128)(2,1)}), bf16[4,272,128]{2,1,0:T(8,128)(2,1)S(1)}, u32[]{:S(2)}, u32[]{:S(2)}) async-start(bf16[4,272,128]{2,1,0:T(8,128)(2,1)} %add_convert_fusion), calls=%async_computation | async-start | bytes 557056 | tf_op jit(solution)/shard_map/all_to_all | solution.py:396
  41.2 5.6 %collective-permute-start.4 = (bf16[272,128]{1,0:T(8,128)(2,1)S(1)}, bf16[272,128]{1,0:T(8,128)(2,1)S(1)}, u32[]{:S(2)}, u32[]{:S(2)}) collective-permute-start(bf16[272,128]{1,0:T(8,128)(2,1)S(1)} %subgrid_transform.1.refs_0_), channel_id=1, source_target_pairs={{0,24},{8,0},{16,8},{24,16},{1,25},{9,1},{17,9},{25,17},{2,26},{10... | collective-permute-start | bytes 208904 | tf_op jit(solution)/shard_map/ppermute | solution.py:367
  44.8 5.2 %collective-permute-start.3 = (bf16[272,128]{1,0:T(8,128)(2,1)S(1)}, bf16[272,128]{1,0:T(8,128)(2,1)S(1)}, u32[]{:S(2)}, u32[]{:S(2)}) collective-permute-start(bf16[272,128]{1,0:T(8,128)(2,1)S(1)} %subgrid_transform.1.refs_0_), channel_id=1, source_target_pairs={{0,16},{8,24},{16,0},{24,8},{1,17},{9,25},{17,1},{25,9},{2,18},{10... | collective-permute-start | bytes 208904 | tf_op jit(solution)/shard_map/ppermute | solution.py:367
  44.8 6.1 %collective-permute-start.2 = (bf16[272,128]{1,0:T(8,128)(2,1)S(1)}, bf16[272,128]{1,0:T(8,128)(2,1)S(1)}, u32[]{:S(2)}, u32[]{:S(2)}) collective-permute-start(bf16[272,128]{1,0:T(8,128)(2,1)S(1)} %subgrid_transform.1.refs_0_), channel_id=1, source_target_pairs={{0,8},{8,16},{16,24},{24,0},{1,9},{9,17},{17,25},{25,1},{2,10},{10... | collective-permute-start | bytes 208904 | tf_op jit(solution)/shard_map/ppermute | solution.py:367

commit v3 on v2

--- a/solution.py
+++ b/solution.py
@@ -16,7 +16,6 @@
 LANES = 128
 ROWS = 40
 W_STEP = 0.25
-highest = lax.Precision.HIGHEST
 f32 = jnp.float32
 bf16 = jnp.bfloat16
 
@@ -47,33 +46,55 @@
     return cosines, sines
 
 
+def odd_halves(coords):
+    c_half, s_half = cos_sin(coords * (math.pi / SUB), 6)
+    twice = {1: 2.0 - 4.0 * s_half * s_half}
+    for base in (2, 4, 8):
+        twice[base] = twice[base // 2] * twice[base // 2] - 2.0
+    cosines, sines = [c_half], [s_half]
+    for j in range(1, HALF):
+        base = 1 << (j.bit_length() - 1)
+        cosines.append(twice[base] * cosines[j - base] - cosines[2 * base - 1 - j])
+        sines.append(twice[base] * sines[j - base] + sines[2 * base - 1 - j])
+    return cosines, sines
+
+
 GROUP = 8
 BATCH = 4
 PITCH = 9
 
 
-def phases(start, scale, inputs, angles, values, coords):
-    uv_ref, mine_ref, theirs_ref = inputs
+def phases(start, scale, inputs, angles, values, wide):
     for group in range(BATCH):
-        block = start + group * GROUP
-        here = pl.ds(pl.multiple_of(block * 4, 4 * GROUP), 4 * GROUP)
-        coords[...] = uv_ref[here, :].astype(f32)
+        rows = pl.ds(pl.multiple_of((start + group * GROUP) * 4, 4 * GROUP), 4 * GROUP)
+        for which, ref in enumerate(inputs):
+            wide[which, : 4 * GROUP, :] = ref[rows, :].astype(f32)
         for part in range(2):
-            for side in range(2):
-                at = (group * 2 + part) * PITCH * SUB
-                cosines, sines = multiples(coords[pl.ds(part * 16 + side, 8, 2), :])
-                for k in range(1, HALF + 1):
-                    row = at + (k - 1) * PITCH
-                    angles[side, row : row + 8, :] = cosines[k]
-                    row += HALF * PITCH
-                    angles[side, row : row + 8, :] = sines[k]
-        rows = slice(group * 4 * GROUP, (group + 1) * 4 * GROUP)
-        values[0, rows, :] = mine_ref[here, :].astype(f32) * scale
-        values[1, rows, :] = theirs_ref[here, :].astype(f32) * scale
+            at = (group * 2 + part) * PITCH * SUB
+
+            def pick(which, component):
+                return wide[which, pl.ds(part * 16 + component, 8, 2), :]
+
+            def put(side, number, value):
+                angles[side, at + number * PITCH : at + number * PITCH + 8, :] = value
+
+            cosines, sines = multiples(pick(0, 0))
+            for k in range(1, HALF + 1):
+                put(0, k - 1, cosines[k])
+                put(0, HALF + k - 1, sines[k])
+            cosines, sines = odd_halves(pick(0, 1))
+            for k in range(HALF):
+                put(1, k, cosines[k])
+                put(1, HALF + k, sines[k])
+            c_half, s_half = cosines[0] * scale, sines[0] * scale
+            chunks = slice((group * 2 + part) * 8, (group * 2 + part + 1) * 8)
+            for product in range(2):
+                real, imag = pick(1 + product, 0), pick(1 + product, 1)
+                values[2 * product, chunks, :] = real * c_half + imag * s_half
+                values[2 * product + 1, chunks, :] = imag * c_half - real * s_half
 
 
 def add_products(id_at, ids_ref, angles, values, sums):
-    last = lax.broadcasted_iota(jnp.int32, (HALF, LANES), 0) == HALF - 1
     ones = jnp.ones((HALF, VB), bf16)
     for block in range(BATCH * GROUP):
         lefts, rights = [], []
@@ -84,12 +105,11 @@
             cosine, sine = phase[:HALF], phase[HALF:]
             pieces = []
             for product in range(2):
-                real = values[product, 2 * chunk : 2 * chunk + 1, :]
-                imag = values[product, 2 * chunk + 1 : 2 * chunk + 2, :]
+                real = values[2 * product, chunk : chunk + 1, :]
+                imag = values[2 * product + 1, chunk : chunk + 1, :]
                 rc, is_, rs, ic = real * cosine, imag * sine, real * sine, imag * cosine
-                for up, down, centre in ((rc - is_, rc + is_, real), (ic + rs, ic - rs, imag)):
-                    pieces.append(jnp.where(last, centre, up).astype(bf16))
-                    pieces.append(down.astype(bf16))
+                for piece in (rc - is_, rc + is_, ic + rs, ic - rs):
+                    pieces.append(piece.astype(bf16))
             rights.append(jnp.concatenate(pieces, axis=0))
         image = lax.dot_general(
             jnp.concatenate([jnp.concatenate(lefts, axis=1), ones], axis=0),
@@ -101,21 +121,14 @@
         sums[at, :] += image[:ROWS]
 
 
-def slot_sums_kernel(place_ref, sign_ref, ids_ref, uv_ref, mine_ref, theirs_ref, keep_ref, send_ref, sums, *scratch):
-    local, sem, scratch = scratch[:3], scratch[3], scratch[4:]
-    blocks = local[0].shape[0] // 4
+def slot_sums_kernel(first_ref, sign_ref, ids_ref, uv_ref, mine_ref, theirs_ref, keep_ref, send_ref, sums, *scratch):
+    local = (uv_ref, mine_ref, theirs_ref)
+    blocks = uv_ref.shape[0] // 4
     step = BATCH * GROUP
-    id_at = place_ref[1]
+    id_at = first_ref[0]
     scale = 0.5 / math.sqrt(VB)
-    own_half = pl.ds(pl.multiple_of(place_ref[0] * 4, 16), blocks * 4)
-    sources = (uv_ref.at[own_half, :], mine_ref.at[own_half, :], theirs_ref)
-    copies = [pltpu.make_async_copy(source, local[n], sem.at[n]) for n, source in enumerate(sources)]
-    for copy in copies:
-        copy.start()
     even, odd = scratch[:3], scratch[3:]
     sums[...] = jnp.zeros_like(sums)
-    for copy in copies:
-        copy.wait()
 
     def fill(start, buffers):
         phases(start, scale, local, *buffers)
@@ -170,16 +183,15 @@
     lax.fori_loop(0, owners, store_owner, 0)
 
 
-def slot_sums(place, sign, block_slot, uv, mine, theirs, shard_count, slots):
+def slot_sums(first, sign, block_slot, uv, mine, theirs, shard_count, slots):
     pairs = slots // 2
     rows = pairs * SUB + 16
     vmem = pl.BlockSpec(memory_space=pltpu.VMEM)
     smem = pl.BlockSpec(memory_space=pltpu.SMEM)
-    hbm = pl.BlockSpec(memory_space=pltpu.HBM)
     buffers = [
-        pltpu.VMEM((2, BATCH * 2 * PITCH * SUB, LANES), f32),
-        pltpu.VMEM((2, BATCH * 4 * GROUP, LANES), f32),
-        pltpu.VMEM((4 * GROUP, LANES), f32),
+        pltpu.VMEM((2, BATCH * 2 * PITCH * SUB + 16, LANES), f32),
+        pltpu.VMEM((4, BATCH * 2 * GROUP, LANES), f32),
+        pltpu.VMEM((3, 4 * GROUP + 8, LANES), f32),
     ]
     return pl.pallas_call(
         slot_sums_kernel,
@@ -187,21 +199,23 @@
             jax.ShapeDtypeStruct((shard_count, rows, LANES), f32),
             jax.ShapeDtypeStruct((shard_count, rows, LANES), bf16),
         ],
-        in_specs=[smem, smem, smem, hbm, hbm, pl.BlockSpec(memory_space=pl.ANY)],
+        in_specs=[smem, smem, smem, vmem, vmem, vmem],
         out_specs=[vmem, vmem],
         scratch_shapes=[pltpu.VMEM((shard_count * slots * ROWS, LANES), f32)]
-        + [pltpu.VMEM(theirs.shape, bf16)] * 3
-        + [pltpu.SemaphoreType.DMA((3,))]
         + buffers
         + buffers,
         compiler_params=pltpu.CompilerParams(vmem_limit_bytes=32 * 1024 * 1024),
         cost_estimate=pl.CostEstimate(flops=60_000_000_000, bytes_accessed=4_000_000, transcendentals=0),
         name="slot_sums",
-    )(place, sign, block_slot, uv, mine, theirs)
+    )(first, sign, block_slot, uv, mine, theirs)
 
 
 def row_order():
     return np.array(list(range(HALF + 1, SUB)) + [HALF] + list(range(HALF - 1, -1, -1)))
+
+
+def column_order():
+    return np.array(list(range(HALF, SUB)) + list(range(HALF - 1, -1, -1)))
 
 
 def dft_matrix():
@@ -220,25 +234,46 @@
 
 
 def constants():
-    order = row_order()
+    rows_at, cols_at = row_order(), column_order()
     dft = dft_matrix()
-    cols = dft.T[order]
+    cols = dft.T[cols_at]
     columns = spread(np.concatenate([cols, 1j * cols], axis=0))
-    rows = dft[:, order]
+    rows = dft[:, rows_at]
     rows = np.concatenate([rows.real, rows.imag], axis=1).astype(np.float32)
-    offsets = (order - HALF) / SUB
-    taper = np.sin(np.pi * (order + 0.5) / SUB)
-    n_term = np.sqrt(1.0 - offsets[:, None] ** 2 - offsets[None, :] ** 2) - 1.0
+
+    def outer(values):
+        return values[rows_at][:, None], values[cols_at][None, :]
+
+    place_x, place_y = outer((np.arange(SUB) - HALF) / SUB)
+    taper_x, taper_y = outer(np.sin(np.pi * (np.arange(SUB) + 0.5) / SUB))
+    n_term = np.sqrt(1.0 - place_x**2 - place_y**2) - 1.0
     turns = np.tile(-W_STEP * n_term, (1, 4)).astype(np.float32)
-    tapers = np.tile(taper[:, None] * taper[None, :], (1, 4)).astype(np.float32)
-    return turns, tapers, columns, rows
-
-
-def transform_kernel(planes_ref, corners_ref, sums_ref, turns_ref, tapers_ref, columns_ref, rows_ref, out_ref):
+    tapers = np.tile(taper_x * taper_y, (1, 4)).astype(np.float32)
+
+    def split(matrix):
+        high = matrix.astype(jnp.bfloat16)
+        return np.stack([high, (matrix - high.astype(np.float32)).astype(jnp.bfloat16)])
+
+    return turns, tapers, split(columns), split(rows)
+
+
+def halves(values):
+    high = values.astype(bf16)
+    return high, (values - high.astype(f32)).astype(bf16)
+
+
+def dot_in_halves(left, right):
+    (a, b), (c, d) = left, right
+    small = jnp.dot(b, c, preferred_element_type=f32) + jnp.dot(a, d, preferred_element_type=f32)
+    return small + jnp.dot(a, c, preferred_element_type=f32)
+
+
+def transform_kernel(planes_ref, corners_ref, turns_ref, tapers_ref, columns_ref, rows_ref, *refs):
+    sum_refs, out_ref = refs[:-1], refs[-1]
     pairs = out_ref.shape[0] // SUB
-    plain = sums_ref[0].astype(f32)
-    for source in range(1, sums_ref.shape[0]):
-        plain = plain + sums_ref[source].astype(f32)
+    plain = sum_refs[0][...].astype(f32)
+    for sum_ref in sum_refs[1:]:
+        plain = plain + sum_ref[...].astype(f32)
     lane = lax.broadcasted_iota(jnp.int32, (1, LANES), 1)
     turned = jnp.where(
         (lane // SUB) % 2 == 0, -pltpu.roll(plain, LANES - SUB, 1), pltpu.roll(plain, SUB, 1)
@@ -260,13 +295,17 @@
         screen_cos = (1.0 - 2.0 * s_half * s_half) * tapers_ref[...]
         screen_sin = (2.0 * s_half * c_half) * tapers_ref[...]
         pieces.append(image * screen_cos + image_i * screen_sin)
-    both = jnp.dot(jnp.concatenate(pieces, axis=0), columns_ref[...], precision=highest, preferred_element_type=f32)
+    both = dot_in_halves(halves(jnp.concatenate(pieces, axis=0)), (columns_ref[0], columns_ref[1]))
+    stacked = jnp.concatenate(
+        [
+            jnp.concatenate([both[pair * SUB : (pair + 1) * SUB, part : part + LANES] for pair in range(pairs)], axis=1)
+            for part in (0, LANES)
+        ],
+        axis=0,
+    )
+    result = dot_in_halves((rows_ref[0], rows_ref[1]), halves(stacked)).astype(out_ref.dtype)
     for pair in range(pairs):
-        at = slice(pair * SUB, (pair + 1) * SUB)
-        stacked = jnp.concatenate([both[at, :LANES], both[at, LANES:]], axis=0)
-        out_ref[at, :] = jnp.dot(rows_ref[...], stacked, precision=highest, preferred_element_type=f32).astype(
-            out_ref.dtype
-        )
+        out_ref[pair * SUB : (pair + 1) * SUB, :] = result[:, pair * LANES : (pair + 1) * LANES]
     out_ref[pairs * SUB :, :] = corners_ref[...].astype(out_ref.dtype)
 
 
@@ -281,27 +320,31 @@
     return pl.pallas_call(
         transform_kernel,
         out_shape=jax.ShapeDtypeStruct((slots // 2 * SUB + 16, LANES), bf16),
-        in_specs=[smem] + [vmem] * 6,
+        in_specs=[smem] + [vmem] * (5 + len(sums)),
         out_specs=vmem,
         compiler_params=pltpu.CompilerParams(vmem_limit_bytes=32 * 1024 * 1024),
         name="subgrid_transform",
-    )(planes, corner_rows(corners), sums, *constants())
-
-
-def place_kernel(origin_ref, *refs):
-    sub_refs = refs[:-5]
-    out_ref, strip, decoded, corners, sem = refs[-5:]
+    )(planes, corner_rows(corners), *constants(), *sums)
+
+
+def place_kernel(first, final, count, origin_ref, *refs):
+    sub_refs = refs[:count]
+    if final:
+        out_ref, strip, decoded, corners, sem = refs[-5:]
+    else:
+        strip, decoded, corners, sem = refs[-4:]
     pairs = sub_refs[0].shape[0] // SUB
     slots = 2 * pairs
-    cols = out_ref.shape[2]
     for source, sub_ref in enumerate(sub_refs):
         digits = sub_ref[pairs * SUB :, :].astype(f32)
         joined = 16.0 * digits + pltpu.roll(digits, LANES - slots, 1)
         decoded[source * 8 : source * 8 + 8, :] = joined[:8].astype(jnp.int32)
     fetch = pltpu.make_async_copy(decoded, corners, sem.at[0, 0])
     fetch.start()
-    strip[...] = jnp.zeros_like(strip)
+    if first:
+        strip[...] = jnp.zeros_like(strip)
     lane = lax.broadcasted_iota(jnp.int32, (SUB, LANES), 1)
+    cols = (strip.shape[1] - 2) * LANES
     fetch.wait()
 
     for source, sub_ref in enumerate(sub_refs):
@@ -319,52 +362,84 @@
                     piece = sub_ref[pl.ds(pl.multiple_of(pair * SUB, SUB), SUB), :].astype(f32)
                     left = (lane >= at) & (lane < at + SUB)
                     right = lane < at + SUB - LANES
+                    rows = pl.ds(row, SUB)
+                    turned = [
+                        pltpu.roll(piece, (at + (LANES - half * 2 * SUB - part * SUB)) % LANES, 1) for part in range(2)
+                    ]
+                    sums = [
+                        strip[part, tile + over, rows, :] + jnp.where(mask, turned[part], 0.0)
+                        for part in range(2)
+                        for over, mask in enumerate((left, right))
+                    ]
                     for part in range(2):
-                        start = half * 2 * SUB + part * SUB
-                        turned = pltpu.roll(piece, (at + (LANES - start)) % LANES, 1)
-                        rows = pl.ds(row, SUB)
-                        strip[part, tile, rows, :] += jnp.where(left, turned, 0.0)
-                        strip[part, tile + 1, rows, :] += jnp.where(right, turned, 0.0)
+                        for over in range(2):
+                            strip[part, tile + over, rows, :] = sums[2 * part + over]
 
             return carry
 
         lax.fori_loop(0, pairs, add_pair, 0)
-    copies = [
-        pltpu.make_async_copy(
-            strip.at[part, tile + 1], out_ref.at[part, :, pl.ds(tile * LANES, LANES)], sem.at[part, tile]
-        )
-        for part in range(2)
-        for tile in range(cols // LANES)
-    ]
-    for copy in copies:
-        copy.start()
-    for copy in copies:
-        copy.wait()
+
+    if final:
+        copies = [
+            pltpu.make_async_copy(
+                strip.at[part, tile + 1, pl.ds(0, out_ref.shape[1]), :],
+                out_ref.at[part, :, pl.ds(tile * LANES, LANES)],
+                sem.at[part, tile],
+            )
+            for part in range(2)
+            for tile in range(cols // LANES)
+        ]
+        for copy in copies:
+            copy.start()
+        for copy in copies:
+            copy.wait()
 
 
 def place(origin, subs, strip_rows, cols):
     smem = pl.BlockSpec(memory_space=pltpu.SMEM)
     vmem = pl.BlockSpec(memory_space=pltpu.VMEM)
-    return pl.pallas_call(
-        place_kernel,
-        out_shape=jax.ShapeDtypeStruct((2, strip_rows, cols), f32),
-        in_specs=[smem] + [vmem] * len(subs),
-        out_specs=pl.BlockSpec(memory_space=pl.ANY),
-        scratch_shapes=[
-            pltpu.VMEM((2, cols // LANES + 2, strip_rows, LANES), f32),
-            pltpu.VMEM((8 * len(subs), LANES), jnp.int32),
-            pltpu.SMEM((8 * len(subs), LANES), jnp.int32),
-            pltpu.SemaphoreType.DMA((2, cols // LANES)),
-        ],
-        compiler_params=pltpu.CompilerParams(vmem_limit_bytes=32 * 1024 * 1024),
-        name="place",
-    )(origin, *subs)
+    tiles = cols // LANES
+    strip_shape = jax.ShapeDtypeStruct((2, tiles + 2, strip_rows + 8, LANES), f32)
+    result = []
+    for first, group in ((True, subs[:1]), (False, subs[1:])):
+        outs, specs = [strip_shape], [vmem]
+        if not first:
+            outs = [jax.ShapeDtypeStruct((2, strip_rows, cols), f32)] + outs
+            specs = [pl.BlockSpec(memory_space=pl.ANY)] + specs
+        result = pl.pallas_call(
+            functools.partial(place_kernel, first, not first, len(group)),
+            out_shape=outs,
+            in_specs=[smem] + [vmem] * (len(group) + len(result)),
+            out_specs=specs,
+            scratch_shapes=[
+                pltpu.VMEM((8 * len(group), LANES), jnp.int32),
+                pltpu.SMEM((8 * len(group), LANES), jnp.int32),
+                pltpu.SemaphoreType.DMA((2, tiles)),
+            ],
+            input_output_aliases={} if first else {1 + len(group): 1},
+            compiler_params=pltpu.CompilerParams(vmem_limit_bytes=32 * 1024 * 1024),
+            name="place_own" if first else "place_others",
+        )(origin, *group, *result)
+    return result[0]
 
 
 def around(block, axis):
     count = lax.axis_size(axis)
     return [block] + [
         lax.ppermute(block, axis, [(i, (i + step) % count) for i in range(count)]) for step in range(1, count)
+    ]
+
+
+def exchange(blocks, axis):
+    count = lax.axis_size(axis)
+    me = lax.axis_index(axis)
+
+    def block_for(step):
+        return lax.dynamic_index_in_dim(blocks, me ^ step, 0, keepdims=False)
+
+    return [block_for(0)] + [
+        lax.ppermute(block_for(step), axis, [(i, i ^ step) for i in range(count)])
+        for step in range(1, count)
     ]
 
 
@@ -385,16 +460,19 @@
         return values.reshape(count, 2, VB // LANES, LANES).transpose(0, 2, 1, 3).reshape(count * 4, LANES)
 
     vis = rows_of(visibilities[0])
-    theirs = lax.ppermute(
-        lax.dynamic_slice_in_dim(vis, (1 - my_pol) * (half * 4), half * 4, 0), "pol", [(0, 1), (1, 0)]
-    )
+    def half_of(rows, which):
+        return lax.dynamic_slice_in_dim(rows, which * (half * 4), half * 4, 0)
+
+    theirs = lax.ppermute(half_of(vis, 1 - my_pol), "pol", [(0, 1), (1, 0)])
     sign = (1.0 - 2.0 * my_pol.astype(f32))[None]
-    at = jnp.stack([my_pol * half, my_shard * blocks + my_pol * half])
-    keep, send = slot_sums(at, sign, block_slot, rows_of(uv_coords), vis, theirs, shard_count, slots)
+    first = (my_shard * blocks + my_pol * half)[None]
+    coords, mine = lax.optimization_barrier((rows_of(uv_coords), vis))
+    coords, mine = half_of(coords, my_pol), half_of(mine, my_pol)
+    keep, send = slot_sums(first, sign, block_slot, coords, mine, theirs, shard_count, slots)
     got = lax.ppermute(send, "pol", [(0, 1), (1, 0)])
     partial = (keep + got.astype(f32)).astype(bf16)
-    partial = lax.all_to_all(partial, "bl", split_axis=0, concat_axis=0, tiled=True)
-    subs = around(subgrid_transform(partial, slot_table[2], slot_table[:2], slots), "chan")
+    parts = exchange(partial, "bl")
+    subs = around(subgrid_transform(parts, slot_table[2], slot_table[:2], slots), "chan")
     origin = jnp.stack([my_shard * strip_rows, my_chan * cols])
     return place(origin, subs, strip_rows, cols)[None]
 

time: 55.6 us -> 49.2 us (0.88)
  waiting for transfers between devices: 13.5 us -> 8.79 us
  other arithmetic: 0.93 us -> 0.15 us
  starting transfers between devices: 10.7 us -> 10.1 us
    all_to_all x1 -> x0, waiting for transfers between devices: 5.79 us -> none  [on_device(): lax.all_to_all(partial, 'bl', split_axis=0, concat_axis=0, tiled=True)]
    all_to_all x1 -> x0, starting transfers between devices: 5.08 us -> none  [on_device(): lax.all_to_all(partial, 'bl', split_axis=0, concat_axis=0, tiled=True)]
    ppermute x1 -> x4, starting transfers between devices: 0.52 us -> 5.03 us  [the longest x3 4.51 us: exchange(): lax.ppermute(block_for(step), axis, [(i, i ^ step) for i in range(count)])]
    ppermute x1 -> x4, waiting for transfers between devices: 1.65 us -> 4.61 us  [the longest x3 4.08 us: exchange(): lax.ppermute(block_for(step), axis, [(i, i ^ step) for i in range(count)])]
    ppermute x3, waiting for transfers between devices: 5.03 us -> 3.01 us  [around(): lax.ppermute(block, axis, [(i, (i + step) % count) for i in range(count)])]
    unnamed x16 -> x14, local copies, waits for them, and re-layouts: 1.36 us -> 0.04 us
    dynamic_slice x1 -> x2, local copies, waits for them, and re-layouts: 1.23 us -> 2.41 us  [half_of(): return lax.dynamic_slice_in_dim(rows, which * (half * 4), half * 4, 0)]
    pallas_call x1 -> x2, Pallas kernels: 4.51 us -> 5.66 us  [place(): pl.pallas_call(functools.partial(place_kernel, first, not first, len(grou...]
  transfers between devices with their start and end apart: 6 -> 8, of which waited for: 6 -> 7; matrix products, arithmetic and copies ran while one was open for 0% -> 3% of each run, Pallas kernels for 0% -> 4%
where the time goes in v3:
time: 49.2 us; the launch traced here: 48.9 us
  Pallas kernels  27.1 us (55%)
  starting transfers between devices  10.1 us (21%)
  waiting for transfers between devices  8.79 us (18%)
  local copies, waits for them, and re-layouts  2.59 us (5%)
    pallas_call x1, Pallas kernels, slot_sums(): pl.pallas_call(slot_sums_kernel, out_shape=[jax.ShapeDtypeStruct((shard_c...  20.3 us
    pallas_call x2, Pallas kernels, place(): pl.pallas_call(functools.partial(place_kernel, first, not first, len(grou...  5.66 us
    ppermute x3, starting transfers between devices, around(): lax.ppermute(block, axis, [(i, (i + step) % count) for i in range(count)])  4.67 us
    ppermute x3, starting transfers between devices, exchange(): lax.ppermute(block_for(step), axis, [(i, i ^ step) for i in range(count)])  4.51 us
    ppermute x3, waiting for transfers between devices, exchange(): lax.ppermute(block_for(step), axis, [(i, i ^ step) for i in range(count)])  4.08 us
    ppermute x3, waiting for transfers between devices, around(): lax.ppermute(block, axis, [(i, (i + step) % count) for i in range(count)])  3.01 us
    dynamic_slice x2, local copies, waits for them, and re-layouts, half_of(): return lax.dynamic_slice_in_dim(rows, which * (half * 4), half * 4, 0)  2.41 us
    pallas_call x1, Pallas kernels, subgrid_transform(): pl.pallas_call(transform_kernel, out_shape=jax.ShapeDtypeStruct((slots //...  1.19 us
  transfers between devices with their start and end apart: 8, of which 7 were waited for; matrix products, arithmetic and copies ran while one was open for 3% of the time, Pallas kernels for 4%

profile of v3, /device:TPU:0, one launch (start us, length us, event | category | flops | bytes accessed | tf_op | source)
XLA Modules:
  0.0 48.9 jit_solution(11549521092409655076)
XLA Ops:
  0.0 0.0 copy-start.5
  0.0 1.2 %constant_dynamic-slice_fusion = bf16[2560,128]{1,0:T(8,128)(2,1)S(1)} fusion(bf16[5120,128]{1,0:T(8,128)(2,1)} %bitcast.29, s32[]{:T(128)S(6)} %select_n.35), kind=kLoop, calls=%fused_computation.8 | loop fusion | bytes 1310724 | tf_op jit(solution)/shard_map/dynamic_slice | solution.py:464
  1.2 0.5 %collective-permute-start = (bf16[2560,128]{1,0:T(8,128)(2,1)S(1)}, bf16[2560,128]{1,0:T(8,128)(2,1)S(1)}, u32[]{:S(2)}, u32[]{:S(2)}) collective-permute-start(bf16[2560,128]{1,0:T(8,128)(2,1)S(1)} %constant_dynamic-slice_fusion), channel_id=1, source_target_pairs={{0,1},{1,0},{2,3},{3,2},{4,5},{5,4},{6,7},{7,6},{8,9},{9,8},{10,11... | collective-permute-start | bytes 1966088 | tf_op jit(solution)/shard_map/ppermute | solution.py:466
  1.8 0.0 copy-done.5
  1.8 0.0 copy-start.4
  1.8 1.2 %constant_dynamic-slice_fusion.1 = (bf16[2560,128]{1,0:T(8,128)(2,1)S(1)}, bf16[2560,128]{1,0:T(8,128)(2,1)S(1)}) fusion(bf16[5120,128]{1,0:T(8,128)(2,1)S(1)} %bitcast.30, s32[]{:T(128)S(6)} %select_n.34, bf16[5120,128]{1,0:T(8,128)(2,1)} %bitcast.31), kind=kLoop, calls=%fused_computation.9 | loop fusion | bytes 2621444 | tf_op jit(solution)/shard_map/dynamic_slice | solution.py:464
  2.9 0.5 %collective-permute-done.theirs_ref = bf16[2560,128]{1,0:T(8,128)(2,1)S(1)} collective-permute-done((bf16[2560,128]{1,0:T(8,128)(2,1)S(1)}, bf16[2560,128]{1,0:T(8,128)(2,1)S(1)}, u32[]{:S(2)}, u32[]{:S(2)}) %collective-permute-start) | collective-permute-done | bytes 655392 | tf_op jit(solution)/shard_map/ppermute | solution.py:466
  3.5 0.0 copy-done.4
  3.5 0.0 copy-start.6
  3.5 20.3 %slot_sums.1 = (f32[4,272,128]{2,1,0:T(8,128)S(1)}, bf16[4,272,128]{2,1,0:T(8,128)(2,1)S(1)}) custom-call(s32[1]{0:T(128)} %bitcast.5.first_ref, f32[1]{0:T(128)} %bitcast.6.sign_ref, s32[5120]{0:T(1024)S(1)} %copy-done.4, bf16[2560,128]{1,0:T(8,128)(2,1)S(1)} %get-tuple-element.22.uv_ref, bf16[2560,128]{1,0:T(8,128)(2,1)S(1)} %get-tuple-element.21.mine_ref, ...), custom_call_target="tpu_custom_call" | custom-call | flops 60000002048 | bytes 4000000 | tf_op jit(solution)/shard_map/slot_sums/pallas_call | solution.py:196
  23.8 0.0 copy-start
  23.8 0.0 copy-start.1
  23.8 0.0 copy-start.2
  23.8 0.0 copy-start.3
  23.8 0.4 collective-permute-start.1
  24.3 0.0 copy-done.6
  24.3 1.2 %collective-permute-done.1 = bf16[4,272,128]{2,1,0:T(8,128)(2,1)S(1)} collective-permute-done((bf16[4,272,128]{2,1,0:T(8,128)(2,1)S(1)}, bf16[4,272,128]{2,1,0:T(8,128)(2,1)S(1)}, u32[]{:S(2)}, u32[]{:S(2)}) %collective-permute-start.1) | collective-permute-done | bytes 278560 | tf_op jit(solution)/shard_map/ppermute | solution.py:472
  25.4 0.1 add_convert_fusion
  25.5 3.9 %collective-permute-start.4 = (bf16[272,128]{1,0:T(8,128)(2,1)S(1)}, bf16[272,128]{1,0:T(8,128)(2,1)S(1)}, u32[]{:S(2)}, u32[]{:S(2)}) collective-permute-start(bf16[272,128]{1,0:T(8,128)(2,1)S(1)} %get-tuple-element.15), channel_id=1, source_target_pairs={{0,6},{2,4},{4,2},{6,0},{1,7},{3,5},{5,3},{7,1},{8,14},{10,12},{12... | collective-permute-start | bytes 208904 | tf_op jit(solution)/shard_map/ppermute | solution.py:441
  29.4 0.5 %collective-permute-start.3 = (bf16[272,128]{1,0:T(8,128)(2,1)S(1)}, bf16[272,128]{1,0:T(8,128)(2,1)S(1)}, u32[]{:S(2)}, u32[]{:S(2)}) collective-permute-start(bf16[272,128]{1,0:T(8,128)(2,1)S(1)} %get-tuple-element.16), channel_id=1, source_target_pairs={{0,4},{2,6},{4,0},{6,2},{1,5},{3,7},{5,1},{7,3},{8,12},{10,14},{12... | collective-permute-start | bytes 208904 | tf_op jit(solution)/shard_map/ppermute | solution.py:441
  29.9 0.1 collective-permute-start.2
  30.1 0.1 convert_element_type.26
  30.2 1.8 %collective-permute-done.4.refs_3_ = bf16[272,128]{1,0:T(8,128)(2,1)S(1)} collective-permute-done((bf16[272,128]{1,0:T(8,128)(2,1)S(1)}, bf16[272,128]{1,0:T(8,128)(2,1)S(1)}, u32[]{:S(2)}, u32[]{:S(2)}) %collective-permute-start.4) | collective-permute-done | bytes 69664 | tf_op jit(solution)/shard_map/ppermute | solution.py:441
  31.9 1.8 %collective-permute-done.3.refs_2_ = bf16[272,128]{1,0:T(8,128)(2,1)S(1)} collective-permute-done((bf16[272,128]{1,0:T(8,128)(2,1)S(1)}, bf16[272,128]{1,0:T(8,128)(2,1)S(1)}, u32[]{:S(2)}, u32[]{:S(2)}) %collective-permute-start.3) | collective-permute-done | bytes 69664 | tf_op jit(solution)/shard_map/ppermute | solution.py:441
  33.7 0.5 %collective-permute-done.2.refs_1_ = bf16[272,128]{1,0:T(8,128)(2,1)S(1)} collective-permute-done((bf16[272,128]{1,0:T(8,128)(2,1)S(1)}, bf16[272,128]{1,0:T(8,128)(2,1)S(1)}, u32[]{:S(2)}, u32[]{:S(2)}) %collective-permute-start.2) | collective-permute-done | bytes 69664 | tf_op jit(solution)/shard_map/ppermute | solution.py:441
  34.2 0.0 copy-done
  34.2 0.0 copy-done.1
  34.2 0.0 copy-done.2
  34.3 0.0 copy-done.3
  34.3 1.2 %subgrid_transform.1.refs_0_ = bf16[272,128]{1,0:T(8,128)(2,1)S(1)} custom-call(s32[16]{0:T(128)S(1)} %slice_bitcast_fusion.planes_ref, f32[16,128]{1,0:T(8,128)S(1)} %pad.4.corners_ref, f32[32,128]{1,0:T(8,128)S(1)} %copy-done.3, f32[32,128]{1,0:T(8,128)S(1)} %copy-done.2, bf16[2,128,256]{2,1,0:T(8,128)(2,1)S(1)} %copy-done, ...), custom_call_target="tpu_custom_call" | custom-call | tf_op jit(solution)/shard_map/subgrid_transform/pallas_call | solution.py:320
  35.5 3.7 %collective-permute-start.7 = (bf16[272,128]{1,0:T(8,128)(2,1)S(1)}, bf16[272,128]{1,0:T(8,128)(2,1)S(1)}, u32[]{:S(2)}, u32[]{:S(2)}) collective-permute-start(bf16[272,128]{1,0:T(8,128)(2,1)S(1)} %subgrid_transform.1.refs_0_), channel_id=1, source_target_pairs={{0,24},{8,0},{16,8},{24,16},{1,25},{9,1},{17,9},{25,17},{2,26},{10... | collective-permute-start | bytes 208904 | tf_op jit(solution)/shard_map/ppermute | solution.py:429
  39.1 0.0 collective-permute-start.6
  39.1 1.0 %collective-permute-start.5 = (bf16[272,128]{1,0:T(8,128)(2,1)S(1)}, bf16[272,128]{1,0:T(8,128)(2,1)S(1)}, u32[]{:S(2)}, u32[]{:S(2)}) collective-permute-start(bf16[272,128]{1,0:T(8,128)(2,1)S(1)} %subgrid_transform.1.refs_0_), channel_id=1, source_target_pairs={{0,8},{8,16},{16,24},{24,0},{1,9},{9,17},{17,25},{25,1},{2,10},{10... | collective-permute-start | bytes 208904 | tf_op jit(solution)/shard_map/ppermute | solution.py:429
  40.1 0.1 pad_add_fusion.origin_ref
  40.2 2.0 %place_own.1.refs_3_ = f32[2,6,520,128]{3,2,1,0:T(8,128)S(1)} custom-call(s32[2]{0:T(128)S(1)} %pad_add_fusion.origin_ref, bf16[272,128]{1,0:T(8,128)(2,1)S(1)} %subgrid_transform.1.refs_0_), custom_call_target="tpu_custom_call" | custom-call | tf_op jit(solution)/shard_map/place_own/pallas_call | solution.py:409
  42.2 0.0 collective-permute-done.7.refs_2_
  42.2 2.1 %collective-permute-done.6.refs_1_ = bf16[272,128]{1,0:T(8,128)(2,1)S(1)} collective-permute-done((bf16[272,128]{1,0:T(8,128)(2,1)S(1)}, bf16[272,128]{1,0:T(8,128)(2,1)S(1)}, u32[]{:S(2)}, u32[]{:S(2)}) %collective-permute-start.6) | collective-permute-done | bytes 69664 | tf_op jit(solution)/shard_map/ppermute | solution.py:429
  44.3 0.9 %collective-permute-done.5.refs_0_ = bf16[272,128]{1,0:T(8,128)(2,1)S(1)} collective-permute-done((bf16[272,128]{1,0:T(8,128)(2,1)S(1)}, bf16[272,128]{1,0:T(8,128)(2,1)S(1)}, u32[]{:S(2)}, u32[]{:S(2)}) %collective-permute-start.5) | collective-permute-done | bytes 69664 | tf_op jit(solution)/shard_map/ppermute | solution.py:429
  45.2 3.7 %place_others.1 = (f32[2,512,512]{2,1,0:T(8,128)}, f32[2,6,520,128]{3,2,1,0:T(8,128)S(1)}) custom-call(s32[2]{0:T(128)S(1)} %pad_add_fusion.origin_ref, bf16[272,128]{1,0:T(8,128)(2,1)S(1)} %collective-permute-done.5.refs_0_, bf16[272,128]{1,0:T(8,128)(2,1)S(1)} %collective-permute-done.6.refs_1_, ...), custom_call_target="tpu_custom_call", output_to_operand_aliasing={{1}: (4, {})} | custom-call | tf_op jit(solution)/shard_map/place_others/pallas_call | solution.py:409
  (6 shorter events, 0.1 us)
Async XLA Ops:
  0.0 1.8 %copy-start.5 = (bf16[1,1280,2,256]{3,2,1,0:T(2,128)(2,1)S(1)}, bf16[1,1280,2,256]{3,2,1,0:T(2,128)(2,1)}, u32[]{:S(2)}) copy-start(bf16[1,1280,2,256]{3,2,1,0:T(2,128)(2,1)} %param.8) | copy-start | bytes 3932164
  1.2 2.2 %collective-permute-start = (bf16[2560,128]{1,0:T(8,128)(2,1)S(1)}, bf16[2560,128]{1,0:T(8,128)(2,1)S(1)}, u32[]{:S(2)}, u32[]{:S(2)}) collective-permute-start(bf16[2560,128]{1,0:T(8,128)(2,1)S(1)} %constant_dynamic-slice_fusion), channel_id=1, source_target_pairs={{0,1},{1,0},{2,3},{3,2},{4,5},{5,4},{6,7},{7,6},{8,9},{9,8},{10,11... | collective-permute-start | bytes 1966088 | tf_op jit(solution)/shard_map/ppermute | solution.py:466
  1.8 1.7 %copy-start.4 = (s32[5120]{0:T(1024)S(1)}, s32[5120]{0:T(1024)}, u32[]{:S(2)}) copy-start(s32[5120]{0:T(1024)} %ids_ref.1) | copy-start | bytes 61444
  3.5 20.8 %copy-start.6 = (s32[3,16]{1,0:T(4,128)S(1)}, s32[3,16]{1,0:T(4,128)}, u32[]{:S(2)}) copy-start(s32[3,16]{1,0:T(4,128)} %param.11) | copy-start | bytes 580
  23.8 10.5 %copy-start = (bf16[2,128,256]{2,1,0:T(8,128)(2,1)S(1)}, bf16[2,128,256]{2,1,0:T(8,128)(2,1)}, u32[]{:S(2)}) copy-start(bf16[2,128,256]{2,1,0:T(8,128)(2,1)} %constant.81.clone.columns_ref) | copy-start | bytes 393220
  23.8 10.5 %copy-start.1 = (bf16[2,32,64]{2,1,0:T(8,128)(2,1)S(1)}, bf16[2,32,64]{2,1,0:T(8,128)(2,1)}, u32[]{:S(2)}) copy-start(bf16[2,32,64]{2,1,0:T(8,128)(2,1)} %constant.82.clone.rows_ref) | copy-start | bytes 24580
  23.8 10.5 %copy-start.2 = (f32[32,128]{1,0:T(8,128)S(1)}, f32[32,128]{1,0:T(8,128)}, u32[]{:S(2)}) copy-start(f32[32,128]{1,0:T(8,128)} %constant.80.clone.tapers_ref) | copy-start | bytes 49156
  23.8 10.4 %copy-start.3 = (f32[32,128]{1,0:T(8,128)S(1)}, f32[32,128]{1,0:T(8,128)}, u32[]{:S(2)}) copy-start(f32[32,128]{1,0:T(8,128)} %constant.79.clone.turns_ref) | copy-start | bytes 49156
  23.8 1.6 %collective-permute-start.1 = (bf16[4,272,128]{2,1,0:T(8,128)(2,1)S(1)}, bf16[4,272,128]{2,1,0:T(8,128)(2,1)S(1)}, u32[]{:S(2)}, u32[]{:S(2)}) collective-permute-start(bf16[4,272,128]{2,1,0:T(8,128)(2,1)S(1)} %get-tuple-element.13), channel_id=1, source_target_pairs={{0,1},{1,0},{2,3},{3,2},{4,5},{5,4},{6,7},{7,6},{8,9},{9,8},{10,11... | collective-permute-start | bytes 835592 | tf_op jit(solution)/shard_map/ppermute | solution.py:472
  25.5 6.4 %collective-permute-start.4 = (bf16[272,128]{1,0:T(8,128)(2,1)S(1)}, bf16[272,128]{1,0:T(8,128)(2,1)S(1)}, u32[]{:S(2)}, u32[]{:S(2)}) collective-permute-start(bf16[272,128]{1,0:T(8,128)(2,1)S(1)} %get-tuple-element.15), channel_id=1, source_target_pairs={{0,6},{2,4},{4,2},{6,0},{1,7},{3,5},{5,3},{7,1},{8,14},{10,12},{12... | collective-permute-start | bytes 208904 | tf_op jit(solution)/shard_map/ppermute | solution.py:441
  29.4 4.3 %collective-permute-start.3 = (bf16[272,128]{1,0:T(8,128)(2,1)S(1)}, bf16[272,128]{1,0:T(8,128)(2,1)S(1)}, u32[]{:S(2)}, u32[]{:S(2)}) collective-permute-start(bf16[272,128]{1,0:T(8,128)(2,1)S(1)} %get-tuple-element.16), channel_id=1, source_target_pairs={{0,4},{2,6},{4,0},{6,2},{1,5},{3,7},{5,1},{7,3},{8,12},{10,14},{12... | collective-permute-start | bytes 208904 | tf_op jit(solution)/shard_map/ppermute | solution.py:441
  29.9 4.3 %collective-permute-start.2 = (bf16[272,128]{1,0:T(8,128)(2,1)S(1)}, bf16[272,128]{1,0:T(8,128)(2,1)S(1)}, u32[]{:S(2)}, u32[]{:S(2)}) collective-permute-start(bf16[272,128]{1,0:T(8,128)(2,1)S(1)} %get-tuple-element.17), channel_id=1, source_target_pairs={{0,2},{2,0},{4,6},{6,4},{1,3},{3,1},{5,7},{7,5},{8,10},{10,8},{12,... | collective-permute-start | bytes 208904 | tf_op jit(solution)/shard_map/ppermute | solution.py:441
  35.5 6.7 %collective-permute-start.7 = (bf16[272,128]{1,0:T(8,128)(2,1)S(1)}, bf16[272,128]{1,0:T(8,128)(2,1)S(1)}, u32[]{:S(2)}, u32[]{:S(2)}) collective-permute-start(bf16[272,128]{1,0:T(8,128)(2,1)S(1)} %subgrid_transform.1.refs_0_), channel_id=1, source_target_pairs={{0,24},{8,0},{16,8},{24,16},{1,25},{9,1},{17,9},{25,17},{2,26},{10... | collective-permute-start | bytes 208904 | tf_op jit(solution)/shard_map/ppermute | solution.py:429
  39.1 5.2 %collective-permute-start.6 = (bf16[272,128]{1,0:T(8,128)(2,1)S(1)}, bf16[272,128]{1,0:T(8,128)(2,1)S(1)}, u32[]{:S(2)}, u32[]{:S(2)}) collective-permute-start(bf16[272,128]{1,0:T(8,128)(2,1)S(1)} %subgrid_transform.1.refs_0_), channel_id=1, source_target_pairs={{0,16},{8,24},{16,0},{24,8},{1,17},{9,25},{17,1},{25,9},{2,18},{10... | collective-permute-start | bytes 208904 | tf_op jit(solution)/shard_map/ppermute | solution.py:429
  39.1 6.1 %collective-permute-start.5 = (bf16[272,128]{1,0:T(8,128)(2,1)S(1)}, bf16[272,128]{1,0:T(8,128)(2,1)S(1)}, u32[]{:S(2)}, u32[]{:S(2)}) collective-permute-start(bf16[272,128]{1,0:T(8,128)(2,1)S(1)} %subgrid_transform.1.refs_0_), channel_id=1, source_target_pairs={{0,8},{8,16},{16,24},{24,0},{1,9},{9,17},{17,25},{25,1},{2,10},{10... | collective-permute-start | bytes 208904 | tf_op jit(solution)/shard_map/ppermute | solution.py:429

commit v4 on v3

--- a/solution.py
+++ b/solution.py
@@ -60,7 +60,7 @@
 
 
 GROUP = 8
-BATCH = 4
+BATCH = 8
 PITCH = 9
 
 
@@ -401,7 +401,7 @@
     tiles = cols // LANES
     strip_shape = jax.ShapeDtypeStruct((2, tiles + 2, strip_rows + 8, LANES), f32)
     result = []
-    for first, group in ((True, subs[:1]), (False, subs[1:])):
+    for first, group in ((True, subs[:1] + subs[-1:]), (False, subs[1:-1])):
         outs, specs = [strip_shape], [vmem]
         if not first:
             outs = [jax.ShapeDtypeStruct((2, strip_rows, cols), f32)] + outs

time: 49.2 us -> 48.4 us (0.984)
  transfers between devices with their start and end apart: 8 -> 8, of which waited for: 7 -> 8; matrix products, arithmetic and copies ran while one was open for 3% -> 3% of each run, Pallas kernels for 4% -> 5%
where the time goes in v4:
time: 48.4 us; the launch traced here: 48.3 us
  Pallas kernels  26.9 us (56%)
  starting transfers between devices  10.2 us (21%)
  waiting for transfers between devices  8.4 us (17%)
  local copies, waits for them, and re-layouts  2.59 us (5%)
    pallas_call x1, Pallas kernels, slot_sums(): pl.pallas_call(slot_sums_kernel, out_shape=[jax.ShapeDtypeStruct((shard_c...  19.8 us
    pallas_call x2, Pallas kernels, place(): pl.pallas_call(functools.partial(place_kernel, first, not first, len(grou...  5.92 us
    ppermute x3, starting transfers between devices, around(): lax.ppermute(block, axis, [(i, (i + step) % count) for i in range(count)])  4.68 us
    ppermute x3, starting transfers between devices, exchange(): lax.ppermute(block_for(step), axis, [(i, i ^ step) for i in range(count)])  4.52 us
    ppermute x3, waiting for transfers between devices, exchange(): lax.ppermute(block_for(step), axis, [(i, i ^ step) for i in range(count)])  4.07 us
    ppermute x3, waiting for transfers between devices, around(): lax.ppermute(block, axis, [(i, (i + step) % count) for i in range(count)])  2.63 us
    dynamic_slice x2, local copies, waits for them, and re-layouts, half_of(): return lax.dynamic_slice_in_dim(rows, which * (half * 4), half * 4, 0)  2.41 us
    pallas_call x1, Pallas kernels, subgrid_transform(): pl.pallas_call(transform_kernel, out_shape=jax.ShapeDtypeStruct((slots //...  1.19 us
  transfers between devices with their start and end apart: 8, of which 8 were waited for; matrix products, arithmetic and copies ran while one was open for 3% of the time, Pallas kernels for 5%

profile of v4, /device:TPU:0, one launch (start us, length us, event | category | flops | bytes accessed | tf_op | source)
XLA Modules:
  0.0 48.3 jit_solution(14609599574074413232)
XLA Ops:
  0.0 0.0 copy-start.5
  0.0 1.2 %constant_dynamic-slice_fusion = bf16[2560,128]{1,0:T(8,128)(2,1)S(1)} fusion(bf16[5120,128]{1,0:T(8,128)(2,1)} %bitcast.29, s32[]{:T(128)S(6)} %select_n.35), kind=kLoop, calls=%fused_computation.8 | loop fusion | bytes 1310724 | tf_op jit(solution)/shard_map/dynamic_slice | solution.py:464
  1.2 0.5 %collective-permute-start = (bf16[2560,128]{1,0:T(8,128)(2,1)S(1)}, bf16[2560,128]{1,0:T(8,128)(2,1)S(1)}, u32[]{:S(2)}, u32[]{:S(2)}) collective-permute-start(bf16[2560,128]{1,0:T(8,128)(2,1)S(1)} %constant_dynamic-slice_fusion), channel_id=1, source_target_pairs={{0,1},{1,0},{2,3},{3,2},{4,5},{5,4},{6,7},{7,6},{8,9},{9,8},{10,11... | collective-permute-start | bytes 1966088 | tf_op jit(solution)/shard_map/ppermute | solution.py:466
  1.8 0.0 copy-done.5
  1.8 0.0 copy-start.4
  1.8 1.2 %constant_dynamic-slice_fusion.1 = (bf16[2560,128]{1,0:T(8,128)(2,1)S(1)}, bf16[2560,128]{1,0:T(8,128)(2,1)S(1)}) fusion(bf16[5120,128]{1,0:T(8,128)(2,1)S(1)} %bitcast.30, s32[]{:T(128)S(6)} %select_n.34, bf16[5120,128]{1,0:T(8,128)(2,1)} %bitcast.31), kind=kLoop, calls=%fused_computation.9 | loop fusion | bytes 2621444 | tf_op jit(solution)/shard_map/dynamic_slice | solution.py:464
  2.9 0.5 %collective-permute-done.theirs_ref = bf16[2560,128]{1,0:T(8,128)(2,1)S(1)} collective-permute-done((bf16[2560,128]{1,0:T(8,128)(2,1)S(1)}, bf16[2560,128]{1,0:T(8,128)(2,1)S(1)}, u32[]{:S(2)}, u32[]{:S(2)}) %collective-permute-start) | collective-permute-done | bytes 655392 | tf_op jit(solution)/shard_map/ppermute | solution.py:466
  3.5 0.0 copy-done.4
  3.5 0.0 copy-start.6
  3.5 19.8 %slot_sums.1 = (f32[4,272,128]{2,1,0:T(8,128)S(1)}, bf16[4,272,128]{2,1,0:T(8,128)(2,1)S(1)}) custom-call(s32[1]{0:T(128)} %bitcast.5.first_ref, f32[1]{0:T(128)} %bitcast.6.sign_ref, s32[5120]{0:T(1024)S(1)} %copy-done.4, bf16[2560,128]{1,0:T(8,128)(2,1)S(1)} %get-tuple-element.22.uv_ref, bf16[2560,128]{1,0:T(8,128)(2,1)S(1)} %get-tuple-element.21.mine_ref, ...), custom_call_target="tpu_custom_call" | custom-call | flops 60000002048 | bytes 4000000 | tf_op jit(solution)/shard_map/slot_sums/pallas_call | solution.py:196
  23.3 0.0 copy-start
  23.3 0.0 copy-start.1
  23.3 0.0 copy-start.2
  23.3 0.0 copy-start.3
  23.3 0.5 collective-permute-start.1
  23.8 0.0 copy-done.6
  23.8 1.2 %collective-permute-done.1 = bf16[4,272,128]{2,1,0:T(8,128)(2,1)S(1)} collective-permute-done((bf16[4,272,128]{2,1,0:T(8,128)(2,1)S(1)}, bf16[4,272,128]{2,1,0:T(8,128)(2,1)S(1)}, u32[]{:S(2)}, u32[]{:S(2)}) %collective-permute-start.1) | collective-permute-done | bytes 278560 | tf_op jit(solution)/shard_map/ppermute | solution.py:472
  25.0 0.1 add_convert_fusion
  25.1 3.9 %collective-permute-start.4 = (bf16[272,128]{1,0:T(8,128)(2,1)S(1)}, bf16[272,128]{1,0:T(8,128)(2,1)S(1)}, u32[]{:S(2)}, u32[]{:S(2)}) collective-permute-start(bf16[272,128]{1,0:T(8,128)(2,1)S(1)} %get-tuple-element.15), channel_id=1, source_target_pairs={{0,6},{2,4},{4,2},{6,0},{1,7},{3,5},{5,3},{7,1},{8,14},{10,12},{12... | collective-permute-start | bytes 208904 | tf_op jit(solution)/shard_map/ppermute | solution.py:441
  29.0 0.5 %collective-permute-start.3 = (bf16[272,128]{1,0:T(8,128)(2,1)S(1)}, bf16[272,128]{1,0:T(8,128)(2,1)S(1)}, u32[]{:S(2)}, u32[]{:S(2)}) collective-permute-start(bf16[272,128]{1,0:T(8,128)(2,1)S(1)} %get-tuple-element.16), channel_id=1, source_target_pairs={{0,4},{2,6},{4,0},{6,2},{1,5},{3,7},{5,1},{7,3},{8,12},{10,14},{12... | collective-permute-start | bytes 208904 | tf_op jit(solution)/shard_map/ppermute | solution.py:441
  29.5 0.1 collective-permute-start.2
  29.6 0.1 convert_element_type.26
  29.7 1.8 %collective-permute-done.4.refs_3_ = bf16[272,128]{1,0:T(8,128)(2,1)S(1)} collective-permute-done((bf16[272,128]{1,0:T(8,128)(2,1)S(1)}, bf16[272,128]{1,0:T(8,128)(2,1)S(1)}, u32[]{:S(2)}, u32[]{:S(2)}) %collective-permute-start.4) | collective-permute-done | bytes 69664 | tf_op jit(solution)/shard_map/ppermute | solution.py:441
  31.5 1.8 %collective-permute-done.3.refs_2_ = bf16[272,128]{1,0:T(8,128)(2,1)S(1)} collective-permute-done((bf16[272,128]{1,0:T(8,128)(2,1)S(1)}, bf16[272,128]{1,0:T(8,128)(2,1)S(1)}, u32[]{:S(2)}, u32[]{:S(2)}) %collective-permute-start.3) | collective-permute-done | bytes 69664 | tf_op jit(solution)/shard_map/ppermute | solution.py:441
  33.3 0.5 %collective-permute-done.2.refs_1_ = bf16[272,128]{1,0:T(8,128)(2,1)S(1)} collective-permute-done((bf16[272,128]{1,0:T(8,128)(2,1)S(1)}, bf16[272,128]{1,0:T(8,128)(2,1)S(1)}, u32[]{:S(2)}, u32[]{:S(2)}) %collective-permute-start.2) | collective-permute-done | bytes 69664 | tf_op jit(solution)/shard_map/ppermute | solution.py:441
  33.8 0.0 copy-done
  33.8 0.0 copy-done.1
  33.8 0.0 copy-done.2
  33.8 0.0 copy-done.3
  33.8 1.2 %subgrid_transform.1.refs_0_ = bf16[272,128]{1,0:T(8,128)(2,1)S(1)} custom-call(s32[16]{0:T(128)S(1)} %slice_bitcast_fusion.planes_ref, f32[16,128]{1,0:T(8,128)S(1)} %pad.4.corners_ref, f32[32,128]{1,0:T(8,128)S(1)} %copy-done.3, f32[32,128]{1,0:T(8,128)S(1)} %copy-done.2, bf16[2,128,256]{2,1,0:T(8,128)(2,1)S(1)} %copy-done, ...), custom_call_target="tpu_custom_call" | custom-call | tf_op jit(solution)/shard_map/subgrid_transform/pallas_call | solution.py:320
  35.0 3.7 %collective-permute-start.7 = (bf16[272,128]{1,0:T(8,128)(2,1)S(1)}, bf16[272,128]{1,0:T(8,128)(2,1)S(1)}, u32[]{:S(2)}, u32[]{:S(2)}) collective-permute-start(bf16[272,128]{1,0:T(8,128)(2,1)S(1)} %subgrid_transform.1.refs_0_), channel_id=1, source_target_pairs={{0,24},{8,0},{16,8},{24,16},{1,25},{9,1},{17,9},{25,17},{2,26},{10... | collective-permute-start | bytes 208904 | tf_op jit(solution)/shard_map/ppermute | solution.py:429
  38.7 0.0 collective-permute-start.6
  38.7 1.0 %collective-permute-start.5 = (bf16[272,128]{1,0:T(8,128)(2,1)S(1)}, bf16[272,128]{1,0:T(8,128)(2,1)S(1)}, u32[]{:S(2)}, u32[]{:S(2)}) collective-permute-start(bf16[272,128]{1,0:T(8,128)(2,1)S(1)} %subgrid_transform.1.refs_0_), channel_id=1, source_target_pairs={{0,8},{8,16},{16,24},{24,0},{1,9},{9,17},{17,25},{25,1},{2,10},{10... | collective-permute-start | bytes 208904 | tf_op jit(solution)/shard_map/ppermute | solution.py:429
  39.7 0.1 pad_add_fusion.origin_ref
  39.7 0.9 %collective-permute-done.7.refs_1_ = bf16[272,128]{1,0:T(8,128)(2,1)S(1)} collective-permute-done((bf16[272,128]{1,0:T(8,128)(2,1)S(1)}, bf16[272,128]{1,0:T(8,128)(2,1)S(1)}, u32[]{:S(2)}, u32[]{:S(2)}) %collective-permute-start.7) | collective-permute-done | bytes 69664 | tf_op jit(solution)/shard_map/ppermute | solution.py:429
  40.6 2.4 %place_own.1.refs_2_ = f32[2,6,520,128]{3,2,1,0:T(8,128)S(1)} custom-call(s32[2]{0:T(128)S(1)} %pad_add_fusion.origin_ref, bf16[272,128]{1,0:T(8,128)(2,1)S(1)} %subgrid_transform.1.refs_0_, bf16[272,128]{1,0:T(8,128)(2,1)S(1)} %collective-permute-done.7.refs_1_), custom_call_target="tpu_custom_call" | custom-call | tf_op jit(solution)/shard_map/place_own/pallas_call | solution.py:409
  43.0 0.9 %collective-permute-done.6.refs_1_ = bf16[272,128]{1,0:T(8,128)(2,1)S(1)} collective-permute-done((bf16[272,128]{1,0:T(8,128)(2,1)S(1)}, bf16[272,128]{1,0:T(8,128)(2,1)S(1)}, u32[]{:S(2)}, u32[]{:S(2)}) %collective-permute-start.6) | collective-permute-done | bytes 69664 | tf_op jit(solution)/shard_map/ppermute | solution.py:429
  43.9 0.9 %collective-permute-done.5.refs_0_ = bf16[272,128]{1,0:T(8,128)(2,1)S(1)} collective-permute-done((bf16[272,128]{1,0:T(8,128)(2,1)S(1)}, bf16[272,128]{1,0:T(8,128)(2,1)S(1)}, u32[]{:S(2)}, u32[]{:S(2)}) %collective-permute-start.5) | collective-permute-done | bytes 69664 | tf_op jit(solution)/shard_map/ppermute | solution.py:429
  44.8 3.5 %place_others.1 = (f32[2,512,512]{2,1,0:T(8,128)}, f32[2,6,520,128]{3,2,1,0:T(8,128)S(1)}) custom-call(s32[2]{0:T(128)S(1)} %pad_add_fusion.origin_ref, bf16[272,128]{1,0:T(8,128)(2,1)S(1)} %collective-permute-done.5.refs_0_, bf16[272,128]{1,0:T(8,128)(2,1)S(1)} %collective-permute-done.6.refs_1_, ...), custom_call_target="tpu_custom_call", output_to_operand_aliasing={{1}: (3, {})} | custom-call | tf_op jit(solution)/shard_map/place_others/pallas_call | solution.py:409
  (6 shorter events, 0.1 us)
Async XLA Ops:
  0.0 1.8 %copy-start.5 = (bf16[1,1280,2,256]{3,2,1,0:T(2,128)(2,1)S(1)}, bf16[1,1280,2,256]{3,2,1,0:T(2,128)(2,1)}, u32[]{:S(2)}) copy-start(bf16[1,1280,2,256]{3,2,1,0:T(2,128)(2,1)} %param.8) | copy-start | bytes 3932164
  1.2 2.2 %collective-permute-start = (bf16[2560,128]{1,0:T(8,128)(2,1)S(1)}, bf16[2560,128]{1,0:T(8,128)(2,1)S(1)}, u32[]{:S(2)}, u32[]{:S(2)}) collective-permute-start(bf16[2560,128]{1,0:T(8,128)(2,1)S(1)} %constant_dynamic-slice_fusion), channel_id=1, source_target_pairs={{0,1},{1,0},{2,3},{3,2},{4,5},{5,4},{6,7},{7,6},{8,9},{9,8},{10,11... | collective-permute-start | bytes 1966088 | tf_op jit(solution)/shard_map/ppermute | solution.py:466
  1.8 1.7 %copy-start.4 = (s32[5120]{0:T(1024)S(1)}, s32[5120]{0:T(1024)}, u32[]{:S(2)}) copy-start(s32[5120]{0:T(1024)} %ids_ref.1) | copy-start | bytes 61444
  3.5 20.3 %copy-start.6 = (s32[3,16]{1,0:T(4,128)S(1)}, s32[3,16]{1,0:T(4,128)}, u32[]{:S(2)}) copy-start(s32[3,16]{1,0:T(4,128)} %param.11) | copy-start | bytes 580
  23.3 10.5 %copy-start = (bf16[2,128,256]{2,1,0:T(8,128)(2,1)S(1)}, bf16[2,128,256]{2,1,0:T(8,128)(2,1)}, u32[]{:S(2)}) copy-start(bf16[2,128,256]{2,1,0:T(8,128)(2,1)} %constant.81.clone.columns_ref) | copy-start | bytes 393220
  23.3 10.5 %copy-start.1 = (bf16[2,32,64]{2,1,0:T(8,128)(2,1)S(1)}, bf16[2,32,64]{2,1,0:T(8,128)(2,1)}, u32[]{:S(2)}) copy-start(bf16[2,32,64]{2,1,0:T(8,128)(2,1)} %constant.82.clone.rows_ref) | copy-start | bytes 24580
  23.3 10.5 %copy-start.2 = (f32[32,128]{1,0:T(8,128)S(1)}, f32[32,128]{1,0:T(8,128)}, u32[]{:S(2)}) copy-start(f32[32,128]{1,0:T(8,128)} %constant.80.clone.tapers_ref) | copy-start | bytes 49156
  23.3 10.5 %copy-start.3 = (f32[32,128]{1,0:T(8,128)S(1)}, f32[32,128]{1,0:T(8,128)}, u32[]{:S(2)}) copy-start(f32[32,128]{1,0:T(8,128)} %constant.79.clone.turns_ref) | copy-start | bytes 49156
  23.3 1.6 %collective-permute-start.1 = (bf16[4,272,128]{2,1,0:T(8,128)(2,1)S(1)}, bf16[4,272,128]{2,1,0:T(8,128)(2,1)S(1)}, u32[]{:S(2)}, u32[]{:S(2)}) collective-permute-start(bf16[4,272,128]{2,1,0:T(8,128)(2,1)S(1)} %get-tuple-element.13), channel_id=1, source_target_pairs={{0,1},{1,0},{2,3},{3,2},{4,5},{5,4},{6,7},{7,6},{8,9},{9,8},{10,11... | collective-permute-start | bytes 835592 | tf_op jit(solution)/shard_map/ppermute | solution.py:472
  25.1 6.4 %collective-permute-start.4 = (bf16[272,128]{1,0:T(8,128)(2,1)S(1)}, bf16[272,128]{1,0:T(8,128)(2,1)S(1)}, u32[]{:S(2)}, u32[]{:S(2)}) collective-permute-start(bf16[272,128]{1,0:T(8,128)(2,1)S(1)} %get-tuple-element.15), channel_id=1, source_target_pairs={{0,6},{2,4},{4,2},{6,0},{1,7},{3,5},{5,3},{7,1},{8,14},{10,12},{12... | collective-permute-start | bytes 208904 | tf_op jit(solution)/shard_map/ppermute | solution.py:441
  29.0 4.3 %collective-permute-start.3 = (bf16[272,128]{1,0:T(8,128)(2,1)S(1)}, bf16[272,128]{1,0:T(8,128)(2,1)S(1)}, u32[]{:S(2)}, u32[]{:S(2)}) collective-permute-start(bf16[272,128]{1,0:T(8,128)(2,1)S(1)} %get-tuple-element.16), channel_id=1, source_target_pairs={{0,4},{2,6},{4,0},{6,2},{1,5},{3,7},{5,1},{7,3},{8,12},{10,14},{12... | collective-permute-start | bytes 208904 | tf_op jit(solution)/shard_map/ppermute | solution.py:441
  29.5 4.3 %collective-permute-start.2 = (bf16[272,128]{1,0:T(8,128)(2,1)S(1)}, bf16[272,128]{1,0:T(8,128)(2,1)S(1)}, u32[]{:S(2)}, u32[]{:S(2)}) collective-permute-start(bf16[272,128]{1,0:T(8,128)(2,1)S(1)} %get-tuple-element.17), channel_id=1, source_target_pairs={{0,2},{2,0},{4,6},{6,4},{1,3},{3,1},{5,7},{7,5},{8,10},{10,8},{12,... | collective-permute-start | bytes 208904 | tf_op jit(solution)/shard_map/ppermute | solution.py:441
  35.0 5.6 %collective-permute-start.7 = (bf16[272,128]{1,0:T(8,128)(2,1)S(1)}, bf16[272,128]{1,0:T(8,128)(2,1)S(1)}, u32[]{:S(2)}, u32[]{:S(2)}) collective-permute-start(bf16[272,128]{1,0:T(8,128)(2,1)S(1)} %subgrid_transform.1.refs_0_), channel_id=1, source_target_pairs={{0,24},{8,0},{16,8},{24,16},{1,25},{9,1},{17,9},{25,17},{2,26},{10... | collective-permute-start | bytes 208904 | tf_op jit(solution)/shard_map/ppermute | solution.py:429
  38.7 5.2 %collective-permute-start.6 = (bf16[272,128]{1,0:T(8,128)(2,1)S(1)}, bf16[272,128]{1,0:T(8,128)(2,1)S(1)}, u32[]{:S(2)}, u32[]{:S(2)}) collective-permute-start(bf16[272,128]{1,0:T(8,128)(2,1)S(1)} %subgrid_transform.1.refs_0_), channel_id=1, source_target_pairs={{0,16},{8,24},{16,0},{24,8},{1,17},{9,25},{17,1},{25,9},{2,18},{10... | collective-permute-start | bytes 208904 | tf_op jit(solution)/shard_map/ppermute | solution.py:429
  38.7 6.1 %collective-permute-start.5 = (bf16[272,128]{1,0:T(8,128)(2,1)S(1)}, bf16[272,128]{1,0:T(8,128)(2,1)S(1)}, u32[]{:S(2)}, u32[]{:S(2)}) collective-permute-start(bf16[272,128]{1,0:T(8,128)(2,1)S(1)} %subgrid_transform.1.refs_0_), channel_id=1, source_target_pairs={{0,8},{8,16},{16,24},{24,0},{1,9},{9,17},{17,25},{25,1},{2,10},{10... | collective-permute-start | bytes 208904 | tf_op jit(solution)/shard_map/ppermute | solution.py:429

commit v5 on v4

--- a/solution.py
+++ b/solution.py
@@ -426,7 +426,7 @@
 def around(block, axis):
     count = lax.axis_size(axis)
     return [block] + [
-        lax.ppermute(block, axis, [(i, (i + step) % count) for i in range(count)]) for step in range(1, count)
+        lax.ppermute(block, axis, [(i, i ^ step) for i in range(count)]) for step in range(1, count)
     ]
 
 

time: 48.4 us -> 47.8 us (0.988)
  transfers between devices with their start and end apart: 8 -> 8, of which waited for: 8 -> 7; matrix products, arithmetic and copies ran while one was open for 3% -> 3% of each run, Pallas kernels for 5% -> 5%
where the time goes in v5:
time: 47.8 us; the launch traced here: 47.9 us
  Pallas kernels  27 us (56%)
  starting transfers between devices  9.91 us (21%)
  waiting for transfers between devices  8.12 us (17%)
  local copies, waits for them, and re-layouts  2.59 us (5%)
    pallas_call x1, Pallas kernels, slot_sums(): pl.pallas_call(slot_sums_kernel, out_shape=[jax.ShapeDtypeStruct((shard_c...  19.8 us
    pallas_call x2, Pallas kernels, place(): pl.pallas_call(functools.partial(place_kernel, first, not first, len(grou...  6 us
    ppermute x3, starting transfers between devices, exchange(): lax.ppermute(block_for(step), axis, [(i, i ^ step) for i in range(count)])  4.52 us
    ppermute x3, starting transfers between devices, around(): lax.ppermute(block, axis, [(i, i ^ step) for i in range(count)])  4.45 us
    ppermute x3, waiting for transfers between devices, exchange(): lax.ppermute(block_for(step), axis, [(i, i ^ step) for i in range(count)])  4.07 us
    dynamic_slice x2, local copies, waits for them, and re-layouts, half_of(): return lax.dynamic_slice_in_dim(rows, which * (half * 4), half * 4, 0)  2.41 us
    ppermute x3, waiting for transfers between devices, around(): lax.ppermute(block, axis, [(i, i ^ step) for i in range(count)])  2.34 us
    pallas_call x1, Pallas kernels, subgrid_transform(): pl.pallas_call(transform_kernel, out_shape=jax.ShapeDtypeStruct((slots //...  1.19 us
  transfers between devices with their start and end apart: 8, of which 7 were waited for; matrix products, arithmetic and copies ran while one was open for 3% of the time, Pallas kernels for 5%

profile of v5, /device:TPU:0, one launch (start us, length us, event | category | flops | bytes accessed | tf_op | source)
XLA Modules:
  0.0 47.9 jit_solution(8892136504377543988)
XLA Ops:
  0.0 0.0 copy-start.5
  0.0 1.2 %constant_dynamic-slice_fusion = bf16[2560,128]{1,0:T(8,128)(2,1)S(1)} fusion(bf16[5120,128]{1,0:T(8,128)(2,1)} %bitcast.29, s32[]{:T(128)S(6)} %select_n.35), kind=kLoop, calls=%fused_computation.8 | loop fusion | bytes 1310724 | tf_op jit(solution)/shard_map/dynamic_slice | solution.py:464
  1.2 0.5 %collective-permute-start = (bf16[2560,128]{1,0:T(8,128)(2,1)S(1)}, bf16[2560,128]{1,0:T(8,128)(2,1)S(1)}, u32[]{:S(2)}, u32[]{:S(2)}) collective-permute-start(bf16[2560,128]{1,0:T(8,128)(2,1)S(1)} %constant_dynamic-slice_fusion), channel_id=1, source_target_pairs={{0,1},{1,0},{2,3},{3,2},{4,5},{5,4},{6,7},{7,6},{8,9},{9,8},{10,11... | collective-permute-start | bytes 1966088 | tf_op jit(solution)/shard_map/ppermute | solution.py:466
  1.8 0.0 copy-done.5
  1.8 0.0 copy-start.4
  1.8 1.2 %constant_dynamic-slice_fusion.1 = (bf16[2560,128]{1,0:T(8,128)(2,1)S(1)}, bf16[2560,128]{1,0:T(8,128)(2,1)S(1)}) fusion(bf16[5120,128]{1,0:T(8,128)(2,1)S(1)} %bitcast.30, s32[]{:T(128)S(6)} %select_n.34, bf16[5120,128]{1,0:T(8,128)(2,1)} %bitcast.31), kind=kLoop, calls=%fused_computation.9 | loop fusion | bytes 2621444 | tf_op jit(solution)/shard_map/dynamic_slice | solution.py:464
  2.9 0.5 %collective-permute-done.theirs_ref = bf16[2560,128]{1,0:T(8,128)(2,1)S(1)} collective-permute-done((bf16[2560,128]{1,0:T(8,128)(2,1)S(1)}, bf16[2560,128]{1,0:T(8,128)(2,1)S(1)}, u32[]{:S(2)}, u32[]{:S(2)}) %collective-permute-start) | collective-permute-done | bytes 655392 | tf_op jit(solution)/shard_map/ppermute | solution.py:466
  3.5 0.0 copy-done.4
  3.5 0.0 copy-start.6
  3.5 19.8 %slot_sums.1 = (f32[4,272,128]{2,1,0:T(8,128)S(1)}, bf16[4,272,128]{2,1,0:T(8,128)(2,1)S(1)}) custom-call(s32[1]{0:T(128)} %bitcast.5.first_ref, f32[1]{0:T(128)} %bitcast.6.sign_ref, s32[5120]{0:T(1024)S(1)} %copy-done.4, bf16[2560,128]{1,0:T(8,128)(2,1)S(1)} %get-tuple-element.22.uv_ref, bf16[2560,128]{1,0:T(8,128)(2,1)S(1)} %get-tuple-element.21.mine_ref, ...), custom_call_target="tpu_custom_call" | custom-call | flops 60000002048 | bytes 4000000 | tf_op jit(solution)/shard_map/slot_sums/pallas_call | solution.py:196
  23.3 0.0 copy-start
  23.3 0.0 copy-start.1
  23.3 0.0 copy-start.2
  23.3 0.0 copy-start.3
  23.4 0.4 collective-permute-start.1
  23.8 0.0 copy-done.6
  23.8 1.2 %collective-permute-done.1 = bf16[4,272,128]{2,1,0:T(8,128)(2,1)S(1)} collective-permute-done((bf16[4,272,128]{2,1,0:T(8,128)(2,1)S(1)}, bf16[4,272,128]{2,1,0:T(8,128)(2,1)S(1)}, u32[]{:S(2)}, u32[]{:S(2)}) %collective-permute-start.1) | collective-permute-done | bytes 278560 | tf_op jit(solution)/shard_map/ppermute | solution.py:472
  25.0 0.1 add_convert_fusion
  25.1 3.9 %collective-permute-start.4 = (bf16[272,128]{1,0:T(8,128)(2,1)S(1)}, bf16[272,128]{1,0:T(8,128)(2,1)S(1)}, u32[]{:S(2)}, u32[]{:S(2)}) collective-permute-start(bf16[272,128]{1,0:T(8,128)(2,1)S(1)} %get-tuple-element.15), channel_id=1, source_target_pairs={{0,6},{2,4},{4,2},{6,0},{1,7},{3,5},{5,3},{7,1},{8,14},{10,12},{12... | collective-permute-start | bytes 208904 | tf_op jit(solution)/shard_map/ppermute | solution.py:441
  29.0 0.5 %collective-permute-start.3 = (bf16[272,128]{1,0:T(8,128)(2,1)S(1)}, bf16[272,128]{1,0:T(8,128)(2,1)S(1)}, u32[]{:S(2)}, u32[]{:S(2)}) collective-permute-start(bf16[272,128]{1,0:T(8,128)(2,1)S(1)} %get-tuple-element.16), channel_id=1, source_target_pairs={{0,4},{2,6},{4,0},{6,2},{1,5},{3,7},{5,1},{7,3},{8,12},{10,14},{12... | collective-permute-start | bytes 208904 | tf_op jit(solution)/shard_map/ppermute | solution.py:441
  29.5 0.1 collective-permute-start.2
  29.6 0.1 convert_element_type.26
  29.7 1.8 %collective-permute-done.4.refs_3_ = bf16[272,128]{1,0:T(8,128)(2,1)S(1)} collective-permute-done((bf16[272,128]{1,0:T(8,128)(2,1)S(1)}, bf16[272,128]{1,0:T(8,128)(2,1)S(1)}, u32[]{:S(2)}, u32[]{:S(2)}) %collective-permute-start.4) | collective-permute-done | bytes 69664 | tf_op jit(solution)/shard_map/ppermute | solution.py:441
  31.5 1.8 %collective-permute-done.3.refs_2_ = bf16[272,128]{1,0:T(8,128)(2,1)S(1)} collective-permute-done((bf16[272,128]{1,0:T(8,128)(2,1)S(1)}, bf16[272,128]{1,0:T(8,128)(2,1)S(1)}, u32[]{:S(2)}, u32[]{:S(2)}) %collective-permute-start.3) | collective-permute-done | bytes 69664 | tf_op jit(solution)/shard_map/ppermute | solution.py:441
  33.3 0.5 %collective-permute-done.2.refs_1_ = bf16[272,128]{1,0:T(8,128)(2,1)S(1)} collective-permute-done((bf16[272,128]{1,0:T(8,128)(2,1)S(1)}, bf16[272,128]{1,0:T(8,128)(2,1)S(1)}, u32[]{:S(2)}, u32[]{:S(2)}) %collective-permute-start.2) | collective-permute-done | bytes 69664 | tf_op jit(solution)/shard_map/ppermute | solution.py:441
  33.8 0.0 copy-done
  33.8 0.0 copy-done.1
  33.8 0.0 copy-done.2
  33.8 0.0 copy-done.3
  33.8 1.2 %subgrid_transform.1.refs_0_ = bf16[272,128]{1,0:T(8,128)(2,1)S(1)} custom-call(s32[16]{0:T(128)S(1)} %slice_bitcast_fusion.planes_ref, f32[16,128]{1,0:T(8,128)S(1)} %pad.4.corners_ref, f32[32,128]{1,0:T(8,128)S(1)} %copy-done.3, f32[32,128]{1,0:T(8,128)S(1)} %copy-done.2, bf16[2,128,256]{2,1,0:T(8,128)(2,1)S(1)} %copy-done, ...), custom_call_target="tpu_custom_call" | custom-call | tf_op jit(solution)/shard_map/subgrid_transform/pallas_call | solution.py:320
  35.0 3.7 %collective-permute-start.7 = (bf16[272,128]{1,0:T(8,128)(2,1)S(1)}, bf16[272,128]{1,0:T(8,128)(2,1)S(1)}, u32[]{:S(2)}, u32[]{:S(2)}) collective-permute-start(bf16[272,128]{1,0:T(8,128)(2,1)S(1)} %subgrid_transform.1.refs_0_), channel_id=1, source_target_pairs={{0,24},{8,16},{16,8},{24,0},{1,25},{9,17},{17,9},{25,1},{2,26},{10... | collective-permute-start | bytes 208904 | tf_op jit(solution)/shard_map/ppermute | solution.py:429
  38.7 0.0 collective-permute-start.6
  38.7 0.8 %collective-permute-start.5 = (bf16[272,128]{1,0:T(8,128)(2,1)S(1)}, bf16[272,128]{1,0:T(8,128)(2,1)S(1)}, u32[]{:S(2)}, u32[]{:S(2)}) collective-permute-start(bf16[272,128]{1,0:T(8,128)(2,1)S(1)} %subgrid_transform.1.refs_0_), channel_id=1, source_target_pairs={{0,8},{8,0},{16,24},{24,16},{1,9},{9,1},{17,25},{25,17},{2,10},{10... | collective-permute-start | bytes 208904 | tf_op jit(solution)/shard_map/ppermute | solution.py:429
  39.4 0.1 pad_add_fusion.origin_ref
  39.5 1.8 %collective-permute-done.7.refs_1_ = bf16[272,128]{1,0:T(8,128)(2,1)S(1)} collective-permute-done((bf16[272,128]{1,0:T(8,128)(2,1)S(1)}, bf16[272,128]{1,0:T(8,128)(2,1)S(1)}, u32[]{:S(2)}, u32[]{:S(2)}) %collective-permute-start.7) | collective-permute-done | bytes 69664 | tf_op jit(solution)/shard_map/ppermute | solution.py:429
  41.3 2.2 %place_own.1.refs_2_ = f32[2,6,520,128]{3,2,1,0:T(8,128)S(1)} custom-call(s32[2]{0:T(128)S(1)} %pad_add_fusion.origin_ref, bf16[272,128]{1,0:T(8,128)(2,1)S(1)} %subgrid_transform.1.refs_0_, bf16[272,128]{1,0:T(8,128)(2,1)S(1)} %collective-permute-done.7.refs_1_), custom_call_target="tpu_custom_call" | custom-call | tf_op jit(solution)/shard_map/place_own/pallas_call | solution.py:409
  43.6 0.5 %collective-permute-done.6.refs_1_ = bf16[272,128]{1,0:T(8,128)(2,1)S(1)} collective-permute-done((bf16[272,128]{1,0:T(8,128)(2,1)S(1)}, bf16[272,128]{1,0:T(8,128)(2,1)S(1)}, u32[]{:S(2)}, u32[]{:S(2)}) %collective-permute-start.6) | collective-permute-done | bytes 69664 | tf_op jit(solution)/shard_map/ppermute | solution.py:429
  44.1 0.0 collective-permute-done.5.refs_0_
  44.1 3.8 %place_others.1 = (f32[2,512,512]{2,1,0:T(8,128)}, f32[2,6,520,128]{3,2,1,0:T(8,128)S(1)}) custom-call(s32[2]{0:T(128)S(1)} %pad_add_fusion.origin_ref, bf16[272,128]{1,0:T(8,128)(2,1)S(1)} %collective-permute-done.5.refs_0_, bf16[272,128]{1,0:T(8,128)(2,1)S(1)} %collective-permute-done.6.refs_1_, ...), custom_call_target="tpu_custom_call", output_to_operand_aliasing={{1}: (3, {})} | custom-call | tf_op jit(solution)/shard_map/place_others/pallas_call | solution.py:409
  (6 shorter events, 0.1 us)
Async XLA Ops:
  0.0 1.8 %copy-start.5 = (bf16[1,1280,2,256]{3,2,1,0:T(2,128)(2,1)S(1)}, bf16[1,1280,2,256]{3,2,1,0:T(2,128)(2,1)}, u32[]{:S(2)}) copy-start(bf16[1,1280,2,256]{3,2,1,0:T(2,128)(2,1)} %param.8) | copy-start | bytes 3932164
  1.2 2.2 %collective-permute-start = (bf16[2560,128]{1,0:T(8,128)(2,1)S(1)}, bf16[2560,128]{1,0:T(8,128)(2,1)S(1)}, u32[]{:S(2)}, u32[]{:S(2)}) collective-permute-start(bf16[2560,128]{1,0:T(8,128)(2,1)S(1)} %constant_dynamic-slice_fusion), channel_id=1, source_target_pairs={{0,1},{1,0},{2,3},{3,2},{4,5},{5,4},{6,7},{7,6},{8,9},{9,8},{10,11... | collective-permute-start | bytes 1966088 | tf_op jit(solution)/shard_map/ppermute | solution.py:466
  1.8 1.7 %copy-start.4 = (s32[5120]{0:T(1024)S(1)}, s32[5120]{0:T(1024)}, u32[]{:S(2)}) copy-start(s32[5120]{0:T(1024)} %ids_ref.1) | copy-start | bytes 61444
  3.5 20.3 %copy-start.6 = (s32[3,16]{1,0:T(4,128)S(1)}, s32[3,16]{1,0:T(4,128)}, u32[]{:S(2)}) copy-start(s32[3,16]{1,0:T(4,128)} %param.11) | copy-start | bytes 580
  23.3 10.5 %copy-start = (bf16[2,128,256]{2,1,0:T(8,128)(2,1)S(1)}, bf16[2,128,256]{2,1,0:T(8,128)(2,1)}, u32[]{:S(2)}) copy-start(bf16[2,128,256]{2,1,0:T(8,128)(2,1)} %constant.81.clone.columns_ref) | copy-start | bytes 393220
  23.3 10.5 %copy-start.1 = (bf16[2,32,64]{2,1,0:T(8,128)(2,1)S(1)}, bf16[2,32,64]{2,1,0:T(8,128)(2,1)}, u32[]{:S(2)}) copy-start(bf16[2,32,64]{2,1,0:T(8,128)(2,1)} %constant.82.clone.rows_ref) | copy-start | bytes 24580
  23.3 10.4 %copy-start.2 = (f32[32,128]{1,0:T(8,128)S(1)}, f32[32,128]{1,0:T(8,128)}, u32[]{:S(2)}) copy-start(f32[32,128]{1,0:T(8,128)} %constant.80.clone.tapers_ref) | copy-start | bytes 49156
  23.3 10.4 %copy-start.3 = (f32[32,128]{1,0:T(8,128)S(1)}, f32[32,128]{1,0:T(8,128)}, u32[]{:S(2)}) copy-start(f32[32,128]{1,0:T(8,128)} %constant.79.clone.turns_ref) | copy-start | bytes 49156
  23.4 1.6 %collective-permute-start.1 = (bf16[4,272,128]{2,1,0:T(8,128)(2,1)S(1)}, bf16[4,272,128]{2,1,0:T(8,128)(2,1)S(1)}, u32[]{:S(2)}, u32[]{:S(2)}) collective-permute-start(bf16[4,272,128]{2,1,0:T(8,128)(2,1)S(1)} %get-tuple-element.13), channel_id=1, source_target_pairs={{0,1},{1,0},{2,3},{3,2},{4,5},{5,4},{6,7},{7,6},{8,9},{9,8},{10,11... | collective-permute-start | bytes 835592 | tf_op jit(solution)/shard_map/ppermute | solution.py:472
  25.1 6.4 %collective-permute-start.4 = (bf16[272,128]{1,0:T(8,128)(2,1)S(1)}, bf16[272,128]{1,0:T(8,128)(2,1)S(1)}, u32[]{:S(2)}, u32[]{:S(2)}) collective-permute-start(bf16[272,128]{1,0:T(8,128)(2,1)S(1)} %get-tuple-element.15), channel_id=1, source_target_pairs={{0,6},{2,4},{4,2},{6,0},{1,7},{3,5},{5,3},{7,1},{8,14},{10,12},{12... | collective-permute-start | bytes 208904 | tf_op jit(solution)/shard_map/ppermute | solution.py:441
  29.0 4.3 %collective-permute-start.3 = (bf16[272,128]{1,0:T(8,128)(2,1)S(1)}, bf16[272,128]{1,0:T(8,128)(2,1)S(1)}, u32[]{:S(2)}, u32[]{:S(2)}) collective-permute-start(bf16[272,128]{1,0:T(8,128)(2,1)S(1)} %get-tuple-element.16), channel_id=1, source_target_pairs={{0,4},{2,6},{4,0},{6,2},{1,5},{3,7},{5,1},{7,3},{8,12},{10,14},{12... | collective-permute-start | bytes 208904 | tf_op jit(solution)/shard_map/ppermute | solution.py:441
  29.5 4.3 %collective-permute-start.2 = (bf16[272,128]{1,0:T(8,128)(2,1)S(1)}, bf16[272,128]{1,0:T(8,128)(2,1)S(1)}, u32[]{:S(2)}, u32[]{:S(2)}) collective-permute-start(bf16[272,128]{1,0:T(8,128)(2,1)S(1)} %get-tuple-element.17), channel_id=1, source_target_pairs={{0,2},{2,0},{4,6},{6,4},{1,3},{3,1},{5,7},{7,5},{8,10},{10,8},{12,... | collective-permute-start | bytes 208904 | tf_op jit(solution)/shard_map/ppermute | solution.py:441
  35.0 6.3 %collective-permute-start.7 = (bf16[272,128]{1,0:T(8,128)(2,1)S(1)}, bf16[272,128]{1,0:T(8,128)(2,1)S(1)}, u32[]{:S(2)}, u32[]{:S(2)}) collective-permute-start(bf16[272,128]{1,0:T(8,128)(2,1)S(1)} %subgrid_transform.1.refs_0_), channel_id=1, source_target_pairs={{0,24},{8,16},{16,8},{24,0},{1,25},{9,17},{17,9},{25,1},{2,26},{10... | collective-permute-start | bytes 208904 | tf_op jit(solution)/shard_map/ppermute | solution.py:429
  38.7 5.5 %collective-permute-start.6 = (bf16[272,128]{1,0:T(8,128)(2,1)S(1)}, bf16[272,128]{1,0:T(8,128)(2,1)S(1)}, u32[]{:S(2)}, u32[]{:S(2)}) collective-permute-start(bf16[272,128]{1,0:T(8,128)(2,1)S(1)} %subgrid_transform.1.refs_0_), channel_id=1, source_target_pairs={{0,16},{8,24},{16,0},{24,8},{1,17},{9,25},{17,1},{25,9},{2,18},{10... | collective-permute-start | bytes 208904 | tf_op jit(solution)/shard_map/ppermute | solution.py:429
  38.7 5.5 %collective-permute-start.5 = (bf16[272,128]{1,0:T(8,128)(2,1)S(1)}, bf16[272,128]{1,0:T(8,128)(2,1)S(1)}, u32[]{:S(2)}, u32[]{:S(2)}) collective-permute-start(bf16[272,128]{1,0:T(8,128)(2,1)S(1)} %subgrid_transform.1.refs_0_), channel_id=1, source_target_pairs={{0,8},{8,0},{16,24},{24,16},{1,9},{9,1},{17,25},{25,17},{2,10},{10... | collective-permute-start | bytes 208904 | tf_op jit(solution)/shard_map/ppermute | solution.py:429

commit v6 on v5

--- a/solution.py
+++ b/solution.py
@@ -60,8 +60,8 @@
 
 
 GROUP = 8
-BATCH = 8
-PITCH = 9
+BATCH = 10
+PITCH = 11
 
 
 def phases(start, scale, inputs, angles, values, wide):

time: 47.8 us -> 47.5 us (level)
  no operation moved by 1% of the time
where the time goes in v6:
time: 47.5 us; the launch traced here: 47.1 us
  Pallas kernels  26.6 us (56%)
  starting transfers between devices  9.92 us (21%)
  waiting for transfers between devices  7.82 us (16%)
  local copies, waits for them, and re-layouts  2.59 us (5%)
    pallas_call x1, Pallas kernels, slot_sums(): pl.pallas_call(slot_sums_kernel, out_shape=[jax.ShapeDtypeStruct((shard_c...  19.6 us
    pallas_call x2, Pallas kernels, place(): pl.pallas_call(functools.partial(place_kernel, first, not first, len(grou...  5.74 us
    ppermute x3, starting transfers between devices, exchange(): lax.ppermute(block_for(step), axis, [(i, i ^ step) for i in range(count)])  4.52 us
    ppermute x3, starting transfers between devices, around(): lax.ppermute(block, axis, [(i, i ^ step) for i in range(count)])  4.45 us
    ppermute x3, waiting for transfers between devices, exchange(): lax.ppermute(block_for(step), axis, [(i, i ^ step) for i in range(count)])  4.08 us
    dynamic_slice x2, local copies, waits for them, and re-layouts, half_of(): return lax.dynamic_slice_in_dim(rows, which * (half * 4), half * 4, 0)  2.41 us
    ppermute x3, waiting for transfers between devices, around(): lax.ppermute(block, axis, [(i, i ^ step) for i in range(count)])  2.02 us
    pallas_call x1, Pallas kernels, subgrid_transform(): pl.pallas_call(transform_kernel, out_shape=jax.ShapeDtypeStruct((slots //...  1.19 us
  transfers between devices with their start and end apart: 8, of which 7 were waited for; matrix products, arithmetic and copies ran while one was open for 3% of the time, Pallas kernels for 5%

profile of v6, /device:TPU:0, one launch (start us, length us, event | category | flops | bytes accessed | tf_op | source)
XLA Modules:
  0.0 47.1 jit_solution(12947411166854015680)
XLA Ops:
  0.0 0.0 copy-start.5
  0.0 1.2 %constant_dynamic-slice_fusion = bf16[2560,128]{1,0:T(8,128)(2,1)S(1)} fusion(bf16[5120,128]{1,0:T(8,128)(2,1)} %bitcast.29, s32[]{:T(128)S(6)} %select_n.35), kind=kLoop, calls=%fused_computation.8 | loop fusion | bytes 1310724 | tf_op jit(solution)/shard_map/dynamic_slice | solution.py:464
  1.2 0.5 %collective-permute-start = (bf16[2560,128]{1,0:T(8,128)(2,1)S(1)}, bf16[2560,128]{1,0:T(8,128)(2,1)S(1)}, u32[]{:S(2)}, u32[]{:S(2)}) collective-permute-start(bf16[2560,128]{1,0:T(8,128)(2,1)S(1)} %constant_dynamic-slice_fusion), channel_id=1, source_target_pairs={{0,1},{1,0},{2,3},{3,2},{4,5},{5,4},{6,7},{7,6},{8,9},{9,8},{10,11... | collective-permute-start | bytes 1966088 | tf_op jit(solution)/shard_map/ppermute | solution.py:466
  1.8 0.0 copy-done.5
  1.8 0.0 copy-start.4
  1.8 1.2 %constant_dynamic-slice_fusion.1 = (bf16[2560,128]{1,0:T(8,128)(2,1)S(1)}, bf16[2560,128]{1,0:T(8,128)(2,1)S(1)}) fusion(bf16[5120,128]{1,0:T(8,128)(2,1)S(1)} %bitcast.30, s32[]{:T(128)S(6)} %select_n.34, bf16[5120,128]{1,0:T(8,128)(2,1)} %bitcast.31), kind=kLoop, calls=%fused_computation.9 | loop fusion | bytes 2621444 | tf_op jit(solution)/shard_map/dynamic_slice | solution.py:464
  2.9 0.5 %collective-permute-done.theirs_ref = bf16[2560,128]{1,0:T(8,128)(2,1)S(1)} collective-permute-done((bf16[2560,128]{1,0:T(8,128)(2,1)S(1)}, bf16[2560,128]{1,0:T(8,128)(2,1)S(1)}, u32[]{:S(2)}, u32[]{:S(2)}) %collective-permute-start) | collective-permute-done | bytes 655392 | tf_op jit(solution)/shard_map/ppermute | solution.py:466
  3.5 0.0 copy-done.4
  3.5 0.0 copy-start.6
  3.5 19.6 %slot_sums.1 = (f32[4,272,128]{2,1,0:T(8,128)S(1)}, bf16[4,272,128]{2,1,0:T(8,128)(2,1)S(1)}) custom-call(s32[1]{0:T(128)} %bitcast.5.first_ref, f32[1]{0:T(128)} %bitcast.6.sign_ref, s32[5120]{0:T(1024)S(1)} %copy-done.4, bf16[2560,128]{1,0:T(8,128)(2,1)S(1)} %get-tuple-element.22.uv_ref, bf16[2560,128]{1,0:T(8,128)(2,1)S(1)} %get-tuple-element.21.mine_ref, ...), custom_call_target="tpu_custom_call" | custom-call | flops 60000002048 | bytes 4000000 | tf_op jit(solution)/shard_map/slot_sums/pallas_call | solution.py:196
  23.1 0.0 copy-start
  23.1 0.0 copy-start.1
  23.1 0.0 copy-start.2
  23.2 0.0 copy-start.3
  23.2 0.4 collective-permute-start.1
  23.6 0.0 copy-done.6
  23.6 1.2 %collective-permute-done.1 = bf16[4,272,128]{2,1,0:T(8,128)(2,1)S(1)} collective-permute-done((bf16[4,272,128]{2,1,0:T(8,128)(2,1)S(1)}, bf16[4,272,128]{2,1,0:T(8,128)(2,1)S(1)}, u32[]{:S(2)}, u32[]{:S(2)}) %collective-permute-start.1) | collective-permute-done | bytes 278560 | tf_op jit(solution)/shard_map/ppermute | solution.py:472
  24.8 0.1 add_convert_fusion
  24.9 3.9 %collective-permute-start.4 = (bf16[272,128]{1,0:T(8,128)(2,1)S(1)}, bf16[272,128]{1,0:T(8,128)(2,1)S(1)}, u32[]{:S(2)}, u32[]{:S(2)}) collective-permute-start(bf16[272,128]{1,0:T(8,128)(2,1)S(1)} %get-tuple-element.15), channel_id=1, source_target_pairs={{0,6},{2,4},{4,2},{6,0},{1,7},{3,5},{5,3},{7,1},{8,14},{10,12},{12... | collective-permute-start | bytes 208904 | tf_op jit(solution)/shard_map/ppermute | solution.py:441
  28.8 0.5 %collective-permute-start.3 = (bf16[272,128]{1,0:T(8,128)(2,1)S(1)}, bf16[272,128]{1,0:T(8,128)(2,1)S(1)}, u32[]{:S(2)}, u32[]{:S(2)}) collective-permute-start(bf16[272,128]{1,0:T(8,128)(2,1)S(1)} %get-tuple-element.16), channel_id=1, source_target_pairs={{0,4},{2,6},{4,0},{6,2},{1,5},{3,7},{5,1},{7,3},{8,12},{10,14},{12... | collective-permute-start | bytes 208904 | tf_op jit(solution)/shard_map/ppermute | solution.py:441
  29.3 0.1 collective-permute-start.2
  29.4 0.1 convert_element_type.26
  29.5 1.8 %collective-permute-done.4.refs_3_ = bf16[272,128]{1,0:T(8,128)(2,1)S(1)} collective-permute-done((bf16[272,128]{1,0:T(8,128)(2,1)S(1)}, bf16[272,128]{1,0:T(8,128)(2,1)S(1)}, u32[]{:S(2)}, u32[]{:S(2)}) %collective-permute-start.4) | collective-permute-done | bytes 69664 | tf_op jit(solution)/shard_map/ppermute | solution.py:441
  31.3 1.8 %collective-permute-done.3.refs_2_ = bf16[272,128]{1,0:T(8,128)(2,1)S(1)} collective-permute-done((bf16[272,128]{1,0:T(8,128)(2,1)S(1)}, bf16[272,128]{1,0:T(8,128)(2,1)S(1)}, u32[]{:S(2)}, u32[]{:S(2)}) %collective-permute-start.3) | collective-permute-done | bytes 69664 | tf_op jit(solution)/shard_map/ppermute | solution.py:441
  33.1 0.5 %collective-permute-done.2.refs_1_ = bf16[272,128]{1,0:T(8,128)(2,1)S(1)} collective-permute-done((bf16[272,128]{1,0:T(8,128)(2,1)S(1)}, bf16[272,128]{1,0:T(8,128)(2,1)S(1)}, u32[]{:S(2)}, u32[]{:S(2)}) %collective-permute-start.2) | collective-permute-done | bytes 69664 | tf_op jit(solution)/shard_map/ppermute | solution.py:441
  33.6 0.0 copy-done
  33.6 0.0 copy-done.1
  33.6 0.0 copy-done.2
  33.6 0.0 copy-done.3
  33.6 1.2 %subgrid_transform.1.refs_0_ = bf16[272,128]{1,0:T(8,128)(2,1)S(1)} custom-call(s32[16]{0:T(128)S(1)} %slice_bitcast_fusion.planes_ref, f32[16,128]{1,0:T(8,128)S(1)} %pad.4.corners_ref, f32[32,128]{1,0:T(8,128)S(1)} %copy-done.3, f32[32,128]{1,0:T(8,128)S(1)} %copy-done.2, bf16[2,128,256]{2,1,0:T(8,128)(2,1)S(1)} %copy-done, ...), custom_call_target="tpu_custom_call" | custom-call | tf_op jit(solution)/shard_map/subgrid_transform/pallas_call | solution.py:320
  34.8 3.7 %collective-permute-start.7 = (bf16[272,128]{1,0:T(8,128)(2,1)S(1)}, bf16[272,128]{1,0:T(8,128)(2,1)S(1)}, u32[]{:S(2)}, u32[]{:S(2)}) collective-permute-start(bf16[272,128]{1,0:T(8,128)(2,1)S(1)} %subgrid_transform.1.refs_0_), channel_id=1, source_target_pairs={{0,24},{8,16},{16,8},{24,0},{1,25},{9,17},{17,9},{25,1},{2,26},{10... | collective-permute-start | bytes 208904 | tf_op jit(solution)/shard_map/ppermute | solution.py:429
  38.5 0.0 collective-permute-start.6
  38.5 0.8 %collective-permute-start.5 = (bf16[272,128]{1,0:T(8,128)(2,1)S(1)}, bf16[272,128]{1,0:T(8,128)(2,1)S(1)}, u32[]{:S(2)}, u32[]{:S(2)}) collective-permute-start(bf16[272,128]{1,0:T(8,128)(2,1)S(1)} %subgrid_transform.1.refs_0_), channel_id=1, source_target_pairs={{0,8},{8,0},{16,24},{24,16},{1,9},{9,1},{17,25},{25,17},{2,10},{10... | collective-permute-start | bytes 208904 | tf_op jit(solution)/shard_map/ppermute | solution.py:429
  39.3 0.1 pad_add_fusion.origin_ref
  39.4 1.8 %collective-permute-done.7.refs_1_ = bf16[272,128]{1,0:T(8,128)(2,1)S(1)} collective-permute-done((bf16[272,128]{1,0:T(8,128)(2,1)S(1)}, bf16[272,128]{1,0:T(8,128)(2,1)S(1)}, u32[]{:S(2)}, u32[]{:S(2)}) %collective-permute-start.7) | collective-permute-done | bytes 69664 | tf_op jit(solution)/shard_map/ppermute | solution.py:429
  41.1 2.6 %place_own.1.refs_2_ = f32[2,6,520,128]{3,2,1,0:T(8,128)S(1)} custom-call(s32[2]{0:T(128)S(1)} %pad_add_fusion.origin_ref, bf16[272,128]{1,0:T(8,128)(2,1)S(1)} %subgrid_transform.1.refs_0_, bf16[272,128]{1,0:T(8,128)(2,1)S(1)} %collective-permute-done.7.refs_1_), custom_call_target="tpu_custom_call" | custom-call | tf_op jit(solution)/shard_map/place_own/pallas_call | solution.py:409
  43.7 0.2 collective-permute-done.6.refs_1_
  44.0 0.0 collective-permute-done.5.refs_0_
  44.0 3.2 %place_others.1 = (f32[2,512,512]{2,1,0:T(8,128)}, f32[2,6,520,128]{3,2,1,0:T(8,128)S(1)}) custom-call(s32[2]{0:T(128)S(1)} %pad_add_fusion.origin_ref, bf16[272,128]{1,0:T(8,128)(2,1)S(1)} %collective-permute-done.5.refs_0_, bf16[272,128]{1,0:T(8,128)(2,1)S(1)} %collective-permute-done.6.refs_1_, ...), custom_call_target="tpu_custom_call", output_to_operand_aliasing={{1}: (3, {})} | custom-call | tf_op jit(solution)/shard_map/place_others/pallas_call | solution.py:409
  (6 shorter events, 0.1 us)
Async XLA Ops:
  0.0 1.8 %copy-start.5 = (bf16[1,1280,2,256]{3,2,1,0:T(2,128)(2,1)S(1)}, bf16[1,1280,2,256]{3,2,1,0:T(2,128)(2,1)}, u32[]{:S(2)}) copy-start(bf16[1,1280,2,256]{3,2,1,0:T(2,128)(2,1)} %param.8) | copy-start | bytes 3932164
  1.2 2.2 %collective-permute-start = (bf16[2560,128]{1,0:T(8,128)(2,1)S(1)}, bf16[2560,128]{1,0:T(8,128)(2,1)S(1)}, u32[]{:S(2)}, u32[]{:S(2)}) collective-permute-start(bf16[2560,128]{1,0:T(8,128)(2,1)S(1)} %constant_dynamic-slice_fusion), channel_id=1, source_target_pairs={{0,1},{1,0},{2,3},{3,2},{4,5},{5,4},{6,7},{7,6},{8,9},{9,8},{10,11... | collective-permute-start | bytes 1966088 | tf_op jit(solution)/shard_map/ppermute | solution.py:466
  1.8 1.7 %copy-start.4 = (s32[5120]{0:T(1024)S(1)}, s32[5120]{0:T(1024)}, u32[]{:S(2)}) copy-start(s32[5120]{0:T(1024)} %ids_ref.1) | copy-start | bytes 61444
  3.5 20.1 %copy-start.6 = (s32[3,16]{1,0:T(4,128)S(1)}, s32[3,16]{1,0:T(4,128)}, u32[]{:S(2)}) copy-start(s32[3,16]{1,0:T(4,128)} %param.11) | copy-start | bytes 580
  23.1 10.5 %copy-start = (bf16[2,128,256]{2,1,0:T(8,128)(2,1)S(1)}, bf16[2,128,256]{2,1,0:T(8,128)(2,1)}, u32[]{:S(2)}) copy-start(bf16[2,128,256]{2,1,0:T(8,128)(2,1)} %constant.81.clone.columns_ref) | copy-start | bytes 393220
  23.1 10.5 %copy-start.1 = (bf16[2,32,64]{2,1,0:T(8,128)(2,1)S(1)}, bf16[2,32,64]{2,1,0:T(8,128)(2,1)}, u32[]{:S(2)}) copy-start(bf16[2,32,64]{2,1,0:T(8,128)(2,1)} %constant.82.clone.rows_ref) | copy-start | bytes 24580
  23.1 10.5 %copy-start.2 = (f32[32,128]{1,0:T(8,128)S(1)}, f32[32,128]{1,0:T(8,128)}, u32[]{:S(2)}) copy-start(f32[32,128]{1,0:T(8,128)} %constant.80.clone.tapers_ref) | copy-start | bytes 49156
  23.2 10.5 %copy-start.3 = (f32[32,128]{1,0:T(8,128)S(1)}, f32[32,128]{1,0:T(8,128)}, u32[]{:S(2)}) copy-start(f32[32,128]{1,0:T(8,128)} %constant.79.clone.turns_ref) | copy-start | bytes 49156
  23.2 1.6 %collective-permute-start.1 = (bf16[4,272,128]{2,1,0:T(8,128)(2,1)S(1)}, bf16[4,272,128]{2,1,0:T(8,128)(2,1)S(1)}, u32[]{:S(2)}, u32[]{:S(2)}) collective-permute-start(bf16[4,272,128]{2,1,0:T(8,128)(2,1)S(1)} %get-tuple-element.13), channel_id=1, source_target_pairs={{0,1},{1,0},{2,3},{3,2},{4,5},{5,4},{6,7},{7,6},{8,9},{9,8},{10,11... | collective-permute-start | bytes 835592 | tf_op jit(solution)/shard_map/ppermute | solution.py:472
  24.9 6.4 %collective-permute-start.4 = (bf16[272,128]{1,0:T(8,128)(2,1)S(1)}, bf16[272,128]{1,0:T(8,128)(2,1)S(1)}, u32[]{:S(2)}, u32[]{:S(2)}) collective-permute-start(bf16[272,128]{1,0:T(8,128)(2,1)S(1)} %get-tuple-element.15), channel_id=1, source_target_pairs={{0,6},{2,4},{4,2},{6,0},{1,7},{3,5},{5,3},{7,1},{8,14},{10,12},{12... | collective-permute-start | bytes 208904 | tf_op jit(solution)/shard_map/ppermute | solution.py:441
  28.8 4.3 %collective-permute-start.3 = (bf16[272,128]{1,0:T(8,128)(2,1)S(1)}, bf16[272,128]{1,0:T(8,128)(2,1)S(1)}, u32[]{:S(2)}, u32[]{:S(2)}) collective-permute-start(bf16[272,128]{1,0:T(8,128)(2,1)S(1)} %get-tuple-element.16), channel_id=1, source_target_pairs={{0,4},{2,6},{4,0},{6,2},{1,5},{3,7},{5,1},{7,3},{8,12},{10,14},{12... | collective-permute-start | bytes 208904 | tf_op jit(solution)/shard_map/ppermute | solution.py:441
  29.3 4.3 %collective-permute-start.2 = (bf16[272,128]{1,0:T(8,128)(2,1)S(1)}, bf16[272,128]{1,0:T(8,128)(2,1)S(1)}, u32[]{:S(2)}, u32[]{:S(2)}) collective-permute-start(bf16[272,128]{1,0:T(8,128)(2,1)S(1)} %get-tuple-element.17), channel_id=1, source_target_pairs={{0,2},{2,0},{4,6},{6,4},{1,3},{3,1},{5,7},{7,5},{8,10},{10,8},{12,... | collective-permute-start | bytes 208904 | tf_op jit(solution)/shard_map/ppermute | solution.py:441
  34.8 6.3 %collective-permute-start.7 = (bf16[272,128]{1,0:T(8,128)(2,1)S(1)}, bf16[272,128]{1,0:T(8,128)(2,1)S(1)}, u32[]{:S(2)}, u32[]{:S(2)}) collective-permute-start(bf16[272,128]{1,0:T(8,128)(2,1)S(1)} %subgrid_transform.1.refs_0_), channel_id=1, source_target_pairs={{0,24},{8,16},{16,8},{24,0},{1,25},{9,17},{17,9},{25,1},{2,26},{10... | collective-permute-start | bytes 208904 | tf_op jit(solution)/shard_map/ppermute | solution.py:429
  38.5 5.5 %collective-permute-start.6 = (bf16[272,128]{1,0:T(8,128)(2,1)S(1)}, bf16[272,128]{1,0:T(8,128)(2,1)S(1)}, u32[]{:S(2)}, u32[]{:S(2)}) collective-permute-start(bf16[272,128]{1,0:T(8,128)(2,1)S(1)} %subgrid_transform.1.refs_0_), channel_id=1, source_target_pairs={{0,16},{8,24},{16,0},{24,8},{1,17},{9,25},{17,1},{25,9},{2,18},{10... | collective-permute-start | bytes 208904 | tf_op jit(solution)/shard_map/ppermute | solution.py:429
  38.5 5.5 %collective-permute-start.5 = (bf16[272,128]{1,0:T(8,128)(2,1)S(1)}, bf16[272,128]{1,0:T(8,128)(2,1)S(1)}, u32[]{:S(2)}, u32[]{:S(2)}) collective-permute-start(bf16[272,128]{1,0:T(8,128)(2,1)S(1)} %subgrid_transform.1.refs_0_), channel_id=1, source_target_pairs={{0,8},{8,0},{16,24},{24,16},{1,9},{9,1},{17,25},{25,17},{2,10},{10... | collective-permute-start | bytes 208904 | tf_op jit(solution)/shard_map/ppermute | solution.py:429
